TPU v7x, 256 devices: a whole 4x4x8 slice. The times are simulated.
256 devices in a mesh: src: 128 (over x, z, y), frm: 2 (over core).
Axes of the slice: x: 4, y: 4, z: 8, core: 2. Of those that a mesh axis runs over, the one named last changes fastest.
Arguments:
- measured: float32 [512, 256], P(None, 'frm'), may hold values from -4 to 4
- lead_field: bfloat16 [512, 524288], P(None, 'src'), may hold values from -0.0078125 to 0.0078125
- depth: float32 [524288], P('src'), may hold values from 0.5 to 2
- coefficients: float32 [524288, 8, 64], P('src', 'frm'), may hold values from -1.2 to 1.2
- offsets: int32 [8], P('frm'), may hold values from 0 to 240, as said below
- group_ids: int32 [524288], P('src'), may hold values from 0 to 255, as said below
Outputs:
- estimate: float32 [524288, 8, 64], P('src', 'frm')
- residual: float32 [512, 256], P(None, 'frm')
Inputs may be any that keep to these rules, and one draw needn't show every extreme that they name: offsets[f] lies between 32 f and 32 f + 16; one frame takes no shift and one the full 32 // 2. `group_ids`: each of the 256 group ids names exactly 2048 sources, which follow one another in circular order of the sources.
All inputs are finite; a program needn't handle non-finite values.
Results may differ from a plain program's by a relative error of at most 0.0019.
Values may be sent and summed in bfloat16 or wider, within the bound.
No kernel may reach another device: no remote copies, remote signals or barrier semaphores. Data moves between devices by JAX's collectives and lax.ppermute only.
A program may use at most 64 MiB of HBM per device.

v0:
```python
import jax
import jax.numpy as jnp
from jax import lax
from jax.sharding import PartitionSpec as P

K = 64
GROUP = 2048
ITERS = 3


step_size = 0.5
shrink_one = 0.05
group_weight = 0.03
epsilon = 1e-06


def from_behind(block, axis, distance):
    devices = range(lax.axis_size(axis))
    route = [((i - distance) % len(devices), i) for i in devices]
    return lax.ppermute(block, axis, route)


def local_atoms(offsets, time_start, seg_len):
    samples = jnp.arange(seg_len, dtype=jnp.int32)
    delay = samples[None, None, :] - (offsets - time_start)[:, None, None]
    inside = (delay >= 0) & (delay < K)
    delayf = delay.astype(jnp.float32)
    freq = jnp.arange(K, dtype=jnp.int32).astype(jnp.float32)[None, :, None]
    window = jnp.sin(jnp.pi * (delayf + 0.5) / K)
    basis = jnp.sqrt(2.0 / K) * jnp.cos(jnp.pi * (freq + 0.5) * (delayf + 0.5) / K)
    table = jnp.where(inside, window * basis, jnp.float32(0.0))
    return table.reshape(offsets.shape[0] * K, seg_len)


def window_basis():
    delayf = jnp.arange(K, dtype=jnp.int32).astype(jnp.float32)[None, :]
    freq = jnp.arange(K, dtype=jnp.int32).astype(jnp.float32)[:, None]
    window = jnp.sin(jnp.pi * (delayf + 0.5) / K)
    basis = jnp.sqrt(2.0 / K) * jnp.cos(jnp.pi * (freq + 0.5) * (delayf + 0.5) / K)
    return window * basis


def local_placement(offsets, time_start, seg_len):
    samples = jnp.arange(seg_len, dtype=jnp.int32)
    delay = samples[None, None, :] - (offsets - time_start)[:, None, None]
    position = jnp.arange(K, dtype=jnp.int32)[None, :, None]
    return (delay == position).astype(jnp.float32).reshape(offsets.shape[0] * K, seg_len)


def intersection_add(values, placing, own_time):
    segment = jnp.dot(values, placing, precision=lax.Precision.HIGHEST)
    carried = from_behind(segment[:, own_time:].astype(jnp.bfloat16), "frm", 1).astype(jnp.float32)
    return segment[:, :own_time].at[:, :K].add(carried)


def project_back(lead_field, depth, values):
    product = lax.dot_general(
        lead_field, values, (((0,), (0,)), ((), ())), preferred_element_type=jnp.float32
    )
    return depth[:, None] * product


def shards(measured, lead_field, depth, coefficients, offsets, group_ids):
    sensors, own_time = measured.shape
    sources = lead_field.shape[1]
    frame_count = coefficients.shape[1]
    src_count = lax.axis_size("src")
    ngroups = sources * src_count // GROUP
    tau = group_weight * (GROUP * frame_count * lax.axis_size("frm") * K) ** 0.5
    time_start = lax.axis_index("frm") * own_time
    table = local_atoms(offsets, time_start, own_time + K)
    placing = local_placement(offsets, time_start, own_time + K)
    wave_table = window_basis()
    onehot = (group_ids[:, None] == jnp.arange(ngroups, dtype=jnp.int32)[None, :]).astype(
        jnp.float32
    )
    state = coefficients.reshape(sources, frame_count * K)
    residual = measured
    for iteration in range(ITERS):
        waveforms = jnp.einsum(
            "sfk,kt->sft",
            state.reshape(sources, frame_count, K),
            wave_table,
            precision=lax.Precision.HIGHEST,
        )
        weighted = (
            (depth[:, None, None] * waveforms)
            .astype(jnp.bfloat16)
            .reshape(sources, frame_count * K)
        )
        frame_sums = jnp.dot(lead_field, weighted, preferred_element_type=jnp.float32)
        summed = lax.psum(frame_sums, "src")
        residual = measured - intersection_add(summed, placing, own_time)
        residual_b = residual.astype(jnp.bfloat16)
        back = project_back(lead_field, depth, residual_b)
        following = from_behind(back[:, :K].astype(jnp.bfloat16), "frm", -1).astype(jnp.float32)
        widened = jnp.concatenate([back, following], axis=1)
        gradient = jnp.dot(widened, table.T, precision=lax.Precision.HIGHEST)
        moved = state + step_size * gradient
        shrunk = jnp.sign(moved) * jnp.maximum(jnp.abs(moved) - shrink_one, 0.0)
        own_power = jnp.dot(
            jnp.sum(shrunk * shrunk, axis=1), onehot, precision=lax.Precision.HIGHEST
        )
        power = lax.psum(own_power, ("src", "frm"))
        scale = jnp.maximum(0.0, 1.0 - tau / jnp.sqrt(power + epsilon))
        per_source = jnp.dot(onehot, scale, precision=lax.Precision.HIGHEST)
        state = shrunk * per_source[:, None]
    return (state.reshape(sources, frame_count, K), residual)


def solution(mesh):
    return jax.shard_map(
        shards,
        mesh=mesh,
        in_specs=(
            P(None, "frm"),
            P(None, "src"),
            P("src"),
            P("src", "frm", None),
            P("frm"),
            P("src"),
        ),
        out_specs=(P("src", "frm", None), P(None, "frm")),
        check_vma=False,
    )
```

profile of v0, /device:TPU:1, one launch (start us, length us, event | category | flops | bytes accessed | tf_op | source)
XLA Modules:
  0.0 982.4 jit_solution(17136710330690770639)
XLA Ops:
  7.3 6.5 fusion.3
  13.9 2.1 convolution_bitcast_fusion.2
  16.3 215.5 %all-reduce.4.cloned.1.call-done = f32[512,256]{0,1:T(8,128)} async-done(((f32[512,256]{0,1:T(8,128)}), f32[512,256]{0,1:T(8,128)}) %all-reduce.4.cloned.1.call-update) | async-done | bytes 524304 | tf_op jit(solution)/shard_map/psum | solution.py:92
  231.8 1.5 fusion.61
  233.3 5.3 collective-permute-start
  238.7 0.6 compare_reduce_fusion
  239.4 0.7 fusion.33
  240.1 2.9 fusion.8
  243.1 0.6 collective-permute-start.1
  244.0 0.9 fusion.30
  245.4 8.6 multiply_reduce_fusion.2
  254.0 1.4 fusion.14
  255.4 74.8 %psum.43 = f32[256]{0:T(256)S(1)} all-reduce(f32[256]{0:T(256)S(1)} %bitcast.93), channel_id=1, replica_groups=mesh['src'=128,'frm'=2] {'src','frm'}, use_global_device_ids=true, to_apply=%region_3.4 | all-reduce | flops 256 | bytes 2048 | tf_op jit(solution)/shard_map/psum | solution.py:104
  330.2 2.1 fusion.13
  332.4 2.9 broadcast_multiply_fusion.2
  335.3 2.1 copy-done.4
  337.4 4.5 fusion.4
  341.9 2.1 convolution_bitcast_fusion.1
  344.0 207.5 %all-reduce.6.cloned.1.call-done = f32[512,256]{0,1:T(8,128)} async-done(((f32[512,256]{0,1:T(8,128)}), f32[512,256]{0,1:T(8,128)}) %all-reduce.6.cloned.1.call-update) | async-done | bytes 524304 | tf_op jit(solution)/shard_map/psum | solution.py:92
  551.5 1.5 fusion.62
  553.0 5.5 collective-permute-start.2
  558.5 0.9 collective-permute-done.2
  559.4 0.7 fusion.34
  560.1 3.1 fusion.7
  563.3 0.4 collective-permute-start.3
  563.7 1.6 collective-permute-done.3
  565.3 7.0 multiply_reduce_fusion.1
  572.4 1.4 fusion.12
  573.8 74.8 %psum.45 = f32[256]{0:T(256)S(1)} all-reduce(f32[256]{0:T(256)S(1)} %bitcast.95), channel_id=1, replica_groups=mesh['src'=128,'frm'=2] {'src','frm'}, use_global_device_ids=true, to_apply=%region_6.7 | all-reduce | flops 256 | bytes 2048 | tf_op jit(solution)/shard_map/psum | solution.py:104
  648.6 2.1 fusion.11
  650.7 2.9 broadcast_multiply_fusion.1
  653.6 2.1 copy-done.3
  655.8 4.5 fusion.5
  660.2 2.1 convolution_bitcast_fusion
  662.3 207.6 %all-reduce.8.cloned.1.call-done = f32[512,256]{0,1:T(8,128)} async-done(((f32[512,256]{0,1:T(8,128)}), f32[512,256]{0,1:T(8,128)}) %all-reduce.8.cloned.1.call-update) | async-done | bytes 524304 | tf_op jit(solution)/shard_map/psum | solution.py:92
  870.0 1.5 fusion.63
  871.5 5.5 collective-permute-start.4
  877.0 0.9 collective-permute-done.4
  877.9 0.7 fusion.35
  878.6 2.9 fusion.6
  881.6 0.4 collective-permute-start.5
  882.0 0.8 copy.11
  882.9 0.7 collective-permute-done.5
  883.7 8.6 multiply_reduce_fusion
  892.3 1.4 fusion.10
  893.7 74.8 %psum.47 = f32[256]{0:T(256)S(1)} all-reduce(f32[256]{0:T(256)S(1)} %bitcast.97), channel_id=1, replica_groups=mesh['src'=128,'frm'=2] {'src','frm'}, use_global_device_ids=true, to_apply=%region_9.10 | all-reduce | flops 256 | bytes 2048 | tf_op jit(solution)/shard_map/psum | solution.py:104
  968.5 2.1 fusion.9
  970.6 4.8 broadcast_multiply_fusion
  (58 shorter events, 1.9 us)
Async XLA Ops:
  7.2 224.6 %all-reduce.4.cloned.1.call-start = ((), (), s32[]{:S(2)}) async-start(), calls=%async_computation | async-start | bytes 1048576 | tf_op jit(solution)/shard_map/psum | solution.py:92
  7.2 6.6 copy-start
  13.8 2.3 copy-start.11
  13.8 224.7 %copy-start.7 = (f32[512,128]{1,0:T(8,128)S(1)}, f32[512,128]{1,0:T(8,128)}, u32[]{:S(2)}) copy-start(f32[512,128]{1,0:T(8,128)} %param.12) | copy-start | bytes 786436
  13.8 226.3 %copy-start.6 = (f32[4096]{0:T(1024)S(1)}, f32[4096]{0:T(1024)}, u32[]{:S(2)}) copy-start(f32[4096]{0:T(1024)} %param.14) | copy-start | bytes 49156
  16.0 535.6 %all-reduce.6.cloned.1.call-start = ((), (), s32[]{:S(2)}) async-start(), calls=%async_computation.1 | async-start | bytes 1048576 | tf_op jit(solution)/shard_map/psum | solution.py:92
  233.3 6.2 collective-permute-start
  243.1 2.2 collective-permute-start.1
  245.0 9.0 copy-start.8
  245.4 8.6 copy-start.10
  335.2 2.1 copy-start.4
  335.2 6.6 copy-start.1
  344.0 526.0 %all-reduce.8.cloned.1.call-start = ((), (), s32[]{:S(2)}) async-start(), calls=%async_computation.2 | async-start | bytes 1048576 | tf_op jit(solution)/shard_map/psum | solution.py:92
  553.0 6.4 collective-permute-start.2
  560.1 5.2 copy-start.5
  560.1 5.2 copy-start.9
  563.3 2.0 collective-permute-start.3
  653.6 2.1 copy-start.3
  653.6 6.6 copy-start.2
  871.5 6.4 collective-permute-start.4
  881.6 2.0 collective-permute-start.5
Sparse Core Ops, SparseCore 0:
  16.1 215.6 all-reduce.3
  344.1 207.4 all-reduce.5
  662.5 207.4 all-reduce.7
where the time goes:
time: 989 us; the launch traced here: 982 us
  waiting for transfers between devices  635 us (64%)
  blocking collectives  225 us (23%)
  matrix products  69.8 us (7%)
  starting transfers between devices  17.9 us (2%)
  other arithmetic  14.8 us (1%)
  between operations  14.6 us (1%)
    psum x3, waiting for transfers between devices, shards(): summed = lax.psum(frame_sums, 'src')  631 us
    psum x3, blocking collectives, shards(): power = lax.psum(own_power, ('src', 'frm'))  225 us
    dot_general x3, matrix products, shards(): gradient = jnp.dot(widened, table.T, precision=lax.Precision.HIGHEST)  24.2 us
  transfers between devices with their start and end apart: 9, of which 9 were waited for; matrix products, arithmetic and copies ran while one was open for 0% of the time, Pallas kernels for 0%

commit v1 on v0

v1 whole, which is shorter than its diff:
```python
import functools

import jax
import jax.numpy as jnp
from jax import lax
from jax.experimental import pallas as pl
from jax.experimental.pallas import tpu as pltpu
from jax.sharding import PartitionSpec as P

K = 64
GROUP = 2048
ITERS = 3
LANES = 128
BLOCK = 512

step_size = 0.5
shrink_one = 0.05
group_weight = 0.03
epsilon = 1e-06

F32 = jnp.float32
BF16 = jnp.bfloat16
HIGHEST = lax.Precision.HIGHEST
EVERY = ("src", "frm")
PARAMS = pltpu.CompilerParams(vmem_limit_bytes=48 * 1024 * 1024)


def atoms_by_owner(offsets, samples, total):
    delay = (samples[None, None, :] - offsets[:, None, None]) % total
    delayf = delay.astype(F32)
    freq = jnp.arange(K, dtype=jnp.int32).astype(F32)[None, :, None]
    window = jnp.sin(jnp.pi * (delayf + 0.5) / K)
    basis = jnp.sqrt(2.0 / K) * jnp.cos(jnp.pi * (freq + 0.5) * (delayf + 0.5) / K)
    table = jnp.where(delay < K, window * basis, F32(0.0))
    return table.reshape(offsets.shape[0] * K, samples.shape[0])


def split(x):
    high = x.astype(BF16)
    return high, (x - high.astype(F32)).astype(BF16)


def against_sources(high, low, lead):
    both = jnp.concatenate([high, low], axis=0)
    product = lax.dot_general(both, lead, (((1,), (1,)), ((), ())), preferred_element_type=F32)
    rows = high.shape[0]
    return product[:rows] + product[rows:]


def to_samples(atoms_t, sums):
    return jnp.dot(atoms_t, sums, precision=HIGHEST, preferred_element_type=F32)


def first_kernel(coef_ref, depth_ref, lead_ref, atoms_t_ref, state_ref, out_ref, acc_ref):
    step = pl.program_id(0)
    frames = coef_ref.shape[1]
    for f in range(frames):
        state_ref[f * K : (f + 1) * K, :] = coef_ref[:, f, :].T
    high, low = split(state_ref[...] * depth_ref[...])
    part = against_sources(high, low, lead_ref[...])

    @pl.when(step == 0)
    def _():
        acc_ref[...] = part

    @pl.when(step != 0)
    def _():
        acc_ref[...] += part

    @pl.when(step == pl.num_programs(0) - 1)
    def _():
        out_ref[...] = to_samples(atoms_t_ref[...], acc_ref[...]).astype(BF16)


def forward_kernel(state_ref, weight_ref, lead_ref, atoms_t_ref, out_ref, acc_ref):
    step = pl.program_id(0)
    high, low = split(state_ref[...] * weight_ref[...])
    part = against_sources(high, low, lead_ref[...])

    @pl.when(step == 0)
    def _():
        acc_ref[...] = part

    @pl.when(step != 0)
    def _():
        acc_ref[...] += part

    @pl.when(step == pl.num_programs(0) - 1)
    def _():
        out_ref[...] = to_samples(atoms_t_ref[...], acc_ref[...]).astype(BF16)


def backward_kernel(
    edge_ref, res_ref, atoms_ref, state_ref, scale_ref, depth_ref, lead_ref, new_ref, power_ref, turned_ref
):
    step = pl.program_id(0)
    coefs, block = state_ref.shape

    @pl.when(step == 0)
    def _():
        turned = jnp.dot(
            atoms_ref[...], res_ref[...].astype(F32), precision=HIGHEST, preferred_element_type=F32
        )
        high, low = split(turned)
        turned_ref[:coefs, :] = high
        turned_ref[coefs:, :] = low
        power_ref[...] = jnp.zeros_like(power_ref)

    both = jnp.dot(turned_ref[...], lead_ref[...], preferred_element_type=F32)
    gradient = both[:coefs] + both[coefs:]
    moved = state_ref[...] * scale_ref[...] + (step_size * depth_ref[...]) * gradient
    shrunk = moved - jnp.clip(moved, -shrink_one, shrink_one)
    new_ref[...] = shrunk
    squares = jnp.sum(shrunk * shrunk, axis=0, keepdims=True)
    source = step * block + lax.broadcasted_iota(jnp.int32, (1, block), 1)
    edge = edge_ref[0]
    groups = (source < edge, (source >= edge) & (source < edge + GROUP), source >= edge + GROUP)
    for g, mine in enumerate(groups):
        power_ref[g : g + 1, :] += jnp.sum(jnp.where(mine, squares, 0.0), axis=1, keepdims=True)


def last_kernel(state_ref, scale_ref, out_ref):
    frames = out_ref.shape[1]
    scaled = state_ref[...] * scale_ref[...]
    for f in range(frames):
        out_ref[:, f, :] = scaled[f * K : (f + 1) * K, :].T


def columns(rows, block=BLOCK):
    return pl.BlockSpec((rows, block), lambda i: (0, i))


def whole(*shape):
    return pl.BlockSpec(shape, lambda i: (0,) * len(shape))


def shards(measured, lead_field, depth, coefficients, offsets, group_ids):
    sensors, own_time = measured.shape
    sources = lead_field.shape[1]
    frame_count = coefficients.shape[1]
    src_count, frm_count = lax.axis_size("src"), lax.axis_size("frm")
    devices = src_count * frm_count
    total = own_time * frm_count
    coefs = frame_count * K
    tau = group_weight * (GROUP * frame_count * frm_count * K) ** 0.5
    grid = (sources // BLOCK,)
    tiles = sensors // LANES

    place = jnp.arange(devices, dtype=jnp.int32)
    samples = (place % frm_count) * own_time + place // frm_count
    table = atoms_by_owner(offsets, samples, total)
    table_t = table.T
    own_row = lax.dynamic_slice_in_dim(measured, lax.axis_index("src"), 1, axis=1)
    own_row = own_row.reshape(tiles, LANES)
    depth_row = depth.reshape(1, sources)
    edge = jnp.sum((group_ids == group_ids[0]).astype(jnp.int32))
    source = jnp.arange(sources, dtype=jnp.int32)

    def exchange(rows):
        return lax.all_to_all(rows, EVERY, 0, 0, tiled=True)

    def broadcast(rows):
        return exchange(jnp.broadcast_to(rows[None], (devices,) + rows.shape))

    def owned_residual(predicted):
        arrived = exchange(predicted.reshape(devices, tiles, LANES))
        return own_row - jnp.sum(arrived.astype(F32), axis=0)

    state, predicted = pl.pallas_call(
        first_kernel,
        grid=grid,
        in_specs=[
            pl.BlockSpec((BLOCK, frame_count, K), lambda i: (i, 0, 0)),
            columns(1),
            columns(sensors),
            whole(total, coefs),
        ],
        out_specs=[columns(coefs), whole(total, sensors)],
        out_shape=[
            jax.ShapeDtypeStruct((coefs, sources), F32),
            jax.ShapeDtypeStruct((total, sensors), BF16),
        ],
        scratch_shapes=[pltpu.VMEM((coefs, sensors), F32)],
        compiler_params=PARAMS,
        name="first_forward",
    )(coefficients, depth_row, lead_field, table_t)

    scale_row = jnp.ones((1, sources), F32)
    for iteration in range(ITERS):
        row = owned_residual(predicted)
        if iteration < ITERS - 1:
            everyone = broadcast(row.astype(BF16)).reshape(total, sensors)
        else:
            high = lax.reduce_precision(row, 8, 7)
            both = jnp.concatenate([high, row - high], axis=0).astype(BF16)
            pair = broadcast(both).reshape(devices, 2, tiles, LANES)
            everyone = pair[:, 0].reshape(total, sensors)
            mine = pair.reshape(src_count, frm_count, 2, sensors)
            mine = lax.dynamic_index_in_dim(mine, lax.axis_index("frm"), 1, keepdims=False)
            residual = (mine[:, 0].astype(F32) + mine[:, 1].astype(F32)).T

        state, power = pl.pallas_call(
            backward_kernel,
            grid=grid,
            in_specs=[
                pl.BlockSpec(memory_space=pltpu.SMEM),
                whole(total, sensors),
                whole(coefs, total),
                columns(coefs),
                columns(1),
                columns(1),
                columns(sensors),
            ],
            out_specs=[columns(coefs), whole(8, LANES)],
            out_shape=[
                jax.ShapeDtypeStruct((coefs, sources), F32),
                jax.ShapeDtypeStruct((8, LANES), F32),
            ],
            scratch_shapes=[pltpu.VMEM((2 * coefs, sensors), BF16)],
            compiler_params=PARAMS,
            name="backward",
        )(edge[None], everyone, table, state, scale_row, depth_row, lead_field)

        chip = power + lax.ppermute(power, "frm", [(i, (i + 1) % frm_count) for i in range(frm_count)])
        ahead = [(i, (i + 1) % src_count) for i in range(src_count)]
        behind = [((i + 1) % src_count, i) for i in range(src_count)]
        before = lax.ppermute(chip, "src", ahead)
        after = lax.ppermute(chip, "src", behind)
        sums = jnp.stack([chip[0, 0] + before[2, 0], chip[1, 0], chip[2, 0] + after[0, 0]])
        scale = jnp.maximum(0.0, 1.0 - tau / jnp.sqrt(sums + epsilon))
        scale_row = jnp.where(
            source < edge, scale[0], jnp.where(source < edge + GROUP, scale[1], scale[2])
        )[None, :]
        if iteration < ITERS - 1:
            predicted = pl.pallas_call(
                forward_kernel,
                grid=grid,
                in_specs=[columns(coefs), columns(1), columns(sensors), whole(total, coefs)],
                out_specs=whole(total, sensors),
                out_shape=jax.ShapeDtypeStruct((total, sensors), BF16),
                scratch_shapes=[pltpu.VMEM((coefs, sensors), F32)],
                compiler_params=PARAMS,
                name="forward",
            )(state, depth_row * scale_row, lead_field, table_t)

    estimate = pl.pallas_call(
        last_kernel,
        grid=grid,
        in_specs=[columns(coefs), columns(1)],
        out_specs=pl.BlockSpec((BLOCK, frame_count, K), lambda i: (i, 0, 0)),
        out_shape=jax.ShapeDtypeStruct((sources, frame_count, K), F32),
        compiler_params=PARAMS,
        name="scaled_estimate",
    )(state, scale_row)
    return (estimate, residual)


def solution(mesh):
    return jax.shard_map(
        shards,
        mesh=mesh,
        in_specs=(
            P(None, "frm"),
            P(None, "src"),
            P("src"),
            P("src", "frm", None),
            P("frm"),
            P("src"),
        ),
        out_specs=(P("src", "frm", None), P(None, "frm")),
        check_vma=False,
    )
```

time: 989 us -> 298 us (0.30)
  waiting for transfers between devices: 635 us -> 62.5 us
  blocking collectives: 225 us -> 48.2 us
  matrix products: 69.8 us -> 0 us
  Pallas kernels: 0 us -> 61.6 us
  local copies, waits for them, and re-layouts: 5.68 us -> 42.4 us
  starting transfers between devices: 17.9 us -> 52.1 us
    psum x3 -> x0, waiting for transfers between devices: 631 us -> none  [shards(): summed = lax.psum(frame_sums, 'src')]
    psum x3 -> x0, blocking collectives: 225 us -> none  [shards(): power = lax.psum(own_power, ('src', 'frm'))]
    dot_general x21 -> x0, matrix products: 69.8 us -> none  [the longest x3 24.2 us: shards(): gradient = jnp.dot(widened, table.T, precision=lax.Precision.HIGHEST)]
    pallas_call x0 -> x7, Pallas kernels: none -> 61.6 us  [the longest x3 27.4 us: shards(): pl.pallas_call(backward_kernel, grid=grid, in_specs=[pl.BlockSpec(memory_...]
    all_to_all x0 -> x4, waiting for transfers between devices: none -> 59.5 us  [exchange(): return lax.all_to_all(rows, EVERY, 0, 0, tiled=True)]
    all_to_all x0 -> x2, blocking collectives: none -> 48.2 us  [exchange(): return lax.all_to_all(rows, EVERY, 0, 0, tiled=True)]
    all_to_all x0 -> x4, starting transfers between devices: none -> 31.3 us  [exchange(): return lax.all_to_all(rows, EVERY, 0, 0, tiled=True)]
    unnamed x26 -> x24, local copies, waits for them, and re-layouts: 5.26 us -> 30.3 us
  transfers between devices with their start and end apart: 9 -> 13, of which waited for: 9 -> 9; matrix products, arithmetic and copies ran while one was open for 0% -> 4% of each run, Pallas kernels for 0% -> 0%
where the time goes in v1:
time: 298 us; the launch traced here: 296 us
  waiting for transfers between devices  62.5 us (21%)
  Pallas kernels  61.6 us (21%)
  starting transfers between devices  52.1 us (17%)
  blocking collectives  48.2 us (16%)
  local copies, waits for them, and re-layouts  42.4 us (14%)
  other arithmetic  19.6 us (7%)
  between operations  9.36 us (3%)
    all_to_all x4, waiting for transfers between devices, exchange(): return lax.all_to_all(rows, EVERY, 0, 0, tiled=True)  59.5 us
    all_to_all x2, blocking collectives, exchange(): return lax.all_to_all(rows, EVERY, 0, 0, tiled=True)  48.2 us
    all_to_all x4, starting transfers between devices, exchange(): return lax.all_to_all(rows, EVERY, 0, 0, tiled=True)  31.3 us
    unnamed x24, local copies, waits for them, and re-layouts  30.3 us
    pallas_call x3, Pallas kernels, shards(): pl.pallas_call(backward_kernel, grid=grid, in_specs=[pl.BlockSpec(memory_...  27.4 us
    ppermute x3, starting transfers between devices, shards(): after = lax.ppermute(chip, 'src', behind)  19.1 us
    pallas_call x2, Pallas kernels, shards(): pl.pallas_call(forward_kernel, grid=grid, in_specs=[columns(coefs), colum...  15.4 us
    pallas_call x1, Pallas kernels, shards(): pl.pallas_call(first_kernel, grid=grid, in_specs=[pl.BlockSpec((BLOCK, fr...  11.3 us
  transfers between devices with their start and end apart: 13, of which 9 were waited for; matrix products, arithmetic and copies ran while one was open for 4% of the time, Pallas kernels for 0%

profile of v1, /device:TPU:1, one launch (start us, length us, event | category | flops | bytes accessed | tf_op | source)
XLA Modules:
  0.0 295.8 jit_solution(2701699929953047562)
XLA Ops:
  0.7 0.8 convert_add_fusion
  1.5 0.7 broadcast_compare_fusion
  2.3 0.9 fusion.atoms_ref
  3.4 8.4 %copy.29.coef_ref = f32[4096,4,64]{2,1,0:T(4,128)} copy(f32[4096,4,64]{0,2,1:T(8,128)} %param.9) | data formatting | bytes 8388608 | tf_op args[3]
  11.9 11.3 %first_forward.1 = (f32[256,4096]{1,0:T(8,128)S(1)}, bf16[256,512]{1,0:T(8,128)(2,1)S(1)}) custom-call(f32[4096,4,64]{2,1,0:T(4,128)} %copy.29.coef_ref, f32[1,4096]{1,0:T(1,128)S(1)} %bitcast.76, bf16[512,4096]{1,0:T(8,128)(2,1)} %lead_ref.11, f32[256,256]{1,0:T(8,128)S(1)} %copy.30.atoms_t_ref), custom_call_target="tpu_custom_call" | custom-call | tf_op jit(solution)/shard_map/first_forward/pallas_call | solution.py:169
  23.2 2.0 copy-done.6
  25.2 0.8 reshape.247
  25.9 15.7 %all-to-all-start = ((bf16[256,4,128]{2,1,0:T(4,128)(2,1)}), bf16[256,4,128]{2,1,0:T(4,128)(2,1)S(1)}, u32[]{:S(2)}, u32[]{:S(2)}) async-start(bf16[256,4,128]{2,1,0:T(4,128)(2,1)} %reshape.247), calls=%async_computation | async-start | bytes 524288 | tf_op jit(solution)/shard_map/all_to_all | solution.py:160
  41.8 15.2 %all-to-all-done = bf16[256,4,128]{2,1,0:T(4,128)(2,1)S(1)} async-done(((bf16[256,4,128]{2,1,0:T(4,128)(2,1)}), bf16[256,4,128]{2,1,0:T(4,128)(2,1)S(1)}, u32[]{:S(2)}, u32[]{:S(2)}) %all-to-all-start) | async-done | bytes 262176 | tf_op jit(solution)/shard_map/all_to_all | solution.py:160
  57.4 0.8 broadcast_in_dim.92
  58.2 5.2 %all-to-all-start.1 = ((bf16[256,4,128]{2,1,0:T(4,128)(2,1)}), bf16[256,4,128]{2,1,0:T(4,128)(2,1)S(1)}, u32[]{:S(2)}, u32[]{:S(2)}) async-start(bf16[256,4,128]{2,1,0:T(4,128)(2,1)} %broadcast_in_dim.92), calls=%async_computation.1 | async-start | bytes 524288 | tf_op jit(solution)/shard_map/all_to_all | solution.py:160
  63.9 1.3 convert_reduce_fusion.3
  65.2 13.6 %all-to-all-done.1 = bf16[256,4,128]{2,1,0:T(4,128)(2,1)S(1)} async-done(((bf16[256,4,128]{2,1,0:T(4,128)(2,1)}), bf16[256,4,128]{2,1,0:T(4,128)(2,1)S(1)}, u32[]{:S(2)}, u32[]{:S(2)}) %all-to-all-start.1) | async-done | bytes 262176 | tf_op jit(solution)/shard_map/all_to_all | solution.py:160
  78.8 9.1 %backward.3 = (f32[256,4096]{1,0:T(8,128)S(1)}, f32[8,128]{1,0:T(8,128)S(1)}) custom-call(s32[1]{0:T(128)} %bitcast.1.edge_ref, bf16[256,512]{1,0:T(8,128)(2,1)S(1)} %bitcast.73, f32[256,256]{1,0:T(8,128)S(1)} %fusion.atoms_ref, f32[256,4096]{1,0:T(8,128)} %copy-done.6, f32[1,4096]{1,0:T(1,128)S(1)} %broadcast_in_dim.93.scale_ref, f32[1,4096]{1,0:T(1,128)S(1)} %bitcast.77, ...), custom_call_target="tpu_custom_call" | custom-call | tf_op jit(solution)/shard_map/backward/pallas_call | solution.py:202
  88.0 2.0 copy-done.2
  91.4 6.6 %collective-permute-start.2 = (f32[8,128]{1,0:T(8,128)S(1)}, f32[8,128]{1,0:T(8,128)S(1)}, u32[]{:S(2)}, u32[]{:S(2)}) collective-permute-start(f32[8,128]{1,0:T(8,128)S(1)} %add.129), channel_id=1, source_target_pairs={{2,0},{4,2},{6,4},{8,6},{10,8},{12,10},{14,12},{16,14},{18,16},{20... | collective-permute-start | bytes 12296 | tf_op jit(solution)/shard_map/ppermute | solution.py:228
  102.8 0.7 subtract_maximum_fusion.2
  103.5 0.7 fusion.19
  104.2 2.5 select_multiply_fusion.1
  106.7 2.2 copy-done.3
  108.9 7.7 %forward.2 = bf16[256,512]{1,0:T(8,128)(2,1)S(1)} custom-call(f32[256,4096]{1,0:T(8,128)S(1)} %copy-done.3, f32[1,4096]{1,0:T(1,128)S(1)} %bitcast.81, bf16[512,4096]{1,0:T(8,128)(2,1)} %lead_ref.11, f32[256,256]{1,0:T(8,128)S(1)} %copy.30.atoms_t_ref), custom_call_target="tpu_custom_call" | custom-call | tf_op jit(solution)/shard_map/forward/pallas_call | solution.py:235
  116.7 24.1 %all_to_all.30 = bf16[256,4,128]{2,1,0:T(4,128)(2,1)S(1)} all-to-all(bf16[256,4,128]{2,1,0:T(4,128)(2,1)S(1)} %reshape.249), channel_id=1, replica_groups=mesh['src'=128,'frm'=2] {'src','frm'}, dimensions={0} | all-to-all | bytes 524288 | tf_op jit(solution)/shard_map/all_to_all | solution.py:160
  141.0 0.8 broadcast_in_dim.97
  141.8 5.3 %all-to-all-start.3 = ((bf16[256,4,128]{2,1,0:T(4,128)(2,1)}), bf16[256,4,128]{2,1,0:T(4,128)(2,1)S(1)}, u32[]{:S(2)}, u32[]{:S(2)}) async-start(bf16[256,4,128]{2,1,0:T(4,128)(2,1)} %broadcast_in_dim.97), calls=%async_computation.3 | async-start | bytes 524288 | tf_op jit(solution)/shard_map/all_to_all | solution.py:160
  147.1 2.6 select_select_fusion.2.scale_ref
  149.7 12.8 %all-to-all-done.3 = bf16[256,4,128]{2,1,0:T(4,128)(2,1)S(1)} async-done(((bf16[256,4,128]{2,1,0:T(4,128)(2,1)}), bf16[256,4,128]{2,1,0:T(4,128)(2,1)S(1)}, u32[]{:S(2)}, u32[]{:S(2)}) %all-to-all-start.3) | async-done | bytes 262176 | tf_op jit(solution)/shard_map/all_to_all | solution.py:160
  162.5 9.1 %backward.4 = (f32[256,4096]{1,0:T(8,128)S(1)}, f32[8,128]{1,0:T(8,128)S(1)}) custom-call(s32[1]{0:T(128)} %bitcast.1.edge_ref, bf16[256,512]{1,0:T(8,128)(2,1)S(1)} %bitcast.75, f32[256,256]{1,0:T(8,128)S(1)} %fusion.atoms_ref, f32[256,4096]{1,0:T(8,128)} %copy-done.2, f32[1,4096]{1,0:T(1,128)S(1)} %select_select_fusion.2.scale_ref, ...), custom_call_target="tpu_custom_call" | custom-call | tf_op jit(solution)/shard_map/backward/pallas_call | solution.py:202
  171.8 1.2 collective-permute-done.3
  173.2 6.6 %collective-permute-start.5 = (f32[8,128]{1,0:T(8,128)S(1)}, f32[8,128]{1,0:T(8,128)S(1)}, u32[]{:S(2)}, u32[]{:S(2)}) collective-permute-start(f32[8,128]{1,0:T(8,128)S(1)} %add.134), channel_id=1, source_target_pairs={{2,0},{4,2},{6,4},{8,6},{10,8},{12,10},{14,12},{16,14},{18,16},{20... | collective-permute-start | bytes 12296 | tf_op jit(solution)/shard_map/ppermute | solution.py:228
  184.4 0.7 subtract_maximum_fusion.1
  185.8 2.5 select_multiply_fusion
  188.3 7.7 %forward.3 = bf16[256,512]{1,0:T(8,128)(2,1)S(1)} custom-call(f32[256,4096]{1,0:T(8,128)S(1)} %get-tuple-element.14.state_ref, f32[1,4096]{1,0:T(1,128)S(1)} %bitcast.80, bf16[512,4096]{1,0:T(8,128)(2,1)} %lead_ref.11, f32[256,256]{1,0:T(8,128)S(1)} %copy.30.atoms_t_ref), custom_call_target="tpu_custom_call" | custom-call | tf_op jit(solution)/shard_map/forward/pallas_call | solution.py:235
  196.1 2.0 copy-done.1
  198.1 24.2 %all_to_all.31 = bf16[256,4,128]{2,1,0:T(4,128)(2,1)S(1)} all-to-all(bf16[256,4,128]{2,1,0:T(4,128)(2,1)S(1)} %reshape.251), channel_id=1, replica_groups=mesh['src'=128,'frm'=2] {'src','frm'}, dimensions={0} | all-to-all | bytes 524288 | tf_op jit(solution)/shard_map/all_to_all | solution.py:160
  222.6 0.9 broadcast_in_dim.104
  223.5 5.2 %all-to-all-start.5 = ((bf16[256,8,128]{2,1,0:T(8,128)(2,1)}), bf16[256,8,128]{2,1,0:T(8,128)(2,1)S(1)}, u32[]{:S(2)}, u32[]{:S(2)}) async-start(bf16[256,8,128]{2,1,0:T(8,128)(2,1)} %broadcast_in_dim.104), calls=%async_computation.5 | async-start | bytes 1048576 | tf_op jit(solution)/shard_map/all_to_all | solution.py:160
  228.7 2.6 select_select_fusion.1.scale_ref
  231.2 18.0 %all-to-all-done.5 = bf16[256,8,128]{2,1,0:T(8,128)(2,1)S(1)} async-done(((bf16[256,8,128]{2,1,0:T(8,128)(2,1)}), bf16[256,8,128]{2,1,0:T(8,128)(2,1)S(1)}, u32[]{:S(2)}, u32[]{:S(2)}) %all-to-all-start.5) | async-done | bytes 524320 | tf_op jit(solution)/shard_map/all_to_all | solution.py:160
  249.6 9.1 %backward.5 = (f32[256,4096]{1,0:T(8,128)S(1)}, f32[8,128]{1,0:T(8,128)S(1)}) custom-call(s32[1]{0:T(128)} %bitcast.1.edge_ref, bf16[256,512]{1,0:T(8,128)(2,1)S(1)} %bitcast.74, f32[256,256]{1,0:T(8,128)S(1)} %fusion.atoms_ref, f32[256,4096]{1,0:T(8,128)} %copy-done.1, f32[1,4096]{1,0:T(1,128)S(1)} %select_select_fusion.1.scale_ref, ...), custom_call_target="tpu_custom_call" | custom-call | tf_op jit(solution)/shard_map/backward/pallas_call | solution.py:202
  258.7 2.0 copy-done.4
  261.2 0.8 copy.37
  262.1 1.0 collective-permute-start.7
  263.1 5.9 %collective-permute-start.8 = (f32[8,128]{1,0:T(8,128)S(1)}, f32[8,128]{1,0:T(8,128)S(1)}, u32[]{:S(2)}, u32[]{:S(2)}) collective-permute-start(f32[8,128]{1,0:T(8,128)S(1)} %add.138), channel_id=1, source_target_pairs={{2,0},{4,2},{6,4},{8,6},{10,8},{12,10},{14,12},{16,14},{18,16},{20... | collective-permute-start | bytes 12296 | tf_op jit(solution)/shard_map/ppermute | solution.py:228
  273.6 0.7 subtract_maximum_fusion
  275.0 2.6 select_select_fusion.scale_ref
  277.6 2.2 copy-done.5
  279.8 7.5 %scaled_estimate.1 = f32[4096,4,64]{2,1,0:T(4,128)} custom-call(f32[256,4096]{1,0:T(8,128)S(1)} %copy-done.5, f32[1,4096]{1,0:T(1,128)S(1)} %select_select_fusion.scale_ref), custom_call_target="tpu_custom_call" | custom-call | tf_op jit(solution)/shard_map/scaled_estimate/pallas_call | solution.py:246
  287.3 8.5 %copy.36 = f32[4096,4,64]{0,2,1:T(8,128)} copy(f32[4096,4,64]{2,1,0:T(4,128)} %scaled_estimate.1) | data formatting | bytes 8388608
  (66 shorter events, 11.8 us)
Async XLA Ops:
  0.6 41.0 %copy-start = (f32[512,128]{1,0:T(8,128)S(1)}, f32[512,128]{1,0:T(8,128)}, u32[]{:S(2)}) copy-start(f32[512,128]{1,0:T(8,128)} %param.6) | copy-start | bytes 786436
  3.4 8.5 %copy-start.7 = (f32[4096]{0:T(1024)S(1)}, f32[4096]{0:T(1024)}, u32[]{:S(2)}) copy-start(f32[4096]{0:T(1024)} %param.8) | copy-start | bytes 49156
  11.9 51.5 %copy-start.8 = (s32[4096]{0:T(1024)S(1)}, s32[4096]{0:T(1024)}, u32[]{:S(2)}) copy-start(s32[4096]{0:T(1024)} %param.11) | copy-start | bytes 49156
  23.1 2.0 copy-start.6
  25.9 31.2 %all-to-all-start = ((bf16[256,4,128]{2,1,0:T(4,128)(2,1)}), bf16[256,4,128]{2,1,0:T(4,128)(2,1)S(1)}, u32[]{:S(2)}, u32[]{:S(2)}) async-start(bf16[256,4,128]{2,1,0:T(4,128)(2,1)} %reshape.247), calls=%async_computation | async-start | bytes 524288 | tf_op jit(solution)/shard_map/all_to_all | solution.py:160
  58.2 20.6 %all-to-all-start.1 = ((bf16[256,4,128]{2,1,0:T(4,128)(2,1)}), bf16[256,4,128]{2,1,0:T(4,128)(2,1)S(1)}, u32[]{:S(2)}, u32[]{:S(2)}) async-start(bf16[256,4,128]{2,1,0:T(4,128)(2,1)} %broadcast_in_dim.92), calls=%async_computation.1 | async-start | bytes 524288 | tf_op jit(solution)/shard_map/all_to_all | solution.py:160
  88.0 2.0 copy-start.2
  90.0 1.2 collective-permute-start
  91.2 7.9 %collective-permute-start.1 = (f32[8,128]{1,0:T(8,128)S(1)}, f32[8,128]{1,0:T(8,128)S(1)}, u32[]{:S(2)}, u32[]{:S(2)}) collective-permute-start(f32[8,128]{1,0:T(8,128)S(1)} %add.129), channel_id=1, source_target_pairs={{0,2},{2,4},{4,6},{6,8},{8,10},{10,12},{12,14},{14,16},{16,18},{18... | collective-permute-start | bytes 12296 | tf_op jit(solution)/shard_map/ppermute | solution.py:227
  91.4 9.5 %collective-permute-start.2 = (f32[8,128]{1,0:T(8,128)S(1)}, f32[8,128]{1,0:T(8,128)S(1)}, u32[]{:S(2)}, u32[]{:S(2)}) collective-permute-start(f32[8,128]{1,0:T(8,128)S(1)} %add.129), channel_id=1, source_target_pairs={{2,0},{4,2},{6,4},{8,6},{10,8},{12,10},{14,12},{16,14},{18,16},{20... | collective-permute-start | bytes 12296 | tf_op jit(solution)/shard_map/ppermute | solution.py:228
  106.7 2.2 copy-start.3
  141.8 20.7 %all-to-all-start.3 = ((bf16[256,4,128]{2,1,0:T(4,128)(2,1)}), bf16[256,4,128]{2,1,0:T(4,128)(2,1)S(1)}, u32[]{:S(2)}, u32[]{:S(2)}) async-start(bf16[256,4,128]{2,1,0:T(4,128)(2,1)} %broadcast_in_dim.97), calls=%async_computation.3 | async-start | bytes 524288 | tf_op jit(solution)/shard_map/all_to_all | solution.py:160
  171.7 1.2 collective-permute-start.3
  172.9 7.9 %collective-permute-start.4 = (f32[8,128]{1,0:T(8,128)S(1)}, f32[8,128]{1,0:T(8,128)S(1)}, u32[]{:S(2)}, u32[]{:S(2)}) collective-permute-start(f32[8,128]{1,0:T(8,128)S(1)} %add.134), channel_id=1, source_target_pairs={{0,2},{2,4},{4,6},{6,8},{8,10},{10,12},{12,14},{14,16},{16,18},{18... | collective-permute-start | bytes 12296 | tf_op jit(solution)/shard_map/ppermute | solution.py:227
  173.2 9.4 %collective-permute-start.5 = (f32[8,128]{1,0:T(8,128)S(1)}, f32[8,128]{1,0:T(8,128)S(1)}, u32[]{:S(2)}, u32[]{:S(2)}) collective-permute-start(f32[8,128]{1,0:T(8,128)S(1)} %add.134), channel_id=1, source_target_pairs={{2,0},{4,2},{6,4},{8,6},{10,8},{12,10},{14,12},{16,14},{18,16},{20... | collective-permute-start | bytes 12296 | tf_op jit(solution)/shard_map/ppermute | solution.py:228
  196.0 2.0 copy-start.1
  223.5 25.7 %all-to-all-start.5 = ((bf16[256,8,128]{2,1,0:T(8,128)(2,1)}), bf16[256,8,128]{2,1,0:T(8,128)(2,1)S(1)}, u32[]{:S(2)}, u32[]{:S(2)}) async-start(bf16[256,8,128]{2,1,0:T(8,128)(2,1)} %broadcast_in_dim.104), calls=%async_computation.5 | async-start | bytes 1048576 | tf_op jit(solution)/shard_map/all_to_all | solution.py:160
  258.7 2.0 copy-start.4
  260.7 1.3 collective-permute-start.6
  262.1 7.9 %collective-permute-start.7 = (f32[8,128]{1,0:T(8,128)S(1)}, f32[8,128]{1,0:T(8,128)S(1)}, u32[]{:S(2)}, u32[]{:S(2)}) collective-permute-start(f32[8,128]{1,0:T(8,128)S(1)} %add.138), channel_id=1, source_target_pairs={{0,2},{2,4},{4,6},{6,8},{8,10},{10,12},{12,14},{14,16},{16,18},{18... | collective-permute-start | bytes 12296 | tf_op jit(solution)/shard_map/ppermute | solution.py:227
  263.1 8.6 %collective-permute-start.8 = (f32[8,128]{1,0:T(8,128)S(1)}, f32[8,128]{1,0:T(8,128)S(1)}, u32[]{:S(2)}, u32[]{:S(2)}) collective-permute-start(f32[8,128]{1,0:T(8,128)S(1)} %add.138), channel_id=1, source_target_pairs={{2,0},{4,2},{6,4},{8,6},{10,8},{12,10},{14,12},{16,14},{18,16},{20... | collective-permute-start | bytes 12296 | tf_op jit(solution)/shard_map/ppermute | solution.py:228
  277.6 2.2 copy-start.5

commit v2 on v0

v2 whole, which is shorter than its diff:
```python
import math

import jax
import jax.numpy as jnp
import numpy as np
from jax import lax
from jax.experimental import pallas as pl
from jax.experimental.pallas import tpu as pltpu
from jax.sharding import PartitionSpec as P

K = 64
GROUP = 2048
ITERS = 3
LANES = 128
BLOCK = 512

step_size = 0.5
shrink_one = 0.05
group_weight = 0.03
epsilon = 1e-06

F32 = jnp.float32
BF16 = jnp.bfloat16
HIGHEST = lax.Precision.HIGHEST
PARAMS = pltpu.CompilerParams(vmem_limit_bytes=24 * 1024 * 1024)


def windowed_cosines():
    t = np.arange(K)[:, None] + 0.5
    k = np.arange(K)[None, :] + 0.5
    return (np.sin(np.pi * t / K) * np.sqrt(2.0 / K) * np.cos(np.pi * k * t / K)).astype(np.float32)


def split(x):
    high = x.astype(BF16)
    return high, (x - high.astype(F32)).astype(BF16)


def dot(a, b):
    return jnp.dot(a, b, preferred_element_type=F32)


def dot_t(a, b):
    return lax.dot_general(a, b, (((1,), (1,)), ((), ())), preferred_element_type=F32)


def to_samples(atoms_ref, sums):
    high, low = split(sums)
    return dot(atoms_ref[0], high) + dot(atoms_ref[0], low) + dot(atoms_ref[1], high)


def group_scale(power, tau):
    return jnp.maximum(0.0, 1.0 - tau / jnp.sqrt(power + epsilon))


def first_kernel(
    offsets_ref, place_ref, wave_ref, coef_ref, depth_ref, lead_ref,
    table_ref, table_t_ref, mine_ref, theirs_ref, acc_ref,
):
    step = pl.program_id(0)
    total = table_ref.shape[2]
    own = mine_ref.shape[0]

    @pl.when(step == 0)
    def _():
        acc_ref[...] = jnp.zeros_like(acc_ref)
        wave = wave_ref[...]
        order = lax.broadcasted_iota(jnp.int32, (total, K), 0)
        sample = (order + place_ref[0]) % total
        position = lax.broadcasted_iota(jnp.int32, (total, K), 1)
        for f in range(offsets_ref.shape[0]):
            delay = (sample - offsets_ref[f] + total) % total
            placing = (delay == position).astype(F32)
            part_t = jnp.dot(placing, wave, precision=HIGHEST, preferred_element_type=F32)
            rows = slice(f * K, (f + 1) * K)
            table_t_ref[0, :, rows], table_t_ref[1, :, rows] = split(part_t)
            table_ref[0, rows, :], table_ref[1, rows, :] = split(part_t.T)

    weighted = (coef_ref[...] * depth_ref[...]).astype(BF16)
    acc_ref[...] += dot_t(weighted, lead_ref[...])

    @pl.when(step == pl.num_programs(0) - 1)
    def _():
        samples = to_samples(table_t_ref, acc_ref[...])
        mine_ref[...] = samples[:own]
        theirs_ref[...] = samples[own:].astype(BF16)


def step_kernel(
    edge_ref, own_ref, other_ref, table_ref, table_t_ref, state_ref, scale_ref, depth_ref, lead_ref,
    new_ref, power_ref, *rest, width, predict,
):
    if predict:
        mine_ref, theirs_ref, turned_ref, rows_ref, acc_ref = rest
    else:
        turned_ref, rows_ref = rest
    step = pl.program_id(0)
    coefs, block = state_ref.shape
    sensors = lead_ref.shape[0]
    tiles = sensors // LANES
    own = table_ref.shape[2] // 2

    @pl.when(step == 0)
    def _():
        for h, ref in enumerate((own_ref, other_ref)):
            rows_ref[h, : ref.shape[0]] = ref[...].astype(F32)
        for t in range(tiles):
            lanes = slice(t * LANES, (t + 1) * LANES)
            turned = jnp.zeros((coefs, LANES), F32)
            for h, apart in enumerate((width, tiles)):
                samples = rows_ref[h, pl.ds(t, own, stride=apart), :].astype(BF16)
                cols = slice(h * own, (h + 1) * own)
                turned += dot(table_ref[0, :, cols], samples) + dot(table_ref[1, :, cols], samples)
            turned_ref[:coefs, lanes], turned_ref[coefs:, lanes] = split(turned)
        power_ref[...] = jnp.zeros_like(power_ref)
        if predict:
            acc_ref[...] = jnp.zeros_like(acc_ref)

    lead = lead_ref[...]
    both = dot(turned_ref[...], lead)
    first = step * block
    source = first + lax.broadcasted_iota(jnp.int32, (1, block), 1)
    start = edge_ref[0]
    end = start + GROUP
    scale = jnp.where(
        source < start, scale_ref[0:1, 0:1], jnp.where(source < end, scale_ref[1:2, 0:1], scale_ref[2:3, 0:1])
    )
    depth = depth_ref[...]
    moved = state_ref[...] * scale + (step_size * depth) * (both[:coefs] + both[coefs:])
    shrunk = moved - jnp.clip(moved, -shrink_one, shrink_one)
    new_ref[...] = shrunk
    squares = jnp.sum(shrunk * shrunk, axis=0, keepdims=True)
    groups = (source < start, (source >= start) & (source < end), source >= end)
    for g, inside in enumerate(groups):
        power_ref[g : g + 1, :] += jnp.sum(jnp.where(inside, squares, 0.0), axis=1, keepdims=True)

    if predict:
        weighted = shrunk * depth
        part = (first >= start).astype(jnp.int32) + (first >= end).astype(jnp.int32)
        bound = jnp.where(part == 0, start, jnp.where(part == 1, end, pl.num_programs(0) * block))
        before = source < bound
        rows = pl.ds(pl.multiple_of(part * coefs, coefs), coefs)
        acc_ref[rows, :] += dot_t(jnp.where(before, weighted, 0.0).astype(BF16), lead)

        @pl.when(bound < first + block)
        def _():
            later = pl.ds(pl.multiple_of((part + 1) * coefs, coefs), coefs)
            acc_ref[later, :] += dot_t(jnp.where(before, 0.0, weighted).astype(BF16), lead)

        @pl.when(step == pl.num_programs(0) - 1)
        def _():
            for g in range(3):
                samples = to_samples(table_t_ref, acc_ref[g * coefs : (g + 1) * coefs, :])
                mine_ref[g * own : (g + 1) * own, :] = samples[:own]
                theirs_ref[g * own : (g + 1) * own, :] = samples[own:].astype(BF16)
            high, low = split(power_ref[...])
            for t in range(tiles):
                lanes = slice(t * LANES, (t + 1) * LANES)
                theirs_ref[3 * own : 3 * own + 16, lanes] = jnp.concatenate([high, low], axis=0)


def first_fold_kernel(mine_ref, theirs_ref, out_ref, rows_ref):
    own = mine_ref.shape[0]
    tiles = mine_ref.shape[1] // LANES
    for t in range(tiles):
        lanes = slice(t * LANES, (t + 1) * LANES)
        rows_ref[pl.ds(t, own, stride=tiles), :] = mine_ref[:, lanes] + theirs_ref[:, lanes].astype(F32)
    out_ref[...] = rows_ref[...].astype(BF16)


def fold_kernel(mine_ref, theirs_ref, power_ref, out_ref, chip_ref, rows_ref, *, tau):
    own = mine_ref.shape[0] // 3
    tiles = mine_ref.shape[1] // LANES
    theirs = theirs_ref[3 * own : 3 * own + 16, :LANES].astype(F32)
    chip = power_ref[...] + theirs[:8] + theirs[8:]
    chip_ref[...] = chip
    middle = group_scale(chip[1:2, :], tau)
    for g, part in enumerate((1, 0, 2)):
        for t in range(tiles):
            lanes = slice(t * LANES, (t + 1) * LANES)
            rows = slice(part * own, (part + 1) * own)
            total = mine_ref[rows, lanes] + theirs_ref[rows, lanes].astype(F32)
            if part == 1:
                total = total * middle
            rows_ref[pl.ds(g * tiles + t, own, stride=16), :] = total
    for g, part in enumerate((0, 2)):
        value = chip[part : part + 1, :]
        high = value.astype(BF16).astype(F32)
        for n, term in enumerate((high, value - high)):
            at = 3 * tiles + 2 * g + n
            rows_ref[pl.ds(at, own, stride=16), :] = jnp.broadcast_to(term, (own, LANES))
    out_ref[...] = rows_ref[...].astype(BF16)


def send_residual(row, out_ref, rows_ref, tiles, last):
    own = out_ref.shape[0] // (2 * tiles if last else tiles)
    if last:
        high = row.astype(BF16).astype(F32)
        row = jnp.concatenate([high, row - high], axis=0)
    out_ref[...] = jnp.concatenate([row.astype(BF16)] * own, axis=0)


def first_owner_kernel(got_ref, measured_ref, out_ref, rows_ref):
    tiles = measured_ref.shape[0]
    senders = got_ref.shape[0] // tiles
    rows_ref[...] = got_ref[...].astype(F32)
    row = [
        measured_ref[t : t + 1, :]
        - jnp.sum(rows_ref[pl.ds(t, senders, stride=tiles), :], axis=0, keepdims=True)
        for t in range(tiles)
    ]
    send_residual(jnp.concatenate(row, axis=0), out_ref, rows_ref, tiles, False)


def owner_kernel(me_ref, got_ref, measured_ref, chip_ref, out_ref, scale_ref, rows_ref, edges_ref, *, tau, last):
    tiles = measured_ref.shape[0]
    senders = got_ref.shape[0] // 16
    rows_ref[...] = got_ref[...].astype(F32)

    def of(k):
        return rows_ref[pl.ds(k, senders, stride=16), :]

    front = of(3 * tiles) + of(3 * tiles + 1)
    back = of(3 * tiles + 2) + of(3 * tiles + 3)
    before = jnp.concatenate([back[senders - 1 :], back[: senders - 1]], axis=0)
    front_scale = group_scale(front + before, tau)
    back_scale = jnp.concatenate([front_scale[1:], front_scale[:1]], axis=0)
    row = []
    for t in range(tiles):
        parts = of(t) + front_scale * of(tiles + t) + back_scale * of(2 * tiles + t)
        row.append(measured_ref[t : t + 1, :] - jnp.sum(parts, axis=0, keepdims=True))
    send_residual(jnp.concatenate(row, axis=0), out_ref, rows_ref, tiles, last)
    edges_ref[0] = front_scale
    edges_ref[1] = back_scale
    me = me_ref[0]
    scale_ref[...] = jnp.zeros_like(scale_ref)
    scale_ref[0:1, :] = edges_ref[0, pl.ds(me, 1), :]
    scale_ref[1:2, :] = group_scale(chip_ref[1:2, :], tau)
    scale_ref[2:3, :] = edges_ref[1, pl.ds(me, 1), :]


def residual_kernel(own_ref, out_ref, rows_ref):
    own = out_ref.shape[1]
    tiles = out_ref.shape[0] // LANES
    rows_ref[...] = own_ref[...].astype(F32)
    for t in range(tiles):
        high = rows_ref[pl.ds(t, own, stride=2 * tiles), :]
        low = rows_ref[pl.ds(tiles + t, own, stride=2 * tiles), :]
        out_ref[t * LANES : (t + 1) * LANES, :] = (high + low).T


def last_kernel(edge_ref, state_ref, chip_ref, before_ref, after_ref, out_ref, *, tau):
    block = state_ref.shape[1]
    source = pl.program_id(0) * block + lax.broadcasted_iota(jnp.int32, (1, block), 1)
    first = group_scale(chip_ref[0:1, 0:1] + before_ref[2:3, 0:1], tau)
    middle = group_scale(chip_ref[1:2, 0:1], tau)
    last = group_scale(chip_ref[2:3, 0:1] + after_ref[0:1, 0:1], tau)
    start = edge_ref[0]
    scale = jnp.where(source < start, first, jnp.where(source < start + GROUP, middle, last))
    out_ref[...] = state_ref[...] * scale


def columns(rows, block=BLOCK):
    return pl.BlockSpec((rows, block), lambda i: (0, i))


def whole(*shape):
    return pl.BlockSpec(shape, lambda i: (0,) * len(shape))


SMEM = pl.BlockSpec(memory_space=pltpu.SMEM)
VMEM = pl.BlockSpec(memory_space=pltpu.VMEM)


def shards(measured, lead_field, depth, coefficients, offsets, group_ids):
    sensors, own = measured.shape
    sources = lead_field.shape[1]
    frames = coefficients.shape[1]
    src_count, frm_count = lax.axis_size("src"), lax.axis_size("frm")
    total = own * frm_count
    coefs = frames * K
    tau = group_weight * math.sqrt(GROUP * frames * frm_count * K)
    grid = (sources // BLOCK,)
    tiles = sensors // LANES
    across = [(i, (i + 1) % frm_count) for i in range(frm_count)]
    ahead = [(i, (i + 1) % src_count) for i in range(src_count)]
    behind = [((i + 1) % src_count, i) for i in range(src_count)]

    me = lax.axis_index("src")
    place = (lax.axis_index("frm") * own)[None]
    own_row = lax.dynamic_slice_in_dim(measured, me, 1, axis=1).reshape(tiles, LANES)
    depth_row = depth.reshape(1, sources)
    edge = jnp.sum((group_ids == group_ids[0]).astype(jnp.int32))[None]

    def struct(dtype, *shape):
        return jax.ShapeDtypeStruct(shape, dtype)

    def call(kernel, name, ins, outs, scratch=()):
        return pl.pallas_call(
            kernel, in_specs=ins, out_specs=[VMEM] * len(outs), out_shape=outs,
            scratch_shapes=list(scratch), compiler_params=PARAMS, name=name,
        )

    def exchange(rows):
        return lax.all_to_all(rows, "src", 0, 0, tiled=True)

    state = coefficients.transpose(1, 2, 0).reshape(coefs, sources)
    table, table_t, mine, theirs = pl.pallas_call(
        first_kernel,
        grid=grid,
        in_specs=[SMEM, SMEM, whole(K, K), columns(coefs), columns(1), columns(sensors)],
        out_specs=[whole(2, coefs, total), whole(2, total, coefs), whole(own, sensors), whole(own, sensors)],
        out_shape=[
            struct(BF16, 2, coefs, total),
            struct(BF16, 2, total, coefs),
            struct(F32, own, sensors),
            struct(BF16, own, sensors),
        ],
        scratch_shapes=[pltpu.VMEM((coefs, sensors), F32)],
        compiler_params=PARAMS,
        name="first_forward",
    )(offsets, place, jnp.asarray(windowed_cosines()), state, depth_row, lead_field)

    folded = call(
        first_fold_kernel,
        "first_fold",
        [VMEM, VMEM],
        [struct(BF16, own * tiles, LANES)],
        [pltpu.VMEM((own * tiles, LANES), F32)],
    )(mine, lax.ppermute(theirs, "frm", across))[0]
    scale = jnp.ones((8, LANES), F32)
    for iteration in range(ITERS):
        last = iteration == ITERS - 1
        got = exchange(folded)
        width = 2 * tiles if last else tiles
        if iteration == 0:
            row = call(
                first_owner_kernel,
                "first_owner",
                [VMEM, VMEM],
                [struct(BF16, own * width, LANES)],
                [pltpu.VMEM((src_count * tiles, LANES), F32)],
            )(got, own_row)[0]
        else:
            row, scale = call(
                lambda *refs, last=last: owner_kernel(*refs, tau=tau, last=last),
                "owner",
                [SMEM, VMEM, VMEM, VMEM],
                [struct(BF16, own * width, LANES), struct(F32, 8, LANES)],
                [pltpu.VMEM((src_count * 16, LANES), F32), pltpu.VMEM((2, src_count, LANES), F32)],
            )(me[None], got, own_row, chip)
        mine = exchange(row)
        send = mine.reshape(own, width, LANES)[:, :tiles].reshape(own * tiles, LANES) if last else mine
        others = lax.ppermute(send, "frm", across)

        outs = [struct(F32, coefs, sources), struct(F32, 8, LANES)]
        out_specs = [columns(coefs), whole(8, LANES)]
        scratch = [pltpu.VMEM((2 * coefs, sensors), BF16), pltpu.VMEM((2, own * width, LANES), F32)]
        if not last:
            outs += [struct(F32, 3 * own, sensors), struct(BF16, 3 * own + 16, sensors)]
            out_specs += [whole(3 * own, sensors), whole(3 * own + 16, sensors)]
            scratch += [pltpu.VMEM((3 * coefs, sensors), F32)]
        results = pl.pallas_call(
            lambda *refs, width=width, last=last: step_kernel(*refs, width=width, predict=not last),
            grid=grid,
            in_specs=[
                SMEM,
                whole(own * width, LANES),
                whole(own * tiles, LANES),
                whole(2, coefs, total),
                whole(2, total, coefs),
                columns(coefs),
                whole(8, LANES),
                columns(1),
                columns(sensors),
            ],
            out_specs=out_specs,
            out_shape=outs,
            scratch_shapes=scratch,
            compiler_params=PARAMS,
            name="step",
        )(edge, mine, others, table, table_t, state, scale, depth_row, lead_field)
        state, power = results[:2]
        if last:
            break
        folded, chip = call(
            lambda *refs: fold_kernel(*refs, tau=tau),
            "fold",
            [VMEM, VMEM, VMEM],
            [struct(BF16, own * 16, LANES), struct(F32, 8, LANES)],
            [pltpu.VMEM((own * 16, LANES), F32)],
        )(results[2], lax.ppermute(results[3], "frm", across), power)

    chip = power + lax.ppermute(power, "frm", across)
    before = lax.ppermute(chip, "src", ahead)
    after = lax.ppermute(chip, "src", behind)
    residual = call(
        residual_kernel,
        "residual",
        [VMEM],
        [struct(F32, sensors, own)],
        [pltpu.VMEM((own * 2 * tiles, LANES), F32)],
    )(mine)[0]
    estimate = pl.pallas_call(
        lambda *refs: last_kernel(*refs, tau=tau),
        grid=grid,
        in_specs=[SMEM, columns(coefs), whole(8, LANES), whole(8, LANES), whole(8, LANES)],
        out_specs=columns(coefs),
        out_shape=struct(F32, coefs, sources),
        compiler_params=PARAMS,
        name="scaled_estimate",
    )(edge, state, chip, before, after)
    return (estimate.reshape(frames, K, sources).transpose(2, 0, 1), residual)


def solution(mesh):
    return jax.shard_map(
        shards,
        mesh=mesh,
        in_specs=(
            P(None, "frm"),
            P(None, "src"),
            P("src"),
            P("src", "frm", None),
            P("frm"),
            P("src"),
        ),
        out_specs=(P("src", "frm", None), P(None, "frm")),
        check_vma=False,
    )
```

time: 989 us -> 208 us (0.21)
  waiting for transfers between devices: 635 us -> 24.5 us
  blocking collectives: 225 us -> 102 us
  matrix products: 69.8 us -> 0 us
  Pallas kernels: 0 us -> 38.6 us
  between operations: 14.6 us -> 0.76 us
  other arithmetic: 14.8 us -> 1.29 us
  starting transfers between devices: 17.9 us -> 29.1 us
    psum x3 -> x0, waiting for transfers between devices: 631 us -> none  [shards(): summed = lax.psum(frame_sums, 'src')]
    psum x3 -> x0, blocking collectives: 225 us -> none  [shards(): power = lax.psum(own_power, ('src', 'frm'))]
    all_to_all x0 -> x5, blocking collectives: none -> 102 us  [exchange(): return lax.all_to_all(rows, 'src', 0, 0, tiled=True)]
    dot_general x21 -> x0, matrix products: 69.8 us -> none  [the longest x3 24.2 us: shards(): gradient = jnp.dot(widened, table.T, precision=lax.Precision.HIGHEST)]
    pallas_call x0 -> x12, Pallas kernels: none -> 38.6 us  [the longest x3 24.8 us: shards(): pl.pallas_call(lambda *refs, width=width, last=last: step_kernel(*refs, w...]
    all_to_all x0 -> x1, starting transfers between devices: none -> 13.8 us  [exchange(): return lax.all_to_all(rows, 'src', 0, 0, tiled=True)]
    all_to_all x0 -> x1, waiting for transfers between devices: none -> 10.7 us  [exchange(): return lax.all_to_all(rows, 'src', 0, 0, tiled=True)]
    mul x5 -> x0, other arithmetic: 10.6 us -> none  [the longest x3 10.6 us: shards(): state = shrunk * per_source[:, None]]
  transfers between devices with their start and end apart: 9 -> 10, of which waited for: 9 -> 9; matrix products, arithmetic and copies ran while one was open for 0% -> 1% of each run, Pallas kernels for 0% -> 0%
where the time goes in v2:
time: 208 us
  blocking collectives  102 us (49%)
  Pallas kernels  38.6 us (19%)
  starting transfers between devices  29.1 us (14%)
  waiting for transfers between devices  24.5 us (12%)
  local copies, waits for them, and re-layouts  11.7 us (6%)
    all_to_all x5, blocking collectives, exchange(): return lax.all_to_all(rows, 'src', 0, 0, tiled=True)  102 us
    pallas_call x3, Pallas kernels, shards(): pl.pallas_call(lambda *refs, width=width, last=last: step_kernel(*refs, w...  24.8 us
    all_to_all x1, starting transfers between devices, exchange(): return lax.all_to_all(rows, 'src', 0, 0, tiled=True)  13.8 us
    unnamed x22, local copies, waits for them, and re-layouts  10.9 us
    all_to_all x1, waiting for transfers between devices, exchange(): return lax.all_to_all(rows, 'src', 0, 0, tiled=True)  10.7 us
    ppermute x3, starting transfers between devices, shards(): others = lax.ppermute(send, 'frm', across)  9.61 us
    ppermute x1, waiting for transfers between devices, shards(): before = lax.ppermute(chip, 'src', ahead)  6.76 us
    pallas_call x1, Pallas kernels, shards(): pl.pallas_call(first_kernel, grid=grid, in_specs=[SMEM, SMEM, whole(K, K)...  5.37 us
  transfers between devices with their start and end apart: 10, of which 9 were waited for; matrix products, arithmetic and copies ran while one was open for 1% of the time, Pallas kernels for 0%

profile of v2, /device:TPU:1, one launch (start us, length us, event | category | flops | bytes accessed | tf_op | source)
XLA Modules:
  0.0 207.6 jit_solution(2107760903555168037)
XLA Ops:
  0.6 0.0 copy-start
  0.7 0.0 copy-start.1
  0.7 2.2 %copy-done.1 = bf16[512,4096]{1,0:T(8,128)(2,1)S(1)} copy-done((bf16[512,4096]{1,0:T(8,128)(2,1)S(1)}, bf16[512,4096]{1,0:T(8,128)(2,1)}, u32[]{:S(2)}) %copy-start.1) | copy-done | bytes 4194328
  2.9 2.2 %copy-done.4 = f32[4096,4,64]{0,2,1:T(8,128)S(1)} copy-done((f32[4096,4,64]{0,2,1:T(8,128)S(1)}, f32[4096,4,64]{0,2,1:T(8,128)}, u32[]{:S(2)}) %copy-start.4) | copy-done | bytes 4194328
  5.1 0.7 copy-done.6
  5.8 0.8 copy-done.8
  6.5 0.7 copy-done.9
  7.2 5.4 %first_forward.1 = (bf16[2,256,256]{2,1,0:T(8,128)(2,1)S(1)}, bf16[2,256,256]{2,1,0:T(8,128)(2,1)S(1)}, f32[128,512]{1,0:T(8,128)S(1)}, bf16[128,512]{1,0:T(8,128)(2,1)S(1)}) custom-call(s32[4]{0:T(128)S(1)} %copy-done.9, s32[1]{0:T(128)} %bitcast.3.place_ref, f32[64,64]{1,0:T(8,128)S(1)} %copy-done.8, f32[256,4096]{1,0:T(8,128)S(1)} %bitcast.25, ...), custom_call_target="tpu_custom_call" | custom-call | tf_op jit(solution)/shard_map/first_forward/pallas_call | solution.py:308
  12.6 3.3 %collective-permute-start = (bf16[128,512]{1,0:T(8,128)(2,1)S(1)}, bf16[128,512]{1,0:T(8,128)(2,1)S(1)}, u32[]{:S(2)}, u32[]{:S(2)}) collective-permute-start(bf16[128,512]{1,0:T(8,128)(2,1)S(1)} %get-tuple-element.25), channel_id=1, source_target_pairs={{0,1},{1,0},{2,3},{3,2},{4,5},{5,4},{6,7},{7,6},{8,9},{9,8},{10,11... | collective-permute-start | bytes 393224 | tf_op jit(solution)/shard_map/ppermute | solution.py:330
  15.9 1.0 collective-permute-done.theirs_ref
  16.9 0.7 first_fold.1
  17.6 13.8 %all-to-all-start = ((bf16[128,4,128]{2,1,0:T(4,128)(2,1)}), bf16[128,4,128]{2,1,0:T(4,128)(2,1)S(1)}, u32[]{:S(2)}, u32[]{:S(2)}) async-start(bf16[128,4,128]{2,1,0:T(4,128)(2,1)} %bitcast.7), calls=%async_computation | async-start | bytes 262144 | tf_op jit(solution)/shard_map/all_to_all | solution.py:305
  31.4 0.2 dynamic-slice_reduce_fusion
  31.6 10.7 %all-to-all-done = bf16[128,4,128]{2,1,0:T(4,128)(2,1)S(1)} async-done(((bf16[128,4,128]{2,1,0:T(4,128)(2,1)}), bf16[128,4,128]{2,1,0:T(4,128)(2,1)S(1)}, u32[]{:S(2)}, u32[]{:S(2)}) %all-to-all-start) | async-done | bytes 131104 | tf_op jit(solution)/shard_map/all_to_all | solution.py:305
  42.3 0.1 first_owner.1
  42.4 17.0 %all_to_all.66 = bf16[128,4,128]{2,1,0:T(4,128)(2,1)S(1)} all-to-all(bf16[128,4,128]{2,1,0:T(4,128)(2,1)S(1)} %bitcast.38), channel_id=1, replica_groups=mesh['src'=128,'frm'=2] {'src'}, dimensions={0} | all-to-all | bytes 262144 | tf_op jit(solution)/shard_map/all_to_all | solution.py:305
  59.4 3.0 %collective-permute-start.1 = (bf16[512,128]{1,0:T(8,128)(2,1)S(1)}, bf16[512,128]{1,0:T(8,128)(2,1)S(1)}, u32[]{:S(2)}, u32[]{:S(2)}) collective-permute-start(bf16[512,128]{1,0:T(8,128)(2,1)S(1)} %bitcast.31), channel_id=1, source_target_pairs={{0,1},{1,0},{2,3},{3,2},{4,5},{5,4},{6,7},{7,6},{8,9},{9,8},{10,11... | collective-permute-start | bytes 393224 | tf_op jit(solution)/shard_map/ppermute | solution.py:354
  62.4 0.5 slice.6
  62.9 1.3 convert_reduce_fusion
  64.2 2.2 %copy-done.2 = bf16[512,4096]{1,0:T(8,128)(2,1)S(1)} copy-done((bf16[512,4096]{1,0:T(8,128)(2,1)S(1)}, bf16[512,4096]{1,0:T(8,128)(2,1)}, u32[]{:S(2)}) %copy-start.2) | copy-done | bytes 4194328
  66.4 2.2 %copy-done.5 = f32[4096,4,64]{0,2,1:T(8,128)S(1)} copy-done((f32[4096,4,64]{0,2,1:T(8,128)S(1)}, f32[4096,4,64]{0,2,1:T(8,128)}, u32[]{:S(2)}) %copy-start.5) | copy-done | bytes 4194328
  68.6 9.3 %step.3 = (f32[256,4096]{1,0:T(8,128)S(1)}, f32[8,128]{1,0:T(8,128)S(1)}, f32[384,512]{1,0:T(8,128)S(1)}, bf16[400,512]{1,0:T(8,128)(2,1)S(1)}) custom-call(s32[1]{0:T(128)} %bitcast.1.refs_0_, bf16[512,128]{1,0:T(8,128)(2,1)S(1)} %bitcast.32, bf16[512,128]{1,0:T(8,128)(2,1)S(1)} %collective-permute-done.1.refs_2_, ...), custom_call_target="tpu_custom_call" | custom-call | tf_op jit(solution)/shard_map/step/pallas_call | solution.py:363
  77.9 0.1 collective-permute-start.2
  78.0 1.7 collective-permute-done.2.refs_1_
  79.8 0.6 fold.2
  80.4 23.3 %all_to_all.67 = bf16[128,16,128]{2,1,0:T(8,128)(2,1)S(1)} all-to-all(bf16[128,16,128]{2,1,0:T(8,128)(2,1)S(1)} %bitcast.35), channel_id=1, replica_groups=mesh['src'=128,'frm'=2] {'src'}, dimensions={0} | all-to-all | bytes 1048576 | tf_op jit(solution)/shard_map/all_to_all | solution.py:305
  103.7 0.5 owner.2
  104.2 18.5 %all_to_all.68 = bf16[128,4,128]{2,1,0:T(4,128)(2,1)S(1)} all-to-all(bf16[128,4,128]{2,1,0:T(4,128)(2,1)S(1)} %bitcast.44), channel_id=1, replica_groups=mesh['src'=128,'frm'=2] {'src'}, dimensions={0} | all-to-all | bytes 262144 | tf_op jit(solution)/shard_map/all_to_all | solution.py:305
  122.7 2.9 %collective-permute-start.3 = (bf16[512,128]{1,0:T(8,128)(2,1)S(1)}, bf16[512,128]{1,0:T(8,128)(2,1)S(1)}, u32[]{:S(2)}, u32[]{:S(2)}) collective-permute-start(bf16[512,128]{1,0:T(8,128)(2,1)S(1)} %bitcast.33), channel_id=1, source_target_pairs={{0,1},{1,0},{2,3},{3,2},{4,5},{5,4},{6,7},{7,6},{8,9},{9,8},{10,11... | collective-permute-start | bytes 393224 | tf_op jit(solution)/shard_map/ppermute | solution.py:354
  125.6 1.0 collective-permute-done.3.refs_2_
  126.6 9.2 %step.4 = (f32[256,4096]{1,0:T(8,128)S(1)}, f32[8,128]{1,0:T(8,128)S(1)}, f32[384,512]{1,0:T(8,128)S(1)}, bf16[400,512]{1,0:T(8,128)(2,1)S(1)}) custom-call(s32[1]{0:T(128)} %bitcast.1.refs_0_, bf16[512,128]{1,0:T(8,128)(2,1)S(1)} %bitcast.34, bf16[512,128]{1,0:T(8,128)(2,1)S(1)} %collective-permute-done.3.refs_2_, ...), custom_call_target="tpu_custom_call" | custom-call | tf_op jit(solution)/shard_map/step/pallas_call | solution.py:363
  135.7 0.4 collective-permute-start.4
  136.2 1.4 collective-permute-done.4.refs_1_
  137.6 0.6 fold.3
  138.2 23.0 %all_to_all.69 = bf16[128,16,128]{2,1,0:T(8,128)(2,1)S(1)} all-to-all(bf16[128,16,128]{2,1,0:T(8,128)(2,1)S(1)} %bitcast.36), channel_id=1, replica_groups=mesh['src'=128,'frm'=2] {'src'}, dimensions={0} | all-to-all | bytes 1048576 | tf_op jit(solution)/shard_map/all_to_all | solution.py:305
  161.2 0.5 owner.3
  161.6 19.7 %all_to_all.70 = bf16[128,8,128]{2,1,0:T(8,128)(2,1)S(1)} all-to-all(bf16[128,8,128]{2,1,0:T(8,128)(2,1)S(1)} %bitcast.43), channel_id=1, replica_groups=mesh['src'=128,'frm'=2] {'src'}, dimensions={0} | all-to-all | bytes 524288 | tf_op jit(solution)/shard_map/all_to_all | solution.py:305
  181.4 3.7 %collective-permute-start.5 = (bf16[512,128]{1,0:T(8,128)(2,1)S(1)}, bf16[512,128]{1,0:T(8,128)(2,1)S(1)}, u32[]{:S(2)}, u32[]{:S(2)}) collective-permute-start(bf16[512,128]{1,0:T(8,128)(2,1)S(1)} %bitcast.49), channel_id=1, source_target_pairs={{0,1},{1,0},{2,3},{3,2},{4,5},{5,4},{6,7},{7,6},{8,9},{9,8},{10,11... | collective-permute-start | bytes 393224 | tf_op jit(solution)/shard_map/ppermute | solution.py:354
  185.1 1.0 collective-permute-done.5.refs_2_
  186.1 6.3 %step.5 = (f32[256,4096]{1,0:T(8,128)S(1)}, f32[8,128]{1,0:T(8,128)S(1)}) custom-call(s32[1]{0:T(128)} %bitcast.1.refs_0_, bf16[1024,128]{1,0:T(8,128)(2,1)S(1)} %bitcast.27, bf16[512,128]{1,0:T(8,128)(2,1)S(1)} %collective-permute-done.5.refs_2_, bf16[2,256,256]{2,1,0:T(8,128)(2,1)S(1)} %get-tuple-element.26.refs_3_, ...), custom_call_target="tpu_custom_call" | custom-call | tf_op jit(solution)/shard_map/step/pallas_call | solution.py:363
  192.4 0.4 collective-permute-start.6
  192.9 0.8 collective-permute-done.6
  193.7 1.3 collective-permute-start.8
  195.0 0.1 collective-permute-start.7
  195.2 0.9 residual.1
  196.0 0.1 collective-permute-done.8.refs_4_
  196.1 6.8 %collective-permute-done.7.refs_3_ = f32[8,128]{1,0:T(8,128)S(1)} collective-permute-done((f32[8,128]{1,0:T(8,128)S(1)}, f32[8,128]{1,0:T(8,128)S(1)}, u32[]{:S(2)}, u32[]{:S(2)}) %collective-permute-start.7) | collective-permute-done | bytes 4128 | tf_op jit(solution)/shard_map/ppermute | solution.py:395
  202.9 4.7 %scaled_estimate.1 = f32[256,4096]{1,0:T(8,128)} custom-call(s32[1]{0:T(128)} %bitcast.1.refs_0_, f32[256,4096]{1,0:T(8,128)S(1)} %get-tuple-element.44.refs_1_, f32[8,128]{1,0:T(8,128)S(1)} %add.7.refs_2_, f32[8,128]{1,0:T(8,128)S(1)} %collective-permute-done.7.refs_3_, f32[8,128]{1,0:T(8,128)S(1)} %collective-permute-done.8.refs_4_), custom_call_target="tpu_custom_call" | custom-call | tf_op jit(solution)/shard_map/scaled_estimate/pallas_call | solution.py:404
  (17 shorter events, 0.1 us)
Async XLA Ops:
  0.6 30.8 %copy-start = (f32[512,128]{1,0:T(8,128)S(1)}, f32[512,128]{1,0:T(8,128)}, u32[]{:S(2)}) copy-start(f32[512,128]{1,0:T(8,128)} %param.7) | copy-start | bytes 786436
  0.7 2.2 %copy-start.1 = (bf16[512,4096]{1,0:T(8,128)(2,1)S(1)}, bf16[512,4096]{1,0:T(8,128)(2,1)}, u32[]{:S(2)}) copy-start(bf16[512,4096]{1,0:T(8,128)(2,1)} %refs_8_.5) | copy-start | bytes 12582916
  2.9 2.2 %copy-start.4 = (f32[4096,4,64]{0,2,1:T(8,128)S(1)}, f32[4096,4,64]{0,2,1:T(8,128)}, u32[]{:S(2)}) copy-start(f32[4096,4,64]{0,2,1:T(8,128)} %param.10) | copy-start | bytes 12582916
  5.1 0.7 copy-start.6
  5.8 0.8 copy-start.8
  6.5 0.7 copy-start.9
  7.2 55.2 %copy-start.10 = (s32[4096]{0:T(1024)S(1)}, s32[4096]{0:T(1024)}, u32[]{:S(2)}) copy-start(s32[4096]{0:T(1024)} %param.12) | copy-start | bytes 49156
  7.2 57.0 %copy-start.7 = (f32[4096]{0:T(1024)S(1)}, f32[4096]{0:T(1024)}, u32[]{:S(2)}) copy-start(f32[4096]{0:T(1024)} %param.9) | copy-start | bytes 49156
  12.6 4.3 %collective-permute-start = (bf16[128,512]{1,0:T(8,128)(2,1)S(1)}, bf16[128,512]{1,0:T(8,128)(2,1)S(1)}, u32[]{:S(2)}, u32[]{:S(2)}) collective-permute-start(bf16[128,512]{1,0:T(8,128)(2,1)S(1)} %get-tuple-element.25), channel_id=1, source_target_pairs={{0,1},{1,0},{2,3},{3,2},{4,5},{5,4},{6,7},{7,6},{8,9},{9,8},{10,11... | collective-permute-start | bytes 393224 | tf_op jit(solution)/shard_map/ppermute | solution.py:330
  17.6 24.7 %all-to-all-start = ((bf16[128,4,128]{2,1,0:T(4,128)(2,1)}), bf16[128,4,128]{2,1,0:T(4,128)(2,1)S(1)}, u32[]{:S(2)}, u32[]{:S(2)}) async-start(bf16[128,4,128]{2,1,0:T(4,128)(2,1)} %bitcast.7), calls=%async_computation | async-start | bytes 262144 | tf_op jit(solution)/shard_map/all_to_all | solution.py:305
  59.4 4.8 %collective-permute-start.1 = (bf16[512,128]{1,0:T(8,128)(2,1)S(1)}, bf16[512,128]{1,0:T(8,128)(2,1)S(1)}, u32[]{:S(2)}, u32[]{:S(2)}) collective-permute-start(bf16[512,128]{1,0:T(8,128)(2,1)S(1)} %bitcast.31), channel_id=1, source_target_pairs={{0,1},{1,0},{2,3},{3,2},{4,5},{5,4},{6,7},{7,6},{8,9},{9,8},{10,11... | collective-permute-start | bytes 393224 | tf_op jit(solution)/shard_map/ppermute | solution.py:354
  64.2 2.2 %copy-start.2 = (bf16[512,4096]{1,0:T(8,128)(2,1)S(1)}, bf16[512,4096]{1,0:T(8,128)(2,1)}, u32[]{:S(2)}) copy-start(bf16[512,4096]{1,0:T(8,128)(2,1)} %refs_8_.5) | copy-start | bytes 12582916
  66.4 2.2 %copy-start.5 = (f32[4096,4,64]{0,2,1:T(8,128)S(1)}, f32[4096,4,64]{0,2,1:T(8,128)}, u32[]{:S(2)}) copy-start(f32[4096,4,64]{0,2,1:T(8,128)} %param.10) | copy-start | bytes 12582916
  68.6 58.0 %copy-start.3 = (bf16[512,4096]{1,0:T(8,128)(2,1)S(1)}, bf16[512,4096]{1,0:T(8,128)(2,1)}, u32[]{:S(2)}) copy-start(bf16[512,4096]{1,0:T(8,128)(2,1)} %refs_8_.5) | copy-start | bytes 12582916
  77.9 1.8 collective-permute-start.2
  122.7 3.9 %collective-permute-start.3 = (bf16[512,128]{1,0:T(8,128)(2,1)S(1)}, bf16[512,128]{1,0:T(8,128)(2,1)S(1)}, u32[]{:S(2)}, u32[]{:S(2)}) collective-permute-start(bf16[512,128]{1,0:T(8,128)(2,1)S(1)} %bitcast.33), channel_id=1, source_target_pairs={{0,1},{1,0},{2,3},{3,2},{4,5},{5,4},{6,7},{7,6},{8,9},{9,8},{10,11... | collective-permute-start | bytes 393224 | tf_op jit(solution)/shard_map/ppermute | solution.py:354
  135.7 1.8 collective-permute-start.4
  181.4 4.7 %collective-permute-start.5 = (bf16[512,128]{1,0:T(8,128)(2,1)S(1)}, bf16[512,128]{1,0:T(8,128)(2,1)S(1)}, u32[]{:S(2)}, u32[]{:S(2)}) collective-permute-start(bf16[512,128]{1,0:T(8,128)(2,1)S(1)} %bitcast.49), channel_id=1, source_target_pairs={{0,1},{1,0},{2,3},{3,2},{4,5},{5,4},{6,7},{7,6},{8,9},{9,8},{10,11... | collective-permute-start | bytes 393224 | tf_op jit(solution)/shard_map/ppermute | solution.py:354
  192.4 1.2 collective-permute-start.6
  193.7 2.5 %collective-permute-start.8 = (f32[8,128]{1,0:T(8,128)S(1)}, f32[8,128]{1,0:T(8,128)S(1)}, u32[]{:S(2)}, u32[]{:S(2)}) collective-permute-start(f32[8,128]{1,0:T(8,128)S(1)} %add.7.refs_2_), channel_id=1, source_target_pairs={{2,0},{4,2},{6,4},{8,6},{10,8},{12,10},{14,12},{16,14},{18,16},{20... | collective-permute-start | bytes 12296 | tf_op jit(solution)/shard_map/ppermute | solution.py:396
  195.0 7.9 %collective-permute-start.7 = (f32[8,128]{1,0:T(8,128)S(1)}, f32[8,128]{1,0:T(8,128)S(1)}, u32[]{:S(2)}, u32[]{:S(2)}) collective-permute-start(f32[8,128]{1,0:T(8,128)S(1)} %add.7.refs_2_), channel_id=1, source_target_pairs={{0,2},{2,4},{4,6},{6,8},{8,10},{10,12},{12,14},{14,16},{16,18},{18... | collective-permute-start | bytes 12296 | tf_op jit(solution)/shard_map/ppermute | solution.py:395

commit v3 on v2

v3 whole, which is shorter than its diff:
```python
import math

import jax
import jax.numpy as jnp
import numpy as np
from jax import lax
from jax.experimental import pallas as pl
from jax.experimental.pallas import tpu as pltpu
from jax.sharding import PartitionSpec as P

K = 64
GROUP = 2048
ITERS = 3
LANES = 128
BLOCK = 512
SPLIT = False

step_size = 0.5
shrink_one = 0.05
group_weight = 0.03
epsilon = 1e-06

F32 = jnp.float32
BF16 = jnp.bfloat16
HIGHEST = lax.Precision.HIGHEST
PARAMS = pltpu.CompilerParams(vmem_limit_bytes=16 * 1024 * 1024)


def windowed_cosines():
    t = np.arange(K)[:, None] + 0.5
    k = np.arange(K)[None, :] + 0.5
    return (np.sin(np.pi * t / K) * np.sqrt(2.0 / K) * np.cos(np.pi * k * t / K)).astype(np.float32)


def split(x):
    high = x.astype(BF16)
    return high, (x - high.astype(F32)).astype(BF16)


def dot(a, b):
    return jnp.dot(a, b, preferred_element_type=F32)


def dot_t(a, b):
    return lax.dot_general(a, b, (((1,), (1,)), ((), ())), preferred_element_type=F32)


def to_samples(atoms_ref, sums):
    high, low = split(sums)
    return dot(atoms_ref[0], high) + dot(atoms_ref[0], low) + dot(atoms_ref[1], high)


def group_scale(power, tau):
    return jnp.maximum(0.0, 1.0 - tau / jnp.sqrt(power + epsilon))


def first_kernel(
    where_ref, offsets_hbm, wave_hbm, group_hbm, depth_hbm, measured_hbm, coef_hbm, lead_hbm,
    table_ref, table_t_ref, mine_ref, theirs_ref, marks_ref, rows_ref, depth_ref, coef_ref, lead_ref,
    offsets_ref, wave_ref, group_ref, measured_ref, acc_ref, coef_sem, lead_sem, small_sem,
):
    total = table_ref.shape[2]
    own = mine_ref.shape[0]
    sources = lead_ref.shape[1]
    blocks = lead_sem.shape[0]
    block = sources // blocks
    pairs = (
        (offsets_hbm, offsets_ref), (wave_hbm, wave_ref), (group_hbm, group_ref), (measured_hbm, measured_ref),
        (depth_hbm, depth_ref),
    )
    small = [pltpu.make_async_copy(a, b, small_sem.at[n]) for n, (a, b) in enumerate(pairs)]
    for load in small:
        load.start()
    loads = []
    for j in range(blocks):
        cols = slice(j * block, (j + 1) * block)
        loads.append(
            (
                pltpu.make_async_copy(lead_hbm.at[:, cols], lead_ref.at[:, cols], lead_sem.at[j]),
                pltpu.make_async_copy(coef_hbm.at[:, cols], coef_ref.at[:, cols], coef_sem.at[j]),
            )
        )
        for load in loads[-1]:
            load.start()
    for load in small:
        load.wait()

    groups = group_ref[...]
    marks_ref[0] = jnp.sum((groups == groups[0:1, 0:1]).astype(jnp.int32))
    marks_ref[1] = where_ref[1]
    for t in range(rows_ref.shape[0]):
        rows_ref[t] = measured_ref[t * LANES : (t + 1) * LANES, :].T
    wave = wave_ref[...]
    order = lax.broadcasted_iota(jnp.int32, (total, K), 0)
    sample = (order + where_ref[0]) % total
    position = lax.broadcasted_iota(jnp.int32, (total, K), 1)
    for f in range(offsets_ref.shape[0]):
        delay = (sample - offsets_ref[f] + total) % total
        placing = (delay == position).astype(F32)
        part_t = jnp.dot(placing, wave, precision=HIGHEST, preferred_element_type=F32)
        rows = slice(f * K, (f + 1) * K)
        table_t_ref[0, :, rows], table_t_ref[1, :, rows] = split(part_t)
        table_ref[0, rows, :], table_ref[1, rows, :] = split(part_t.T)

    for j in range(blocks):
        for load in loads[j]:
            load.wait()
        cols = slice(j * block, (j + 1) * block)
        part = dot_t((coef_ref[:, cols] * depth_ref[:, cols]).astype(BF16), lead_ref[:, cols])
        if j == 0:
            acc_ref[...] = part
        else:
            acc_ref[...] += part
    samples = to_samples(table_t_ref, acc_ref[...])
    mine_ref[...] = samples[:own]
    theirs_ref[...] = samples[own:].astype(BF16)


def step_kernel(
    marks_ref, own_ref, other_ref, table_ref, table_t_ref, depth_ref, state_ref, lead_ref,
    *rest, width, predict, first, block,
):
    if not first:
        scale_ref, *rest = rest
    new_ref, power_ref, *rest = rest
    if predict:
        mine_ref, theirs_ref, rows_ref, samples_ref, turned_ref, weighted_ref = rest
    else:
        rows_ref, samples_ref, turned_ref = rest
    coefs, sources = state_ref.shape
    tiles = lead_ref.shape[0] // LANES
    own = table_ref.shape[2] // 2

    for h, ref in enumerate((own_ref, other_ref)):
        rows_ref[h] = ref[...].astype(F32)
        for t in range(tiles):
            lanes = slice(t * LANES, (t + 1) * LANES)
            part = rows_ref[h, pl.ds(t, own, stride=width), :]
            samples_ref[h * own : (h + 1) * own, lanes] = part.astype(BF16)
    turned = dot(table_ref[0], samples_ref[...]) + dot(table_ref[1], samples_ref[...])
    if SPLIT:
        turned_ref[:coefs], turned_ref[coefs:] = split(turned)
    else:
        turned_ref[...] = turned.astype(BF16)

    start = marks_ref[0]
    bounds = (start, start + GROUP)
    scales = None if first else [scale_ref[g : g + 1, 0:1] for g in range(3)]
    sums = [jnp.zeros((1, block), F32) for _ in range(4)]
    for j in range(sources // block):
        cols = slice(j * block, (j + 1) * block)
        half = j * block // GROUP
        gradient = dot(turned_ref[...], lead_ref[:, cols])
        if SPLIT:
            gradient = gradient[:coefs] + gradient[coefs:]
        source = j * block + lax.broadcasted_iota(jnp.int32, (1, block), 1)
        before = source < bounds[half]
        depth = depth_ref[:, cols]
        state = state_ref[:, cols]
        if not first:
            state = state * jnp.where(before, scales[half], scales[half + 1])
        moved = state + (step_size * depth) * gradient
        shrunk = moved - jnp.clip(moved, -shrink_one, shrink_one)
        new_ref[:, cols] = shrunk
        if predict:
            weighted = (shrunk * depth).astype(BF16)
            inner = slice(j * block - half * GROUP, (j + 1) * block - half * GROUP)
            none = jnp.zeros((), BF16)
            weighted_ref[half, :coefs, inner] = jnp.where(before, weighted, none)
            weighted_ref[half, coefs:, inner] = jnp.where(before, none, weighted)
        squares = jnp.sum(shrunk * shrunk, axis=0, keepdims=True)
        sums[2 * half] += jnp.where(before, squares, 0.0)
        sums[2 * half + 1] += jnp.where(before, 0.0, squares)
    power_ref[...] = jnp.zeros_like(power_ref)
    for g, total in enumerate((sums[0], sums[1] + sums[2], sums[3])):
        power_ref[g : g + 1, :] = jnp.broadcast_to(jnp.sum(total, axis=1, keepdims=True), (1, LANES))

    if predict:
        halves = [dot_t(weighted_ref[h], lead_ref[:, h * GROUP : (h + 1) * GROUP]) for h in range(2)]
        parts = (halves[0][:coefs], halves[0][coefs:] + halves[1][:coefs], halves[1][coefs:])
        for g in range(3):
            samples = to_samples(table_t_ref, parts[g])
            mine_ref[g * own : (g + 1) * own, :] = samples[:own]
            theirs_ref[g * own : (g + 1) * own, :] = samples[own:].astype(BF16)
        high, low = split(power_ref[...])
        for t in range(tiles):
            lanes = slice(t * LANES, (t + 1) * LANES)
            theirs_ref[3 * own : 3 * own + 16, lanes] = jnp.concatenate([high, low], axis=0)


def first_fold_kernel(mine_ref, theirs_ref, out_ref, rows_ref):
    own = mine_ref.shape[0]
    tiles = mine_ref.shape[1] // LANES
    for t in range(tiles):
        lanes = slice(t * LANES, (t + 1) * LANES)
        rows_ref[pl.ds(t, own, stride=tiles), :] = mine_ref[:, lanes] + theirs_ref[:, lanes].astype(F32)
    out_ref[...] = rows_ref[...].astype(BF16)


def fold_kernel(mine_ref, theirs_ref, power_ref, out_ref, chip_ref, rows_ref, *, tau):
    own = mine_ref.shape[0] // 3
    tiles = mine_ref.shape[1] // LANES
    theirs = theirs_ref[3 * own : 3 * own + 16, :LANES].astype(F32)
    chip = power_ref[...] + theirs[:8] + theirs[8:]
    chip_ref[...] = chip
    middle = group_scale(chip[1:2, :], tau)
    for g, part in enumerate((1, 0, 2)):
        for t in range(tiles):
            lanes = slice(t * LANES, (t + 1) * LANES)
            rows = slice(part * own, (part + 1) * own)
            total = mine_ref[rows, lanes] + theirs_ref[rows, lanes].astype(F32)
            if part == 1:
                total = total * middle
            rows_ref[pl.ds(g * tiles + t, own, stride=16), :] = total
    for g, part in enumerate((0, 2)):
        value = chip[part : part + 1, :]
        high = value.astype(BF16).astype(F32)
        for n, term in enumerate((high, value - high)):
            at = 3 * tiles + 2 * g + n
            rows_ref[pl.ds(at, own, stride=16), :] = jnp.broadcast_to(term, (own, LANES))
    out_ref[...] = rows_ref[...].astype(BF16)


def send_residual(row, out_ref, rows_ref, tiles, last):
    own = out_ref.shape[0] // (2 * tiles if last else tiles)
    if last:
        high = row.astype(BF16).astype(F32)
        row = jnp.concatenate([high, row - high], axis=0)
    out_ref[...] = jnp.concatenate([row.astype(BF16)] * own, axis=0)


def first_owner_kernel(marks_ref, got_ref, measured_ref, out_ref, rows_ref):
    me = marks_ref[1]
    tiles = measured_ref.shape[0]
    senders = got_ref.shape[0] // tiles
    rows_ref[...] = got_ref[...].astype(F32)
    row = [
        measured_ref[t, pl.ds(me, 1), :]
        - jnp.sum(rows_ref[pl.ds(t, senders, stride=tiles), :], axis=0, keepdims=True)
        for t in range(tiles)
    ]
    send_residual(jnp.concatenate(row, axis=0), out_ref, rows_ref, tiles, False)


def owner_kernel(marks_ref, got_ref, measured_ref, chip_ref, out_ref, scale_ref, rows_ref, edges_ref, *, tau, last):
    me = marks_ref[1]
    tiles = measured_ref.shape[0]
    senders = got_ref.shape[0] // 16
    rows_ref[...] = got_ref[...].astype(F32)

    def of(k):
        return rows_ref[pl.ds(k, senders, stride=16), :]

    front = of(3 * tiles) + of(3 * tiles + 1)
    back = of(3 * tiles + 2) + of(3 * tiles + 3)
    before = jnp.concatenate([back[senders - 1 :], back[: senders - 1]], axis=0)
    front_scale = group_scale(front + before, tau)
    back_scale = jnp.concatenate([front_scale[1:], front_scale[:1]], axis=0)
    row = []
    for t in range(tiles):
        parts = of(t) + front_scale * of(tiles + t) + back_scale * of(2 * tiles + t)
        row.append(measured_ref[t, pl.ds(me, 1), :] - jnp.sum(parts, axis=0, keepdims=True))
    send_residual(jnp.concatenate(row, axis=0), out_ref, rows_ref, tiles, last)
    edges_ref[0] = front_scale
    edges_ref[1] = back_scale
    scale_ref[...] = jnp.zeros_like(scale_ref)
    scale_ref[0:1, :] = edges_ref[0, pl.ds(me, 1), :]
    scale_ref[1:2, :] = group_scale(chip_ref[1:2, :], tau)
    scale_ref[2:3, :] = edges_ref[1, pl.ds(me, 1), :]


def add_kernel(a_ref, b_ref, out_ref):
    out_ref[...] = a_ref[...] + b_ref[...]


def residual_kernel(own_ref, out_ref, rows_ref):
    own = out_ref.shape[1]
    tiles = out_ref.shape[0] // LANES
    rows_ref[...] = own_ref[...].astype(F32)
    for t in range(tiles):
        high = rows_ref[pl.ds(t, own, stride=2 * tiles), :]
        low = rows_ref[pl.ds(tiles + t, own, stride=2 * tiles), :]
        out_ref[t * LANES : (t + 1) * LANES, :] = (high + low).T


def last_kernel(marks_ref, state_ref, chip_ref, before_ref, after_ref, out_hbm, scaled_ref, sem, *, tau):
    blocks, _, block = scaled_ref.shape
    first = group_scale(chip_ref[0:1, 0:1] + before_ref[2:3, 0:1], tau)
    middle = group_scale(chip_ref[1:2, 0:1], tau)
    last = group_scale(chip_ref[2:3, 0:1] + after_ref[0:1, 0:1], tau)
    start = marks_ref[0]
    stores = []
    for j in range(blocks):
        cols = slice(j * block, (j + 1) * block)
        source = j * block + lax.broadcasted_iota(jnp.int32, (1, block), 1)
        scale = jnp.where(source < start, first, jnp.where(source < start + GROUP, middle, last))
        scaled_ref[j] = state_ref[:, cols] * scale
        stores.append(pltpu.make_async_copy(scaled_ref.at[j], out_hbm.at[:, cols], sem.at[j]))
        stores[-1].start()
    for store in stores:
        store.wait()


SMEM = pl.BlockSpec(memory_space=pltpu.SMEM)
VMEM = pl.BlockSpec(memory_space=pltpu.VMEM)
HBM = pl.BlockSpec(memory_space=pltpu.HBM)


def struct(dtype, *shape):
    return jax.ShapeDtypeStruct(shape, dtype)


def call(kernel, name, ins, outs, out_specs=None, scratch=()):
    return pl.pallas_call(
        kernel, in_specs=ins, out_specs=out_specs or [VMEM] * len(outs), out_shape=outs,
        scratch_shapes=list(scratch), compiler_params=PARAMS, name=name,
    )


def stay(x):
    return pltpu.with_memory_space_constraint(x, pltpu.HBM)


def first_call(where, offsets, groups, depth, measured, state, lead):
    coefs, sources = state.shape
    sensors, own = measured.shape
    total = 2 * own
    dma = pltpu.SemaphoreType.DMA((sources // BLOCK,))
    inputs = (offsets, jnp.asarray(windowed_cosines()), groups, depth, measured, state, lead)
    return call(
        first_kernel,
        "first_forward",
        [SMEM] + [HBM] * len(inputs),
        [
            struct(BF16, 2, coefs, total),
            struct(BF16, 2, total, coefs),
            struct(F32, own, sensors),
            struct(BF16, own, sensors),
            struct(jnp.int32, 2),
            struct(F32, sensors // LANES, own, LANES),
            struct(F32, 1, sources),
            struct(F32, coefs, sources),
            struct(BF16, sensors, sources),
        ],
        [VMEM, VMEM, VMEM, VMEM, SMEM, VMEM, VMEM, VMEM, VMEM],
        [
            pltpu.SMEM(offsets.shape, jnp.int32),
            pltpu.VMEM((K, K), F32),
            pltpu.VMEM((1, sources), jnp.int32),
            pltpu.VMEM((sensors, own), F32),
            pltpu.VMEM((coefs, sensors), F32),
            dma,
            dma,
            pltpu.SemaphoreType.DMA((5,)),
        ],
    )(where, *(stay(x) for x in inputs))


def step_call(marks, mine, others, table, table_t, scale, depth, state, lead, *, first, last):
    coefs, sources = state.shape
    sensors = lead.shape[0]
    own = table.shape[2] // 2
    tiles = sensors // LANES
    width = mine.shape[0] // own
    outs = [struct(F32, coefs, sources), struct(F32, 8, LANES)]
    scratch = [
        pltpu.VMEM((2, own * width, LANES), F32),
        pltpu.VMEM((2 * own, sensors), BF16),
        pltpu.VMEM(((2 if SPLIT else 1) * coefs, sensors), BF16),
    ]
    if not last:
        outs += [struct(F32, 3 * own, sensors), struct(BF16, 3 * own + 16, sensors)]
        scratch += [pltpu.VMEM((2, 2 * coefs, GROUP), BF16)]

    def kernel(*refs):
        step_kernel(*refs, width=width, predict=not last, first=first, block=BLOCK)

    ins = [marks, mine, others, table, table_t, depth, state, lead] + ([] if first else [scale])
    return call(kernel, "step", [SMEM] + [VMEM] * (len(ins) - 1), outs, None, scratch)(*ins)


def last_call(marks, state, chip, before, after, tau):
    coefs, sources = state.shape
    blocks = sources // BLOCK
    return call(
        lambda *refs: last_kernel(*refs, tau=tau),
        "scaled_estimate",
        [SMEM] + [VMEM] * 4,
        [struct(F32, coefs, sources)],
        [HBM],
        [pltpu.VMEM((blocks, coefs, BLOCK), F32), pltpu.SemaphoreType.DMA((blocks,))],
    )(marks, state, chip, before, after)[0]


def shards(measured, lead_field, depth, coefficients, offsets, group_ids):
    sensors, own = measured.shape
    sources = lead_field.shape[1]
    frames = coefficients.shape[1]
    src_count, frm_count = lax.axis_size("src"), lax.axis_size("frm")
    coefs = frames * K
    tau = group_weight * math.sqrt(GROUP * frames * frm_count * K)
    tiles = sensors // LANES
    across = [(i, (i + 1) % frm_count) for i in range(frm_count)]
    ahead = [(i, (i + 1) % src_count) for i in range(src_count)]
    behind = [((i + 1) % src_count, i) for i in range(src_count)]

    where = jnp.stack([lax.axis_index("frm") * own, lax.axis_index("src")])

    def exchange(rows):
        return lax.all_to_all(rows, "src", 0, 0, tiled=True)

    state = coefficients.transpose(1, 2, 0).reshape(coefs, sources)
    table, table_t, mine, theirs, marks, rows, depth_row, state, lead = first_call(
        where, offsets, group_ids.reshape(1, sources), depth.reshape(1, sources), measured, state, lead_field
    )
    folded = call(
        first_fold_kernel,
        "first_fold",
        [VMEM, VMEM],
        [struct(BF16, own * tiles, LANES)],
        None,
        [pltpu.VMEM((own * tiles, LANES), F32)],
    )(mine, lax.ppermute(theirs, "frm", across))[0]
    scale = None
    for iteration in range(ITERS):
        first, last = iteration == 0, iteration == ITERS - 1
        got = exchange(folded)
        width = 2 * tiles if last else tiles
        if first:
            row = call(
                first_owner_kernel,
                "first_owner",
                [SMEM, VMEM, VMEM],
                [struct(BF16, own * width, LANES)],
                None,
                [pltpu.VMEM((src_count * tiles, LANES), F32)],
            )(marks, got, rows)[0]
        else:
            row, scale = call(
                lambda *refs, last=last: owner_kernel(*refs, tau=tau, last=last),
                "owner",
                [SMEM, VMEM, VMEM, VMEM],
                [struct(BF16, own * width, LANES), struct(F32, 8, LANES)],
                None,
                [pltpu.VMEM((src_count * 16, LANES), F32), pltpu.VMEM((2, src_count, LANES), F32)],
            )(marks, got, rows, chip)
        mine = exchange(row)
        others = lax.ppermute(mine, "frm", across)
        results = step_call(
            marks, mine, others, table, table_t, scale, depth_row, state, lead, first=first, last=last
        )
        state, power = results[:2]
        if last:
            break
        folded, chip = call(
            lambda *refs: fold_kernel(*refs, tau=tau),
            "fold",
            [VMEM, VMEM, VMEM],
            [struct(BF16, own * 16, LANES), struct(F32, 8, LANES)],
            None,
            [pltpu.VMEM((own * 16, LANES), F32)],
        )(results[2], lax.ppermute(results[3], "frm", across), power)

    chip = call(add_kernel, "chip_power", [VMEM, VMEM], [struct(F32, 8, LANES)])(
        power, lax.ppermute(power, "frm", across)
    )[0]
    before = lax.ppermute(chip, "src", ahead)
    after = lax.ppermute(chip, "src", behind)
    residual = call(
        residual_kernel,
        "residual",
        [VMEM],
        [struct(F32, sensors, own)],
        None,
        [pltpu.VMEM((own * 2 * tiles, LANES), F32)],
    )(mine)[0]
    estimate = last_call(marks, state, chip, before, after, tau)
    return (estimate.reshape(frames, K, sources).transpose(2, 0, 1), residual)


def solution(mesh):
    return jax.shard_map(
        shards,
        mesh=mesh,
        in_specs=(
            P(None, "frm"),
            P(None, "src"),
            P("src"),
            P("src", "frm", None),
            P("frm"),
            P("src"),
        ),
        out_specs=(P("src", "frm", None), P(None, "frm")),
        check_vma=False,
    )
```

time: 208 us -> 186 us (0.89)
  blocking collectives: 102 us -> 126 us
  starting transfers between devices: 29.1 us -> 15.9 us
  local copies, waits for them, and re-layouts: 11.7 us -> 0 us
  Pallas kernels: 38.6 us -> 28.4 us
  waiting for transfers between devices: 24.5 us -> 14.6 us
    all_to_all x5 -> x6, blocking collectives: 102 us -> 126 us  [exchange(): return lax.all_to_all(rows, 'src', 0, 0, tiled=True)]
    all_to_all x1 -> x0, starting transfers between devices: 13.8 us -> none  [exchange(): return lax.all_to_all(rows, 'src', 0, 0, tiled=True)]
    unnamed x22 -> x0, local copies, waits for them, and re-layouts: 10.9 us -> none
    all_to_all x1 -> x0, waiting for transfers between devices: 10.7 us -> none  [exchange(): return lax.all_to_all(rows, 'src', 0, 0, tiled=True)]
    pallas_call x7 -> x8, Pallas kernels: 35.8 us -> 25.2 us  [the longest x3 13.8 us: step_call(): call(kernel, 'step', [SMEM] + [VMEM] * (len(ins) - 1), outs, None, scratch)]
  transfers between devices with their start and end apart: 10 -> 9, of which waited for: 9 -> 9; matrix products, arithmetic and copies ran while one was open for 1% -> 0% of each run, Pallas kernels for 0% -> 0%
where the time goes in v3:
time: 186 us
  blocking collectives  126 us (68%)
  Pallas kernels  28.4 us (15%)
  starting transfers between devices  15.9 us (9%)
  waiting for transfers between devices  14.6 us (8%)
    all_to_all x6, blocking collectives, exchange(): return lax.all_to_all(rows, 'src', 0, 0, tiled=True)  126 us
    pallas_call x3, Pallas kernels, step_call(): call(kernel, 'step', [SMEM] + [VMEM] * (len(ins) - 1), outs, None, scratch)  13.8 us
    ppermute x3, starting transfers between devices, shards(): others = lax.ppermute(mine, 'frm', across)  9.56 us
    pallas_call x1, Pallas kernels, first_call(): call(first_kernel, 'first_forward', [SMEM] + [HBM] * len(inputs), [struct...  7.11 us
    ppermute x1, waiting for transfers between devices, shards(): before = lax.ppermute(chip, 'src', ahead)  6.76 us
  transfers between devices with their start and end apart: 9, of which 9 were waited for; matrix products, arithmetic and copies ran while one was open for 0% of the time, Pallas kernels for 0%

profile of v3, /device:TPU:1, one launch (start us, length us, event | category | flops | bytes accessed | tf_op | source)
XLA Modules:
  0.0 185.8 jit_solution(11093013227264175239)
XLA Ops:
  0.6 0.1 pad_add_fusion.where_ref
  0.7 7.1 %first_forward.1 = (bf16[2,256,256]{2,1,0:T(8,128)(2,1)S(1)}, bf16[2,256,256]{2,1,0:T(8,128)(2,1)S(1)}, f32[128,512]{1,0:T(8,128)S(1)}, bf16[128,512]{1,0:T(8,12...) custom-call(s32[2]{0:T(128)S(1)} %pad_add_fusion.where_ref, ...), custom_call_target="tpu_custom_call" | custom-call | tf_op jit(solution)/shard_map/first_forward/pallas_call | solution.py:330
  7.8 3.3 %collective-permute-start = (bf16[128,512]{1,0:T(8,128)(2,1)S(1)}, bf16[128,512]{1,0:T(8,128)(2,1)S(1)}, u32[]{:S(2)}, u32[]{:S(2)}) collective-permute-start(bf16[128,512]{1,0:T(8,128)(2,1)S(1)} %get-tuple-element.31), channel_id=1, source_target_pairs={{0,1},{1,0},{2,3},{3,2},{4,5},{5,4},{6,7},{7,6},{8,9},{9,8},{10,11... | collective-permute-start | bytes 393224 | tf_op jit(solution)/shard_map/ppermute | solution.py:423
  11.2 1.0 collective-permute-done.theirs_ref
  12.2 24.6 %all_to_all.66 = bf16[128,4,128]{2,1,0:T(4,128)(2,1)S(1)} all-to-all(bf16[128,4,128]{2,1,0:T(4,128)(2,1)S(1)} %bitcast.35), channel_id=1, replica_groups=mesh['src'=128,'frm'=2] {'src'}, dimensions={0} | all-to-all | bytes 262144 | tf_op jit(solution)/shard_map/all_to_all | solution.py:410
  36.8 0.6 first_owner.1
  37.4 17.0 %all_to_all.67 = bf16[128,4,128]{2,1,0:T(4,128)(2,1)S(1)} all-to-all(bf16[128,4,128]{2,1,0:T(4,128)(2,1)S(1)} %bitcast.32), channel_id=1, replica_groups=mesh['src'=128,'frm'=2] {'src'}, dimensions={0} | all-to-all | bytes 262144 | tf_op jit(solution)/shard_map/all_to_all | solution.py:410
  54.4 3.0 %collective-permute-start.1 = (bf16[512,128]{1,0:T(8,128)(2,1)S(1)}, bf16[512,128]{1,0:T(8,128)(2,1)S(1)}, u32[]{:S(2)}, u32[]{:S(2)}) collective-permute-start(bf16[512,128]{1,0:T(8,128)(2,1)S(1)} %bitcast.29), channel_id=1, source_target_pairs={{0,1},{1,0},{2,3},{3,2},{4,5},{5,4},{6,7},{7,6},{8,9},{9,8},{10,11... | collective-permute-start | bytes 393224 | tf_op jit(solution)/shard_map/ppermute | solution.py:448
  57.3 1.0 collective-permute-done.1.refs_2_
  58.3 5.6 %step.3 = (f32[256,4096]{1,0:T(8,128)S(1)}, f32[8,128]{1,0:T(8,128)S(1)}, f32[384,512]{1,0:T(8,128)S(1)}, bf16[400,512]{1,0:T(8,128)(2,1)S(1)}) custom-call(s32[2]{0:T(128)S(1)} %get-tuple-element.29.marks_ref.refs_0_, bf16[512,128]{1,0:T(8,128)(2,1)S(1)} %bitcast.30, bf16[512,128]{1,0:T(8,128)(2,1)S(1)} %collective-permute-done.1.refs_2_, ...), custom_call_target="tpu_custom_call" | custom-call | tf_op jit(solution)/shard_map/step/pallas_call | solution.py:379
  63.9 0.6 collective-permute-start.2
  64.5 1.4 collective-permute-done.2.refs_1_
  65.9 0.6 fold.2
  66.5 23.0 %all_to_all.68 = bf16[128,16,128]{2,1,0:T(8,128)(2,1)S(1)} all-to-all(bf16[128,16,128]{2,1,0:T(8,128)(2,1)S(1)} %bitcast.33), channel_id=1, replica_groups=mesh['src'=128,'frm'=2] {'src'}, dimensions={0} | all-to-all | bytes 1048576 | tf_op jit(solution)/shard_map/all_to_all | solution.py:410
  89.5 1.0 owner.2
  90.5 18.8 %all_to_all.69 = bf16[128,4,128]{2,1,0:T(4,128)(2,1)S(1)} all-to-all(bf16[128,4,128]{2,1,0:T(4,128)(2,1)S(1)} %bitcast.37), channel_id=1, replica_groups=mesh['src'=128,'frm'=2] {'src'}, dimensions={0} | all-to-all | bytes 262144 | tf_op jit(solution)/shard_map/all_to_all | solution.py:410
  109.3 3.0 %collective-permute-start.3 = (bf16[512,128]{1,0:T(8,128)(2,1)S(1)}, bf16[512,128]{1,0:T(8,128)(2,1)S(1)}, u32[]{:S(2)}, u32[]{:S(2)}) collective-permute-start(bf16[512,128]{1,0:T(8,128)(2,1)S(1)} %bitcast.27), channel_id=1, source_target_pairs={{0,1},{1,0},{2,3},{3,2},{4,5},{5,4},{6,7},{7,6},{8,9},{9,8},{10,11... | collective-permute-start | bytes 393224 | tf_op jit(solution)/shard_map/ppermute | solution.py:448
  112.3 1.0 collective-permute-done.3.refs_2_
  113.2 5.6 %step.4 = (f32[256,4096]{1,0:T(8,128)S(1)}, f32[8,128]{1,0:T(8,128)S(1)}, f32[384,512]{1,0:T(8,128)S(1)}, bf16[400,512]{1,0:T(8,128)(2,1)S(1)}) custom-call(s32[2]{0:T(128)S(1)} %get-tuple-element.29.marks_ref.refs_0_, bf16[512,128]{1,0:T(8,128)(2,1)S(1)} %bitcast.28, bf16[512,128]{1,0:T(8,128)(2,1)S(1)} %collective-permute-done.3.refs_2_, ...), custom_call_target="tpu_custom_call" | custom-call | tf_op jit(solution)/shard_map/step/pallas_call | solution.py:379
  118.9 0.4 collective-permute-start.4
  119.3 1.4 collective-permute-done.4.refs_1_
  120.7 0.6 fold.3
  121.3 22.9 %all_to_all.70 = bf16[128,16,128]{2,1,0:T(8,128)(2,1)S(1)} all-to-all(bf16[128,16,128]{2,1,0:T(8,128)(2,1)S(1)} %bitcast.34), channel_id=1, replica_groups=mesh['src'=128,'frm'=2] {'src'}, dimensions={0} | all-to-all | bytes 1048576 | tf_op jit(solution)/shard_map/all_to_all | solution.py:410
  144.2 1.0 owner.3
  145.3 19.8 %all_to_all.71 = bf16[128,8,128]{2,1,0:T(8,128)(2,1)S(1)} all-to-all(bf16[128,8,128]{2,1,0:T(8,128)(2,1)S(1)} %bitcast.36), channel_id=1, replica_groups=mesh['src'=128,'frm'=2] {'src'}, dimensions={0} | all-to-all | bytes 524288 | tf_op jit(solution)/shard_map/all_to_all | solution.py:410
  165.0 3.6 %collective-permute-start.5 = (bf16[1024,128]{1,0:T(8,128)(2,1)S(1)}, bf16[1024,128]{1,0:T(8,128)(2,1)S(1)}, u32[]{:S(2)}, u32[]{:S(2)}) collective-permute-start(bf16[1024,128]{1,0:T(8,128)(2,1)S(1)} %bitcast.22), channel_id=1, source_target_pairs={{0,1},{1,0},{2,3},{3,2},{4,5},{5,4},{6,7},{7,6},{8,9},{9,8},{10,11... | collective-permute-start | bytes 786440 | tf_op jit(solution)/shard_map/ppermute | solution.py:448
  168.7 1.2 collective-permute-done.5.refs_2_
  169.8 2.6 %step.5 = (f32[256,4096]{1,0:T(8,128)S(1)}, f32[8,128]{1,0:T(8,128)S(1)}) custom-call(s32[2]{0:T(128)S(1)} %get-tuple-element.29.marks_ref.refs_0_, bf16[1024,128]{1,0:T(8,128)(2,1)S(1)} %bitcast.23, bf16[1024,128]{1,0:T(8,128)(2,1)S(1)} %collective-permute-done.5.refs_2_, bf16[2,256,256]{2,1,0:T(8,128)(2,1)S(1)} %get-tuple-element.33.refs_3_, ...), custom_call_target="tpu_custom_call" | custom-call | tf_op jit(solution)/shard_map/step/pallas_call | solution.py:379
  172.5 0.4 collective-permute-start.6
  172.9 0.8 collective-permute-done.6.b_ref
  173.7 1.3 collective-permute-start.8
  175.0 0.1 collective-permute-start.7
  175.2 0.9 residual.1
  176.0 0.1 collective-permute-done.8.refs_4_
  176.1 6.8 %collective-permute-done.7.refs_3_ = f32[8,128]{1,0:T(8,128)S(1)} collective-permute-done((f32[8,128]{1,0:T(8,128)S(1)}, f32[8,128]{1,0:T(8,128)S(1)}, u32[]{:S(2)}, u32[]{:S(2)}) %collective-permute-start.7) | collective-permute-done | bytes 4128 | tf_op jit(solution)/shard_map/ppermute | solution.py:467
  182.9 2.7 %scaled_estimate.1 = f32[256,4096]{1,0:T(8,128)} custom-call(s32[2]{0:T(128)S(1)} %get-tuple-element.29.marks_ref.refs_0_, f32[256,4096]{1,0:T(8,128)S(1)} %get-tuple-element.54.refs_1_, f32[8,128]{1,0:T(8,128)S(1)} %chip_power.1.refs_2_, f32[8,128]{1,0:T(8,128)S(1)} %collective-permute-done.7.refs_3_, f32[8,128]{1,0:T(8,128)S(1)} %collective-permute-done.8.refs_4_), custom_call_target="tpu_custom_call" | custom-call | tf_op jit(solution)/shard_map/scaled_estimate/pallas_call | solution.py:385
  (2 shorter events, 0.0 us)
Async XLA Ops:
  7.8 4.3 %collective-permute-start = (bf16[128,512]{1,0:T(8,128)(2,1)S(1)}, bf16[128,512]{1,0:T(8,128)(2,1)S(1)}, u32[]{:S(2)}, u32[]{:S(2)}) collective-permute-start(bf16[128,512]{1,0:T(8,128)(2,1)S(1)} %get-tuple-element.31), channel_id=1, source_target_pairs={{0,1},{1,0},{2,3},{3,2},{4,5},{5,4},{6,7},{7,6},{8,9},{9,8},{10,11... | collective-permute-start | bytes 393224 | tf_op jit(solution)/shard_map/ppermute | solution.py:423
  54.4 3.9 %collective-permute-start.1 = (bf16[512,128]{1,0:T(8,128)(2,1)S(1)}, bf16[512,128]{1,0:T(8,128)(2,1)S(1)}, u32[]{:S(2)}, u32[]{:S(2)}) collective-permute-start(bf16[512,128]{1,0:T(8,128)(2,1)S(1)} %bitcast.29), channel_id=1, source_target_pairs={{0,1},{1,0},{2,3},{3,2},{4,5},{5,4},{6,7},{7,6},{8,9},{9,8},{10,11... | collective-permute-start | bytes 393224 | tf_op jit(solution)/shard_map/ppermute | solution.py:448
  63.9 2.0 %collective-permute-start.2 = (bf16[400,512]{1,0:T(8,128)(2,1)S(1)}, bf16[400,512]{1,0:T(8,128)(2,1)S(1)}, u32[]{:S(2)}, u32[]{:S(2)}) collective-permute-start(bf16[400,512]{1,0:T(8,128)(2,1)S(1)} %get-tuple-element.39), channel_id=1, source_target_pairs={{0,1},{1,0},{2,3},{3,2},{4,5},{5,4},{6,7},{7,6},{8,9},{9,8},{10,11... | collective-permute-start | bytes 1228808 | tf_op jit(solution)/shard_map/ppermute | solution.py:462
  109.3 3.9 %collective-permute-start.3 = (bf16[512,128]{1,0:T(8,128)(2,1)S(1)}, bf16[512,128]{1,0:T(8,128)(2,1)S(1)}, u32[]{:S(2)}, u32[]{:S(2)}) collective-permute-start(bf16[512,128]{1,0:T(8,128)(2,1)S(1)} %bitcast.27), channel_id=1, source_target_pairs={{0,1},{1,0},{2,3},{3,2},{4,5},{5,4},{6,7},{7,6},{8,9},{9,8},{10,11... | collective-permute-start | bytes 393224 | tf_op jit(solution)/shard_map/ppermute | solution.py:448
  118.9 1.8 collective-permute-start.4
  165.0 4.8 %collective-permute-start.5 = (bf16[1024,128]{1,0:T(8,128)(2,1)S(1)}, bf16[1024,128]{1,0:T(8,128)(2,1)S(1)}, u32[]{:S(2)}, u32[]{:S(2)}) collective-permute-start(bf16[1024,128]{1,0:T(8,128)(2,1)S(1)} %bitcast.22), channel_id=1, source_target_pairs={{0,1},{1,0},{2,3},{3,2},{4,5},{5,4},{6,7},{7,6},{8,9},{9,8},{10,11... | collective-permute-start | bytes 786440 | tf_op jit(solution)/shard_map/ppermute | solution.py:448
  172.5 1.2 collective-permute-start.6
  173.7 2.5 %collective-permute-start.8 = (f32[8,128]{1,0:T(8,128)S(1)}, f32[8,128]{1,0:T(8,128)S(1)}, u32[]{:S(2)}, u32[]{:S(2)}) collective-permute-start(f32[8,128]{1,0:T(8,128)S(1)} %chip_power.1.refs_2_), channel_id=1, source_target_pairs={{2,0},{4,2},{6,4},{8,6},{10,8},{12,10},{14,12},{16,14},{18,16},{20... | collective-permute-start | bytes 12296 | tf_op jit(solution)/shard_map/ppermute | solution.py:468
  175.0 7.9 %collective-permute-start.7 = (f32[8,128]{1,0:T(8,128)S(1)}, f32[8,128]{1,0:T(8,128)S(1)}, u32[]{:S(2)}, u32[]{:S(2)}) collective-permute-start(f32[8,128]{1,0:T(8,128)S(1)} %chip_power.1.refs_2_), channel_id=1, source_target_pairs={{0,2},{2,4},{4,6},{6,8},{8,10},{10,12},{12,14},{14,16},{16,18},{18... | collective-permute-start | bytes 12296 | tf_op jit(solution)/shard_map/ppermute | solution.py:467

commit v4 on v3

v4 whole, which is shorter than its diff:
```python
import math

import jax
import jax.numpy as jnp
import numpy as np
from jax import lax
from jax.experimental import pallas as pl
from jax.experimental.pallas import tpu as pltpu
from jax.sharding import Mesh
from jax.sharding import PartitionSpec as P

K = 64
GROUP = 2048
ITERS = 3
LANES = 128
BLOCK = 512
SPILL = 64

step_size = 0.5
shrink_one = 0.05
group_weight = 0.03
epsilon = 1e-06

F32 = jnp.float32
BF16 = jnp.bfloat16
HIGHEST = lax.Precision.HIGHEST
PARAMS = pltpu.CompilerParams(vmem_limit_bytes=16 * 1024 * 1024)
AXES = {"x": 4, "z": 8, "y": 4}
SRC = ("x", "z", "y")
PLANE = ("x", "y")


def windowed_cosines():
    t = np.arange(K)[:, None] + 0.5
    k = np.arange(K)[None, :] + 0.5
    return (np.sin(np.pi * t / K) * np.sqrt(2.0 / K) * np.cos(np.pi * k * t / K)).astype(np.float32)


def split(x):
    high = x.astype(BF16)
    return high, (x - high.astype(F32)).astype(BF16)


def dot(a, b):
    return jnp.dot(a, b, preferred_element_type=F32)


def dot_t(a, b):
    return lax.dot_general(a, b, (((1,), (1,)), ((), ())), preferred_element_type=F32)


def to_samples(atoms_ref, sums):
    high, low = split(sums)
    return dot(atoms_ref[0], high) + dot(atoms_ref[0], low) + dot(atoms_ref[1], high)


def group_scale(power, tau):
    return jnp.maximum(0.0, 1.0 - tau / jnp.sqrt(power + epsilon))


def scales_of(chip_ref, before_ref, after_ref, tau):
    return (
        group_scale(chip_ref[0:1, :] + before_ref[2:3, :], tau),
        group_scale(chip_ref[1:2, :], tau),
        group_scale(chip_ref[2:3, :] + after_ref[0:1, :], tau),
    )


def first_kernel(
    where_ref, offsets_hbm, wave_hbm, group_hbm, depth_hbm, measured_hbm, coef_hbm, lead_hbm,
    table_ref, table_t_ref, mine_ref, theirs_ref, marks_ref, rows_ref, depth_ref, coef_ref, lead_ref,
    offsets_ref, wave_ref, group_ref, measured_ref, acc_ref, coef_sem, lead_sem, small_sem,
):
    total = table_ref.shape[2]
    own = mine_ref.shape[0]
    sources = lead_ref.shape[1]
    blocks = lead_sem.shape[0]
    block = sources // blocks
    pairs = (
        (offsets_hbm, offsets_ref), (wave_hbm, wave_ref), (group_hbm, group_ref), (measured_hbm, measured_ref),
        (depth_hbm, depth_ref),
    )
    small = [pltpu.make_async_copy(a, b, small_sem.at[n]) for n, (a, b) in enumerate(pairs)]
    for load in small:
        load.start()
    loads = []
    for j in range(blocks):
        cols = slice(j * block, (j + 1) * block)
        loads.append(
            (
                pltpu.make_async_copy(lead_hbm.at[:, cols], lead_ref.at[:, cols], lead_sem.at[j]),
                pltpu.make_async_copy(coef_hbm.at[:, cols], coef_ref.at[:, cols], coef_sem.at[j]),
            )
        )
        for load in loads[-1]:
            load.start()
    for load in small:
        load.wait()

    groups = group_ref[...]
    marks_ref[0] = jnp.sum((groups == groups[0:1, 0:1]).astype(jnp.int32))
    marks_ref[1] = where_ref[1]
    for t in range(measured_ref.shape[0] // LANES):
        lanes = slice(t * LANES, (t + 1) * LANES)
        rows_ref[:, lanes] = measured_ref[lanes, :].T
    wave = wave_ref[...]
    order = lax.broadcasted_iota(jnp.int32, (total, K), 0)
    sample = lax.rem(order + where_ref[0], total)
    position = lax.broadcasted_iota(jnp.int32, (total, K), 1)
    for f in range(offsets_ref.shape[0]):
        delay = lax.rem(sample - offsets_ref[f] + total, total)
        placing = (delay == position).astype(F32)
        part_t = jnp.dot(placing, wave, precision=HIGHEST, preferred_element_type=F32)
        rows = slice(f * K, (f + 1) * K)
        table_t_ref[0, :, rows], table_t_ref[1, :, rows] = split(part_t)
        table_ref[0, rows, :], table_ref[1, rows, :] = split(part_t.T)

    for j in range(blocks):
        for load in loads[j]:
            load.wait()
        cols = slice(j * block, (j + 1) * block)
        part = dot_t((coef_ref[:, cols] * depth_ref[:, cols]).astype(BF16), lead_ref[:, cols])
        if j == 0:
            acc_ref[...] = part
        else:
            acc_ref[...] += part
    samples = to_samples(table_t_ref, acc_ref[...])
    mine_ref[...] = samples[:own]
    theirs_ref[...] = samples[own : own + SPILL].astype(BF16)


def slabs(x):
    return [x[i : i + 8] for i in range(0, x.shape[0], 8)]


def step_kernel(
    marks_ref, own_ref, other_ref, table_ref, depth_ref, state_ref, lead_ref, *rest, first, last, block
):
    if not first:
        scale_ref, *rest = rest
    new_ref, power_ref, samples_ref, turned_ref = rest
    sources = state_ref.shape[1]
    own = table_ref.shape[2] // 2

    for h, ref in enumerate((own_ref, other_ref)):
        samples = ref[...]
        if last:
            samples = jnp.concatenate(slabs(samples.astype(F32))[::2], axis=0).astype(BF16)
        samples_ref[h * own : (h + 1) * own, :] = samples
    turned = dot(table_ref[0], samples_ref[...]) + dot(table_ref[1], samples_ref[...])
    turned_ref[...] = turned.astype(BF16)

    start = marks_ref[0]
    bounds = (start, start + GROUP)
    scales = None if first else [scale_ref[g : g + 1, 0:1] for g in range(3)]
    sums = [jnp.zeros((1, block), F32) for _ in range(4)]
    for j in range(sources // block):
        cols = slice(j * block, (j + 1) * block)
        half = j * block // GROUP
        gradient = dot(turned_ref[...], lead_ref[:, cols])
        source = j * block + lax.broadcasted_iota(jnp.int32, (1, block), 1)
        before = source < bounds[half]
        state = state_ref[:, cols]
        if not first:
            state = state * jnp.where(before, scales[half], scales[half + 1])
        moved = state + (step_size * depth_ref[:, cols]) * gradient
        shrunk = moved - jnp.clip(moved, -shrink_one, shrink_one)
        new_ref[:, cols] = shrunk
        squares = jnp.sum(shrunk * shrunk, axis=0, keepdims=True)
        sums[2 * half] += jnp.where(before, squares, 0.0)
        sums[2 * half + 1] += jnp.where(before, 0.0, squares)
    power_ref[...] = jnp.zeros_like(power_ref)
    for g, total in enumerate((sums[0], sums[1] + sums[2], sums[3])):
        power_ref[g : g + 1, :] = jnp.broadcast_to(jnp.sum(total, axis=1, keepdims=True), (1, LANES))


def forward_kernel(
    marks_ref, state_ref, depth_ref, lead_ref, table_t_ref, chip_ref, mine_ref, theirs_ref, weighted_ref, *,
    block, tau,
):
    coefs, sources = state_ref.shape
    own = mine_ref.shape[0] // 3
    start = marks_ref[0]
    bounds = (start, start + GROUP)
    none = jnp.zeros((), BF16)
    for j in range(sources // block):
        cols = slice(j * block, (j + 1) * block)
        half = j * block // GROUP
        before = j * block + lax.broadcasted_iota(jnp.int32, (1, block), 1) < bounds[half]
        weighted = (state_ref[:, cols] * depth_ref[:, cols]).astype(BF16)
        inner = slice(j * block - half * GROUP, (j + 1) * block - half * GROUP)
        weighted_ref[half, :coefs, inner] = jnp.where(before, weighted, none)
        weighted_ref[half, coefs:, inner] = jnp.where(before, none, weighted)
    halves = [dot_t(weighted_ref[h], lead_ref[:, h * GROUP : (h + 1) * GROUP]) for h in range(2)]
    middle = group_scale(chip_ref[1:2, 0:1], tau) * (halves[0][coefs:] + halves[1][:coefs])
    parts = (halves[0][:coefs], middle, halves[1][coefs:])
    for g in range(3):
        samples = to_samples(table_t_ref, parts[g])
        mine_ref[g * own : (g + 1) * own, :] = samples[:own]
        theirs_ref[g * SPILL : (g + 1) * SPILL, :] = samples[own : own + SPILL].astype(BF16)


def fold_kernel(mine_ref, theirs_ref, *rest, tau=None):
    *powers, out_ref = rest if tau is None else rest[:-1]
    own = out_ref.shape[0]
    if tau is None:
        mine, theirs = mine_ref[...], theirs_ref[...].astype(F32)
    else:
        scale_ref = rest[-1]
        scales = scales_of(*powers, tau)
        scale_ref[...] = jnp.zeros_like(scale_ref)
        mine, theirs = 0.0, 0.0
        for g, scale in enumerate(scales):
            scale_ref[g : g + 1, :] = scale
            scale = 1.0 if g == 1 else scale[:, 0:1]
            mine += scale * mine_ref[g * own : (g + 1) * own, :]
            theirs += scale * theirs_ref[g * SPILL : (g + 1) * SPILL, :].astype(F32)
    out_ref[:SPILL] = (mine[:SPILL] + theirs).astype(BF16)
    out_ref[SPILL:] = mine[SPILL:].astype(BF16)


def plane_kernel(got_ref, out_ref):
    total = sum(slabs(got_ref[...].astype(F32)))
    out_ref[...] = jnp.concatenate([total] * (out_ref.shape[0] // 8), axis=0)


def owner_kernel(marks_ref, got_ref, measured_ref, out_ref, *, last):
    at = pl.ds(pl.multiple_of(marks_ref[1] * 8, 8), 8)
    row = measured_ref[at, :] - sum(slabs(got_ref[...]))
    if last:
        high = row.astype(BF16).astype(F32)
        row = jnp.concatenate([high, row - high], axis=0)
    out_ref[...] = jnp.concatenate([row] * (out_ref.shape[0] // row.shape[0]), axis=0).astype(BF16)


def add_kernel(a_ref, b_ref, out_ref):
    out_ref[...] = a_ref[...] + b_ref[...]


def residual_kernel(own_ref, out_ref):
    pieces = slabs(own_ref[...].astype(F32))
    rows = jnp.concatenate([high + low for high, low in zip(pieces[::2], pieces[1::2])], axis=0)
    for t in range(out_ref.shape[0] // LANES):
        lanes = slice(t * LANES, (t + 1) * LANES)
        out_ref[lanes, :] = rows[:, lanes].T


def last_kernel(marks_ref, state_ref, chip_ref, before_ref, after_ref, out_hbm, scaled_ref, sem, *, tau):
    blocks, _, block = scaled_ref.shape
    scales = [scale[:, 0:1] for scale in scales_of(chip_ref, before_ref, after_ref, tau)]
    start = marks_ref[0]
    bounds = (start, start + GROUP)
    stores = []
    for j in range(blocks):
        cols = slice(j * block, (j + 1) * block)
        half = j * block // GROUP
        before = j * block + lax.broadcasted_iota(jnp.int32, (1, block), 1) < bounds[half]
        scaled_ref[j] = state_ref[:, cols] * jnp.where(before, scales[half], scales[half + 1])
        stores.append(pltpu.make_async_copy(scaled_ref.at[j], out_hbm.at[:, cols], sem.at[j]))
        stores[-1].start()
    for store in stores:
        store.wait()


SMEM = pl.BlockSpec(memory_space=pltpu.SMEM)
VMEM = pl.BlockSpec(memory_space=pltpu.VMEM)
HBM = pl.BlockSpec(memory_space=pltpu.HBM)


def struct(dtype, *shape):
    return jax.ShapeDtypeStruct(shape, dtype)


def call(kernel, name, args, outs, *, ins=None, out_specs=None, scratch=(), cost=None):
    return pl.pallas_call(
        kernel, in_specs=ins or [VMEM] * len(args), out_specs=out_specs or [VMEM] * len(outs), out_shape=outs,
        scratch_shapes=list(scratch), compiler_params=PARAMS, name=name, cost_estimate=cost,
    )(*args)


def stay(x):
    return pltpu.with_memory_space_constraint(x, pltpu.HBM)


def first_call(where, offsets, groups, depth, measured, state, lead):
    coefs, sources = state.shape
    sensors, own = measured.shape
    total = 2 * own
    dma = pltpu.SemaphoreType.DMA((sources // BLOCK,))
    inputs = (offsets, jnp.asarray(windowed_cosines()), groups, depth, measured, state, lead)
    return call(
        first_kernel,
        "first_forward",
        [where] + [stay(x) for x in inputs],
        [
            struct(BF16, 2, coefs, total),
            struct(BF16, 2, total, coefs),
            struct(F32, own, sensors),
            struct(BF16, SPILL, sensors),
            struct(jnp.int32, 2),
            struct(F32, own, sensors),
            struct(F32, 1, sources),
            struct(F32, coefs, sources),
            struct(BF16, sensors, sources),
        ],
        ins=[SMEM] + [HBM] * len(inputs),
        out_specs=[VMEM, VMEM, VMEM, VMEM, SMEM, VMEM, VMEM, VMEM, VMEM],
        scratch=[
            pltpu.SMEM(offsets.shape, jnp.int32),
            pltpu.VMEM((K, K), F32),
            pltpu.VMEM((1, sources), jnp.int32),
            pltpu.VMEM((sensors, own), F32),
            pltpu.VMEM((coefs, sensors), F32),
            dma,
            dma,
            pltpu.SemaphoreType.DMA((5,)),
        ],
    )


def step_call(marks, mine, others, table, scale, depth, state, lead, *, first, last):
    coefs, sources = state.shape
    sensors = lead.shape[0]
    args = [marks, mine, others, table, depth, state, lead] + ([] if first else [scale])
    return call(
        lambda *refs: step_kernel(*refs, first=first, last=last, block=BLOCK),
        "step",
        args,
        [struct(F32, coefs, sources), struct(F32, 8, LANES)],
        ins=[SMEM] + [VMEM] * (len(args) - 1),
        scratch=[pltpu.VMEM((table.shape[2], sensors), BF16), pltpu.VMEM((coefs, sensors), BF16)],
    )


def forward_call(marks, state, depth, lead, table_t, chip, tau):
    coefs, sources = state.shape
    sensors = lead.shape[0]
    own = table_t.shape[1] // 2
    return call(
        lambda *refs: forward_kernel(*refs, block=BLOCK, tau=tau),
        "forward",
        [marks, state, depth, lead, table_t, chip],
        [struct(F32, 3 * own, sensors), struct(BF16, 3 * SPILL, sensors)],
        ins=[SMEM] + [VMEM] * 5,
        scratch=[pltpu.VMEM((2, 2 * coefs, GROUP), BF16)],
        cost=pl.CostEstimate(flops=4 * coefs * sources * sensors, bytes_accessed=8 << 20, transcendentals=0),
    )


def last_call(marks, state, chip, before, after, tau):
    coefs, sources = state.shape
    blocks = sources // BLOCK
    return call(
        lambda *refs: last_kernel(*refs, tau=tau),
        "scaled_estimate",
        [marks, state, chip, before, after],
        [struct(F32, coefs, sources)],
        ins=[SMEM] + [VMEM] * 4,
        out_specs=[HBM],
        scratch=[pltpu.VMEM((blocks, coefs, BLOCK), F32), pltpu.SemaphoreType.DMA((blocks,))],
    )[0]


def shards(measured, lead_field, depth, coefficients, offsets, group_ids):
    sensors, own = measured.shape
    sources = lead_field.shape[1]
    frames = coefficients.shape[1]
    frm_count = lax.axis_size("frm")
    src_count = math.prod(AXES.values())
    coefs = frames * K
    tau = group_weight * math.sqrt(GROUP * frames * frm_count * K)
    across = [(i, (i + 1) % frm_count) for i in range(frm_count)]
    ahead = [(i, (i + 1) % src_count) for i in range(src_count)]
    behind = [((i + 1) % src_count, i) for i in range(src_count)]
    where = jnp.stack([lax.axis_index("frm") * own, lax.axis_index(PLANE)])

    def exchange(rows, axes):
        return lax.all_to_all(rows, axes, 0, 0, tiled=True)

    def chip_sums(power):
        chip = call(add_kernel, "chip_power", [power, lax.ppermute(power, "frm", across)], [struct(F32, 8, LANES)])[0]
        return chip, lax.ppermute(chip, SRC, ahead), lax.ppermute(chip, SRC, behind)

    state = coefficients.transpose(1, 2, 0).reshape(coefs, sources)
    table, table_t, mine, theirs, marks, rows, depth_row, state, lead = first_call(
        where, offsets, group_ids.reshape(1, sources), depth.reshape(1, sources), measured, state, lead_field
    )
    folded = call(
        fold_kernel, "first_fold", [mine, lax.ppermute(theirs, "frm", across)], [struct(BF16, own, sensors)]
    )[0]
    scale = None
    for iteration in range(ITERS):
        first, last = iteration == 0, iteration == ITERS - 1
        plane = call(
            plane_kernel, "plane_sum", [exchange(folded, PLANE)], [struct(F32, 8 * AXES["z"], sensors)]
        )[0]
        slab = call(
            lambda *refs, last=last: owner_kernel(*refs, last=last),
            "owner",
            [marks, exchange(plane, "z"), rows],
            [struct(BF16, own * (2 if last else 1), sensors)],
            ins=[SMEM, VMEM, VMEM],
        )[0]
        mine = exchange(slab, PLANE)
        others = lax.ppermute(mine, "frm", across)
        state, power = step_call(
            marks, mine, others, table, scale, depth_row, state, lead, first=first, last=last
        )
        chip, before, after = chip_sums(power)
        if not last:
            parts, theirs = forward_call(marks, state, depth_row, lead, table_t, chip, tau)
            theirs, before, after = lax.optimization_barrier((theirs, before, after))
            folded, scale = call(
                lambda *refs: fold_kernel(*refs, tau=tau),
                "fold",
                [parts, lax.ppermute(theirs, "frm", across), chip, before, after],
                [struct(BF16, own, sensors), struct(F32, 8, LANES)],
            )

    residual = call(residual_kernel, "residual", [mine], [struct(F32, sensors, own)])[0]
    estimate = last_call(marks, state, chip, before, after, tau)
    return (estimate.reshape(frames, K, sources).transpose(2, 0, 1), residual)


def solution(mesh):
    fine = Mesh(mesh.devices.reshape(*AXES.values(), mesh.shape["frm"]), (*AXES, "frm"))
    return jax.shard_map(
        shards,
        mesh=fine,
        in_specs=(
            P(None, "frm"),
            P(None, SRC),
            P(SRC),
            P(SRC, "frm", None),
            P("frm"),
            P(SRC),
        ),
        out_specs=(P(SRC, "frm", None), P(None, "frm")),
        check_vma=False,
    )
```

time: 186 us -> 173 us (0.930)
  blocking collectives: 126 us -> 97.7 us
  starting transfers between devices: 15.9 us -> 24.3 us
  waiting for transfers between devices: 14.6 us -> 22.8 us
    all_to_all x6 -> x9, blocking collectives: 126 us -> 97.7 us  [exchange(): return lax.all_to_all(rows, axes, 0, 0, tiled=True)]
    ppermute x5 -> x9, waiting for transfers between devices: 10.5 us -> 16.7 us  [the longest x3 14 us: chip_sums(): lax.ppermute(chip, SRC, ahead)]
    ppermute x1 -> x3, starting transfers between devices: 3.34 us -> 6.87 us  [shards(): lax.ppermute(theirs, 'frm', across)]
    ppermute x5 -> x9, starting transfers between devices: 2.95 us -> 5.56 us  [the longest x3 2.87 us: chip_sums(): lax.ppermute(chip, SRC, behind)]
    ppermute x3, starting transfers between devices: 9.56 us -> 11.9 us  [shards(): others = lax.ppermute(mine, 'frm', across)]
    ppermute x1 -> x3, waiting for transfers between devices: 0.99 us -> 3.04 us  [shards(): lax.ppermute(theirs, 'frm', across)]
    pallas_call x13 -> x20, Pallas kernels: 28.4 us -> 27.2 us  [call(): pl.pallas_call(kernel, in_specs=ins or [VMEM] * len(args), out_specs=out_...]
  transfers between devices with their start and end apart: 9 -> 15, of which waited for: 9 -> 13; matrix products, arithmetic and copies ran while one was open for 0% -> 0% of each run, Pallas kernels for 0% -> 5%
where the time goes in v4:
time: 173 us
  blocking collectives  97.7 us (56%)
  Pallas kernels  27.2 us (16%)
  starting transfers between devices  24.3 us (14%)
  waiting for transfers between devices  22.8 us (13%)
    all_to_all x9, blocking collectives, exchange(): return lax.all_to_all(rows, axes, 0, 0, tiled=True)  97.7 us
    pallas_call x20, Pallas kernels, call(): pl.pallas_call(kernel, in_specs=ins or [VMEM] * len(args), out_specs=out_...  27.2 us
    ppermute x3, waiting for transfers between devices, chip_sums(): lax.ppermute(chip, SRC, ahead)  14 us
    ppermute x3, starting transfers between devices, shards(): others = lax.ppermute(mine, 'frm', across)  11.9 us
    ppermute x3, starting transfers between devices, shards(): lax.ppermute(theirs, 'frm', across)  6.87 us
  transfers between devices with their start and end apart: 15, of which 13 were waited for; matrix products, arithmetic and copies ran while one was open for 0% of the time, Pallas kernels for 5%

profile of v4, /device:TPU:1, one launch (start us, length us, event | category | flops | bytes accessed | tf_op | source)
XLA Modules:
  0.0 173.0 jit_solution(9237247328316650689)
XLA Ops:
  0.7 7.0 %first_forward.1 = (bf16[2,256,256]{2,1,0:T(8,128)(2,1)S(1)}, bf16[2,256,256]{2,1,0:T(8,128)(2,1)S(1)}, f32[128,512]{1,0:T(8,128)S(1)}, bf16[64,512]{1,0:T(8,128...) custom-call(s32[2]{0:T(128)S(1)} %pad_add_fusion.where_ref, ...), custom_call_target="tpu_custom_call" | custom-call | tf_op jit(solution)/shard_map/first_forward/pallas_call | solution.py:275
  7.7 3.3 %collective-permute-start = (bf16[64,512]{1,0:T(8,128)(2,1)S(1)}, bf16[64,512]{1,0:T(8,128)(2,1)S(1)}, u32[]{:S(2)}, u32[]{:S(2)}) collective-permute-start(bf16[64,512]{1,0:T(8,128)(2,1)S(1)} %get-tuple-element.33), channel_id=1, source_target_pairs={{0,1},{1,0},{2,3},{3,2},{4,5},{5,4},{6,7},{7,6},{8,9},{9,8},{10,11... | collective-permute-start | bytes 196616 | tf_op jit(solution)/shard_map/ppermute | solution.py:389
  11.1 0.9 collective-permute-done.theirs_ref
  12.0 11.5 %all_to_all.99 = bf16[16,8,512]{2,1,0:T(8,128)(2,1)S(1)} all-to-all(bf16[16,8,512]{2,1,0:T(8,128)(2,1)S(1)} %bitcast.36), channel_id=1, replica_groups=mesh['x'=4,'z'=8,'y'=4,'frm'=2] {'x','y'}, dimensions={0} | all-to-all | bytes 262144 | tf_op jit(solution)/shard_map/all_to_all | solution.py:378
  23.5 16.0 %all_to_all.100 = f32[8,8,512]{2,1,0:T(8,128)S(1)} all-to-all(f32[8,8,512]{2,1,0:T(8,128)S(1)} %bitcast.42), channel_id=1, replica_groups=mesh['x'=4,'z'=8,'y'=4,'frm'=2] {'z'}, dimensions={0} | all-to-all | bytes 262144 | tf_op jit(solution)/shard_map/all_to_all | solution.py:378
  39.5 0.6 owner.3
  40.1 10.0 %all_to_all.101 = bf16[16,8,512]{2,1,0:T(8,128)(2,1)S(1)} all-to-all(bf16[16,8,512]{2,1,0:T(8,128)(2,1)S(1)} %bitcast.38), channel_id=1, replica_groups=mesh['x'=4,'z'=8,'y'=4,'frm'=2] {'x','y'}, dimensions={0} | all-to-all | bytes 262144 | tf_op jit(solution)/shard_map/all_to_all | solution.py:378
  50.1 4.3 %collective-permute-start.1 = (bf16[128,512]{1,0:T(8,128)(2,1)S(1)}, bf16[128,512]{1,0:T(8,128)(2,1)S(1)}, u32[]{:S(2)}, u32[]{:S(2)}) collective-permute-start(bf16[128,512]{1,0:T(8,128)(2,1)S(1)} %bitcast.34), channel_id=1, source_target_pairs={{0,1},{1,0},{2,3},{3,2},{4,5},{5,4},{6,7},{7,6},{8,9},{9,8},{10,11... | collective-permute-start | bytes 393224 | tf_op jit(solution)/shard_map/ppermute | solution.py:405
  54.5 1.0 collective-permute-done.1.refs_2_
  55.4 2.4 %step.3 = (f32[256,4096]{1,0:T(8,128)S(1)}, f32[8,128]{1,0:T(8,128)S(1)}) custom-call(s32[2]{0:T(128)S(1)} %get-tuple-element.31.refs_0_, bf16[128,512]{1,0:T(8,128)(2,1)S(1)} %bitcast.35, bf16[128,512]{1,0:T(8,128)(2,1)S(1)} %collective-permute-done.1.refs_2_, bf16[2,256,256]{2,1,0:T(8,128)(2,1)S(1)} %get-tuple-element.35.refs_3_, ...), custom_call_target="tpu_custom_call" | custom-call | tf_op jit(solution)/shard_map/step/pallas_call | solution.py:275
  57.9 0.4 collective-permute-start.2
  58.2 0.8 collective-permute-done.2.b_ref
  59.1 1.4 collective-permute-start.4
  60.5 3.5 %forward.2 = (f32[384,512]{1,0:T(8,128)S(1)}, bf16[192,512]{1,0:T(8,128)(2,1)S(1)}) custom-call(s32[2]{0:T(128)S(1)} %get-tuple-element.31.refs_0_, f32[256,4096]{1,0:T(8,128)S(1)} %get-tuple-element.39.refs_1_.refs_5_, f32[1,4096]{1,0:T(1,128)S(1)} %get-tuple-element.36.refs_4_.refs_2_, bf16[512,4096]{1,0:T(8,128)(2,1)S(1)} %get-tuple-element.38.refs_6_.refs_3_, ...), custom_call_target="tpu_custom_call" | custom-call | flops 2147483648 | bytes 8388608 | tf_op jit(solution)/shard_map/forward/pallas_call | solution.py:275
  64.1 4.3 %collective-permute-done.3.refs_3_ = f32[8,128]{1,0:T(8,128)S(1)} collective-permute-done((f32[8,128]{1,0:T(8,128)S(1)}, f32[8,128]{1,0:T(8,128)S(1)}, u32[]{:S(2)}, u32[]{:S(2)}) %collective-permute-start.3) | collective-permute-done | bytes 4128 | tf_op jit(solution)/shard_map/ppermute | solution.py:382
  68.3 1.8 %collective-permute-start.5 = (bf16[192,512]{1,0:T(8,128)(2,1)S(1)}, bf16[192,512]{1,0:T(8,128)(2,1)S(1)}, u32[]{:S(2)}, u32[]{:S(2)}) collective-permute-start(bf16[192,512]{1,0:T(8,128)(2,1)S(1)} %get-tuple-element.44), channel_id=1, source_target_pairs={{0,1},{1,0},{2,3},{3,2},{4,5},{5,4},{6,7},{7,6},{8,9},{9,8},{10,11... | collective-permute-start | bytes 589832 | tf_op jit(solution)/shard_map/ppermute | solution.py:416
  70.1 1.1 collective-permute-done.5.refs_1_
  71.2 0.2 fold.2
  71.4 9.3 %all_to_all.102 = bf16[16,8,512]{2,1,0:T(8,128)(2,1)S(1)} all-to-all(bf16[16,8,512]{2,1,0:T(8,128)(2,1)S(1)} %bitcast.48), channel_id=1, replica_groups=mesh['x'=4,'z'=8,'y'=4,'frm'=2] {'x','y'}, dimensions={0} | all-to-all | bytes 262144 | tf_op jit(solution)/shard_map/all_to_all | solution.py:378
  80.7 10.4 %all_to_all.103 = f32[8,8,512]{2,1,0:T(8,128)S(1)} all-to-all(f32[8,8,512]{2,1,0:T(8,128)S(1)} %bitcast.44), channel_id=1, replica_groups=mesh['x'=4,'z'=8,'y'=4,'frm'=2] {'z'}, dimensions={0} | all-to-all | bytes 262144 | tf_op jit(solution)/shard_map/all_to_all | solution.py:378
  91.2 0.6 owner.4
  91.7 10.0 %all_to_all.104 = bf16[16,8,512]{2,1,0:T(8,128)(2,1)S(1)} all-to-all(bf16[16,8,512]{2,1,0:T(8,128)(2,1)S(1)} %bitcast.40), channel_id=1, replica_groups=mesh['x'=4,'z'=8,'y'=4,'frm'=2] {'x','y'}, dimensions={0} | all-to-all | bytes 262144 | tf_op jit(solution)/shard_map/all_to_all | solution.py:378
  101.7 3.8 %collective-permute-start.6 = (bf16[128,512]{1,0:T(8,128)(2,1)S(1)}, bf16[128,512]{1,0:T(8,128)(2,1)S(1)}, u32[]{:S(2)}, u32[]{:S(2)}) collective-permute-start(bf16[128,512]{1,0:T(8,128)(2,1)S(1)} %bitcast.32), channel_id=1, source_target_pairs={{0,1},{1,0},{2,3},{3,2},{4,5},{5,4},{6,7},{7,6},{8,9},{9,8},{10,11... | collective-permute-start | bytes 393224 | tf_op jit(solution)/shard_map/ppermute | solution.py:405
  105.5 1.0 collective-permute-done.6.refs_2_
  106.5 2.5 %step.4 = (f32[256,4096]{1,0:T(8,128)S(1)}, f32[8,128]{1,0:T(8,128)S(1)}) custom-call(s32[2]{0:T(128)S(1)} %get-tuple-element.31.refs_0_, bf16[128,512]{1,0:T(8,128)(2,1)S(1)} %bitcast.33, bf16[128,512]{1,0:T(8,128)(2,1)S(1)} %collective-permute-done.6.refs_2_, bf16[2,256,256]{2,1,0:T(8,128)(2,1)S(1)} %get-tuple-element.35.refs_3_, ...), custom_call_target="tpu_custom_call" | custom-call | tf_op jit(solution)/shard_map/step/pallas_call | solution.py:275
  109.0 0.4 collective-permute-start.7
  109.4 0.8 collective-permute-done.7.b_ref
  110.2 0.9 collective-permute-start.9
  111.1 0.5 collective-permute-start.8
  111.7 3.5 %forward.3 = (f32[384,512]{1,0:T(8,128)S(1)}, bf16[192,512]{1,0:T(8,128)(2,1)S(1)}) custom-call(s32[2]{0:T(128)S(1)} %get-tuple-element.31.refs_0_, f32[256,4096]{1,0:T(8,128)S(1)} %get-tuple-element.49.refs_1_.refs_5_, f32[1,4096]{1,0:T(1,128)S(1)} %get-tuple-element.36.refs_4_.refs_2_, bf16[512,4096]{1,0:T(8,128)(2,1)S(1)} %get-tuple-element.38.refs_6_.refs_3_, ...), custom_call_target="tpu_custom_call" | custom-call | flops 2147483648 | bytes 8388608 | tf_op jit(solution)/shard_map/forward/pallas_call | solution.py:275
  115.2 3.8 %collective-permute-done.8.refs_3_ = f32[8,128]{1,0:T(8,128)S(1)} collective-permute-done((f32[8,128]{1,0:T(8,128)S(1)}, f32[8,128]{1,0:T(8,128)S(1)}, u32[]{:S(2)}, u32[]{:S(2)}) %collective-permute-start.8) | collective-permute-done | bytes 4128 | tf_op jit(solution)/shard_map/ppermute | solution.py:382
  119.0 1.8 %collective-permute-start.10 = (bf16[192,512]{1,0:T(8,128)(2,1)S(1)}, bf16[192,512]{1,0:T(8,128)(2,1)S(1)}, u32[]{:S(2)}, u32[]{:S(2)}) collective-permute-start(bf16[192,512]{1,0:T(8,128)(2,1)S(1)} %get-tuple-element.53), channel_id=1, source_target_pairs={{0,1},{1,0},{2,3},{3,2},{4,5},{5,4},{6,7},{7,6},{8,9},{9,8},{10,11... | collective-permute-start | bytes 589832 | tf_op jit(solution)/shard_map/ppermute | solution.py:416
  120.8 1.1 collective-permute-done.10.refs_1_
  121.8 0.2 fold.3
  122.0 9.3 %all_to_all.105 = bf16[16,8,512]{2,1,0:T(8,128)(2,1)S(1)} all-to-all(bf16[16,8,512]{2,1,0:T(8,128)(2,1)S(1)} %bitcast.49), channel_id=1, replica_groups=mesh['x'=4,'z'=8,'y'=4,'frm'=2] {'x','y'}, dimensions={0} | all-to-all | bytes 262144 | tf_op jit(solution)/shard_map/all_to_all | solution.py:378
  131.4 10.4 %all_to_all.106 = f32[8,8,512]{2,1,0:T(8,128)S(1)} all-to-all(f32[8,8,512]{2,1,0:T(8,128)S(1)} %bitcast.46), channel_id=1, replica_groups=mesh['x'=4,'z'=8,'y'=4,'frm'=2] {'z'}, dimensions={0} | all-to-all | bytes 262144 | tf_op jit(solution)/shard_map/all_to_all | solution.py:378
  141.8 0.6 owner.5
  142.4 10.6 %all_to_all.107 = bf16[16,16,512]{2,1,0:T(8,128)(2,1)S(1)} all-to-all(bf16[16,16,512]{2,1,0:T(8,128)(2,1)S(1)} %bitcast.31), channel_id=1, replica_groups=mesh['x'=4,'z'=8,'y'=4,'frm'=2] {'x','y'}, dimensions={0} | all-to-all | bytes 524288 | tf_op jit(solution)/shard_map/all_to_all | solution.py:378
  153.0 3.8 %collective-permute-start.11 = (bf16[256,512]{1,0:T(8,128)(2,1)S(1)}, bf16[256,512]{1,0:T(8,128)(2,1)S(1)}, u32[]{:S(2)}, u32[]{:S(2)}) collective-permute-start(bf16[256,512]{1,0:T(8,128)(2,1)S(1)} %bitcast.28), channel_id=1, source_target_pairs={{0,1},{1,0},{2,3},{3,2},{4,5},{5,4},{6,7},{7,6},{8,9},{9,8},{10,11... | collective-permute-start | bytes 786440 | tf_op jit(solution)/shard_map/ppermute | solution.py:405
  156.8 1.2 collective-permute-done.11.refs_2_
  157.9 2.5 %step.5 = (f32[256,4096]{1,0:T(8,128)S(1)}, f32[8,128]{1,0:T(8,128)S(1)}) custom-call(s32[2]{0:T(128)S(1)} %get-tuple-element.31.refs_0_, bf16[256,512]{1,0:T(8,128)(2,1)S(1)} %bitcast.29, bf16[256,512]{1,0:T(8,128)(2,1)S(1)} %collective-permute-done.11.refs_2_, bf16[2,256,256]{2,1,0:T(8,128)(2,1)S(1)} %get-tuple-element.35.refs_3_, ...), custom_call_target="tpu_custom_call" | custom-call | tf_op jit(solution)/shard_map/step/pallas_call | solution.py:275
  160.4 0.4 collective-permute-start.12
  160.8 0.8 collective-permute-done.12.b_ref
  161.7 0.6 collective-permute-start.14
  162.2 0.9 collective-permute-start.13
  163.1 0.8 residual.1
  164.1 6.0 %collective-permute-done.13.refs_3_ = f32[8,128]{1,0:T(8,128)S(1)} collective-permute-done((f32[8,128]{1,0:T(8,128)S(1)}, f32[8,128]{1,0:T(8,128)S(1)}, u32[]{:S(2)}, u32[]{:S(2)}) %collective-permute-start.13) | collective-permute-done | bytes 4128 | tf_op jit(solution)/shard_map/ppermute | solution.py:382
  170.1 2.7 %scaled_estimate.1 = f32[256,4096]{1,0:T(8,128)} custom-call(s32[2]{0:T(128)S(1)} %get-tuple-element.31.refs_0_, f32[256,4096]{1,0:T(8,128)S(1)} %get-tuple-element.58.refs_1_, f32[8,128]{1,0:T(8,128)S(1)} %chip_power.5.refs_2_, f32[8,128]{1,0:T(8,128)S(1)} %collective-permute-done.13.refs_3_, f32[8,128]{1,0:T(8,128)S(1)} %collective-permute-done.14.refs_4_), custom_call_target="tpu_custom_call" | custom-call | tf_op jit(solution)/shard_map/scaled_estimate/pallas_call | solution.py:275
  (12 shorter events, 0.4 us)
Async XLA Ops:
  7.7 4.2 %collective-permute-start = (bf16[64,512]{1,0:T(8,128)(2,1)S(1)}, bf16[64,512]{1,0:T(8,128)(2,1)S(1)}, u32[]{:S(2)}, u32[]{:S(2)}) collective-permute-start(bf16[64,512]{1,0:T(8,128)(2,1)S(1)} %get-tuple-element.33), channel_id=1, source_target_pairs={{0,1},{1,0},{2,3},{3,2},{4,5},{5,4},{6,7},{7,6},{8,9},{9,8},{10,11... | collective-permute-start | bytes 196616 | tf_op jit(solution)/shard_map/ppermute | solution.py:389
  50.1 5.3 %collective-permute-start.1 = (bf16[128,512]{1,0:T(8,128)(2,1)S(1)}, bf16[128,512]{1,0:T(8,128)(2,1)S(1)}, u32[]{:S(2)}, u32[]{:S(2)}) collective-permute-start(bf16[128,512]{1,0:T(8,128)(2,1)S(1)} %bitcast.34), channel_id=1, source_target_pairs={{0,1},{1,0},{2,3},{3,2},{4,5},{5,4},{6,7},{7,6},{8,9},{9,8},{10,11... | collective-permute-start | bytes 393224 | tf_op jit(solution)/shard_map/ppermute | solution.py:405
  57.9 1.2 collective-permute-start.2
  59.1 5.0 %collective-permute-start.4 = (f32[8,128]{1,0:T(8,128)S(1)}, f32[8,128]{1,0:T(8,128)S(1)}, u32[]{:S(2)}, u32[]{:S(2)}) collective-permute-start(f32[8,128]{1,0:T(8,128)S(1)} %chip_power.3.refs_5_.refs_2_), channel_id=1, source_target_pairs={{2,0},{4,2},{6,4},{8,6},{10,8},{12,10},{14,12},{16,14},{18,16},{20... | collective-permute-start | bytes 12296 | tf_op jit(solution)/shard_map/ppermute | solution.py:382
  60.5 7.9 %collective-permute-start.3 = (f32[8,128]{1,0:T(8,128)S(1)}, f32[8,128]{1,0:T(8,128)S(1)}, u32[]{:S(2)}, u32[]{:S(2)}) collective-permute-start(f32[8,128]{1,0:T(8,128)S(1)} %chip_power.3.refs_5_.refs_2_), channel_id=1, source_target_pairs={{0,2},{2,4},{4,6},{6,8},{8,10},{10,12},{12,14},{14,16},{16,18},{18... | collective-permute-start | bytes 12296 | tf_op jit(solution)/shard_map/ppermute | solution.py:382
  68.3 2.8 %collective-permute-start.5 = (bf16[192,512]{1,0:T(8,128)(2,1)S(1)}, bf16[192,512]{1,0:T(8,128)(2,1)S(1)}, u32[]{:S(2)}, u32[]{:S(2)}) collective-permute-start(bf16[192,512]{1,0:T(8,128)(2,1)S(1)} %get-tuple-element.44), channel_id=1, source_target_pairs={{0,1},{1,0},{2,3},{3,2},{4,5},{5,4},{6,7},{7,6},{8,9},{9,8},{10,11... | collective-permute-start | bytes 589832 | tf_op jit(solution)/shard_map/ppermute | solution.py:416
  101.7 4.8 %collective-permute-start.6 = (bf16[128,512]{1,0:T(8,128)(2,1)S(1)}, bf16[128,512]{1,0:T(8,128)(2,1)S(1)}, u32[]{:S(2)}, u32[]{:S(2)}) collective-permute-start(bf16[128,512]{1,0:T(8,128)(2,1)S(1)} %bitcast.32), channel_id=1, source_target_pairs={{0,1},{1,0},{2,3},{3,2},{4,5},{5,4},{6,7},{7,6},{8,9},{9,8},{10,11... | collective-permute-start | bytes 393224 | tf_op jit(solution)/shard_map/ppermute | solution.py:405
  109.0 1.2 collective-permute-start.7
  110.2 5.0 %collective-permute-start.9 = (f32[8,128]{1,0:T(8,128)S(1)}, f32[8,128]{1,0:T(8,128)S(1)}, u32[]{:S(2)}, u32[]{:S(2)}) collective-permute-start(f32[8,128]{1,0:T(8,128)S(1)} %chip_power.4.refs_5_.refs_2_), channel_id=1, source_target_pairs={{2,0},{4,2},{6,4},{8,6},{10,8},{12,10},{14,12},{16,14},{18,16},{20... | collective-permute-start | bytes 12296 | tf_op jit(solution)/shard_map/ppermute | solution.py:382
  111.1 7.9 %collective-permute-start.8 = (f32[8,128]{1,0:T(8,128)S(1)}, f32[8,128]{1,0:T(8,128)S(1)}, u32[]{:S(2)}, u32[]{:S(2)}) collective-permute-start(f32[8,128]{1,0:T(8,128)S(1)} %chip_power.4.refs_5_.refs_2_), channel_id=1, source_target_pairs={{0,2},{2,4},{4,6},{6,8},{8,10},{10,12},{12,14},{14,16},{16,18},{18... | collective-permute-start | bytes 12296 | tf_op jit(solution)/shard_map/ppermute | solution.py:382
  119.0 2.8 %collective-permute-start.10 = (bf16[192,512]{1,0:T(8,128)(2,1)S(1)}, bf16[192,512]{1,0:T(8,128)(2,1)S(1)}, u32[]{:S(2)}, u32[]{:S(2)}) collective-permute-start(bf16[192,512]{1,0:T(8,128)(2,1)S(1)} %get-tuple-element.53), channel_id=1, source_target_pairs={{0,1},{1,0},{2,3},{3,2},{4,5},{5,4},{6,7},{7,6},{8,9},{9,8},{10,11... | collective-permute-start | bytes 589832 | tf_op jit(solution)/shard_map/ppermute | solution.py:416
  153.0 4.9 %collective-permute-start.11 = (bf16[256,512]{1,0:T(8,128)(2,1)S(1)}, bf16[256,512]{1,0:T(8,128)(2,1)S(1)}, u32[]{:S(2)}, u32[]{:S(2)}) collective-permute-start(bf16[256,512]{1,0:T(8,128)(2,1)S(1)} %bitcast.28), channel_id=1, source_target_pairs={{0,1},{1,0},{2,3},{3,2},{4,5},{5,4},{6,7},{7,6},{8,9},{9,8},{10,11... | collective-permute-start | bytes 786440 | tf_op jit(solution)/shard_map/ppermute | solution.py:405
  160.4 1.2 collective-permute-start.12
  161.7 2.5 %collective-permute-start.14 = (f32[8,128]{1,0:T(8,128)S(1)}, f32[8,128]{1,0:T(8,128)S(1)}, u32[]{:S(2)}, u32[]{:S(2)}) collective-permute-start(f32[8,128]{1,0:T(8,128)S(1)} %chip_power.5.refs_2_), channel_id=1, source_target_pairs={{2,0},{4,2},{6,4},{8,6},{10,8},{12,10},{14,12},{16,14},{18,16},{20... | collective-permute-start | bytes 12296 | tf_op jit(solution)/shard_map/ppermute | solution.py:382
  162.2 7.9 %collective-permute-start.13 = (f32[8,128]{1,0:T(8,128)S(1)}, f32[8,128]{1,0:T(8,128)S(1)}, u32[]{:S(2)}, u32[]{:S(2)}) collective-permute-start(f32[8,128]{1,0:T(8,128)S(1)} %chip_power.5.refs_2_), channel_id=1, source_target_pairs={{0,2},{2,4},{4,6},{6,8},{8,10},{10,12},{12,14},{14,16},{16,18},{18... | collective-permute-start | bytes 12296 | tf_op jit(solution)/shard_map/ppermute | solution.py:382

commit v5 on v4

v5 whole, which is shorter than its diff:
```python
import math

import jax
import jax.numpy as jnp
import ml_dtypes
import numpy as np
from jax import lax
from jax.experimental import pallas as pl
from jax.experimental.pallas import tpu as pltpu
from jax.sharding import Mesh
from jax.sharding import PartitionSpec as P

K = 64
GROUP = 2048
ITERS = 3
LANES = 128
BLOCK = 512
step_size = 0.5
shrink_one = 0.05
group_weight = 0.03
epsilon = 1e-06

F32 = jnp.float32
BF16 = jnp.bfloat16
HIGHEST = lax.Precision.HIGHEST
PARAMS = pltpu.CompilerParams(vmem_limit_bytes=16 * 1024 * 1024)
AXES = {"x": 4, "z": 8, "y": 4}
SRC = ("x", "z", "y")
PLANE = ("x", "y")
PLANES = ("frm", "x", "y")


def windowed_cosines():
    t = np.arange(K)[:, None] + 0.5
    k = np.arange(K)[None, :] + 0.5
    wave = np.sin(np.pi * t / K) * np.sqrt(2.0 / K) * np.cos(np.pi * k * t / K)
    high = wave.astype(ml_dtypes.bfloat16)
    low = (wave - high.astype(np.float64)).astype(ml_dtypes.bfloat16)
    return np.stack([high, low, high.T, low.T])


def split(x):
    high = x.astype(BF16)
    return high, (x - high.astype(F32)).astype(BF16)


def dot(a, b):
    return jnp.dot(a, b, preferred_element_type=F32)


def dot_t(a, b):
    return lax.dot_general(a, b, (((1,), (1,)), ((), ())), preferred_element_type=F32)


def to_samples(atoms_ref, sums):
    high, low = split(sums)
    return dot(atoms_ref[0], high) + dot(atoms_ref[0], low) + dot(atoms_ref[1], high)


def group_scale(power, tau):
    return jnp.maximum(0.0, 1.0 - tau / jnp.sqrt(power + epsilon))


def scales_of(powers, tau):
    mine, pair, before, before_pair, after, after_pair = (ref[...] for ref in powers)
    chip = mine + pair
    return (
        group_scale(chip[0:1] + (before + before_pair)[2:3], tau),
        group_scale(chip[1:2], tau),
        group_scale(chip[2:3] + (after + after_pair)[0:1], tau),
    )


def first_kernel(
    where_ref, offsets_hbm, wave_hbm, group_hbm, depth_hbm, measured_hbm, coef_hbm, lead_hbm,
    table_ref, table_t_ref, out_ref, marks_ref, rows_ref, depth_ref, coef_ref, lead_ref,
    offsets_ref, wave_ref, group_ref, measured_ref, acc_ref, coef_sem, lead_sem, small_sem,
):
    total = table_ref.shape[2]
    sources = lead_ref.shape[1]
    blocks = lead_sem.shape[0]
    block = sources // blocks
    pairs = (
        (offsets_hbm, offsets_ref), (wave_hbm, wave_ref), (group_hbm, group_ref), (measured_hbm, measured_ref),
        (depth_hbm, depth_ref),
    )
    small = [pltpu.make_async_copy(a, b, small_sem.at[n]) for n, (a, b) in enumerate(pairs)]
    for load in small:
        load.start()
    loads = []
    for j in range(blocks):
        cols = slice(j * block, (j + 1) * block)
        loads.append(
            (
                pltpu.make_async_copy(lead_hbm.at[:, cols], lead_ref.at[:, cols], lead_sem.at[j]),
                pltpu.make_async_copy(coef_hbm.at[:, cols], coef_ref.at[:, cols], coef_sem.at[j]),
            )
        )
        for load in loads[-1]:
            load.start()
    for load in small:
        load.wait()

    groups = group_ref[...]
    marks_ref[0] = jnp.sum((groups == groups[0:1, 0:1]).astype(jnp.int32))
    marks_ref[1] = where_ref[1]
    marks_ref[2] = where_ref[0]
    for t in range(measured_ref.shape[0] // LANES):
        lanes = slice(t * LANES, (t + 1) * LANES)
        rows_ref[:, lanes] = measured_ref[lanes, :].T
    for f in range(offsets_ref.shape[0]):
        rows = slice(f * K, (f + 1) * K)
        for axis in range(2):
            shape = (total, K) if axis == 0 else (K, total)
            sample = lax.broadcasted_iota(jnp.int32, shape, axis)
            position = lax.broadcasted_iota(jnp.int32, shape, 1 - axis)
            delay = lax.rem(sample - offsets_ref[f] + total, total)
            placing = (delay == position).astype(F32).astype(BF16)
            for h in range(2):
                if axis == 0:
                    table_t_ref[h, :, rows] = dot(placing, wave_ref[h]).astype(BF16)
                else:
                    table_ref[h, rows, :] = dot(wave_ref[2 + h], placing).astype(BF16)

    for j in range(blocks):
        for load in loads[j]:
            load.wait()
        cols = slice(j * block, (j + 1) * block)
        part = dot_t((coef_ref[:, cols] * depth_ref[:, cols]).astype(BF16), lead_ref[:, cols])
        if j == 0:
            acc_ref[...] = part
        else:
            acc_ref[...] += part
    out_ref[...] = to_samples(table_t_ref, acc_ref[...]).astype(BF16)


def slabs(x):
    return [x[i : i + 8] for i in range(0, x.shape[0], 8)]


def step_kernel(
    marks_ref, got_ref, *rest, first, last, block
):
    if last:
        other_ref, *rest = rest
    table_ref, depth_ref, state_ref, lead_ref, *rest = rest
    if not first:
        scale_ref, *rest = rest
    new_ref, power_ref, turned_ref, *rest = rest
    sources = state_ref.shape[1]
    if last:
        (samples_ref,) = rest
        own = samples_ref.shape[0] // 2
        for ref, core in ((got_ref, marks_ref[2]), (other_ref, 1 - marks_ref[2])):
            at = pl.ds(pl.multiple_of(core * own, own), own)
            samples_ref[at, :] = jnp.concatenate(slabs(ref[...].astype(F32))[::2], axis=0).astype(BF16)
    else:
        samples_ref = got_ref
    turned = dot(table_ref[0], samples_ref[...]) + dot(table_ref[1], samples_ref[...])
    turned_ref[...] = turned.astype(BF16)

    start = marks_ref[0]
    bounds = (start, start + GROUP)
    scales = None if first else [scale_ref[g : g + 1, 0:1] for g in range(3)]
    sums = [jnp.zeros((1, block), F32) for _ in range(4)]
    for j in range(sources // block):
        cols = slice(j * block, (j + 1) * block)
        half = j * block // GROUP
        gradient = dot(turned_ref[...], lead_ref[:, cols])
        source = j * block + lax.broadcasted_iota(jnp.int32, (1, block), 1)
        before = source < bounds[half]
        state = state_ref[:, cols]
        if not first:
            state = state * jnp.where(before, scales[half], scales[half + 1])
        moved = state + (step_size * depth_ref[:, cols]) * gradient
        shrunk = moved - jnp.clip(moved, -shrink_one, shrink_one)
        new_ref[:, cols] = shrunk
        squares = jnp.sum(shrunk * shrunk, axis=0, keepdims=True)
        sums[2 * half] += jnp.where(before, squares, 0.0)
        sums[2 * half + 1] += jnp.where(before, 0.0, squares)
    power_ref[...] = jnp.zeros_like(power_ref)
    for g, total in enumerate((sums[0], sums[1] + sums[2], sums[3])):
        power_ref[g : g + 1, :] = jnp.broadcast_to(jnp.sum(total, axis=1, keepdims=True), (1, LANES))


def forward_kernel(
    marks_ref, state_ref, depth_ref, lead_ref, table_t_ref, power_ref, pair_ref, out_ref, weighted_ref, *,
    block, tau,
):
    coefs, sources = state_ref.shape
    total = out_ref.shape[0] // 3
    start = marks_ref[0]
    bounds = (start, start + GROUP)
    none = jnp.zeros((), BF16)
    for j in range(sources // block):
        cols = slice(j * block, (j + 1) * block)
        half = j * block // GROUP
        before = j * block + lax.broadcasted_iota(jnp.int32, (1, block), 1) < bounds[half]
        weighted = (state_ref[:, cols] * depth_ref[:, cols]).astype(BF16)
        inner = slice(j * block - half * GROUP, (j + 1) * block - half * GROUP)
        weighted_ref[half, :coefs, inner] = jnp.where(before, weighted, none)
        weighted_ref[half, coefs:, inner] = jnp.where(before, none, weighted)
    halves = [dot_t(weighted_ref[h], lead_ref[:, h * GROUP : (h + 1) * GROUP]) for h in range(2)]
    middle = group_scale(power_ref[1:2, 0:1] + pair_ref[1:2, 0:1], tau) * (halves[0][coefs:] + halves[1][:coefs])
    parts = (halves[0][:coefs], middle, halves[1][coefs:])
    for g in range(3):
        out_ref[g * total : (g + 1) * total, :] = to_samples(table_t_ref, parts[g])


def fold_kernel(parts_ref, *rest, tau):
    *powers, out_ref, scale_ref = rest
    total = out_ref.shape[0]
    scale_ref[...] = jnp.zeros_like(scale_ref)
    scales = scales_of(powers, tau)
    for g, scale in enumerate(scales):
        scale_ref[g : g + 1, :] = scale
    first, middle, last = (parts_ref[g * total : (g + 1) * total, :] for g in range(3))
    out_ref[...] = (scales[0][:, 0:1] * first + middle + scales[2][:, 0:1] * last).astype(BF16)


def plane_kernel(got_ref, out_ref):
    total = sum(slabs(got_ref[...].astype(F32)))
    out_ref[...] = jnp.concatenate([total] * (out_ref.shape[0] // 8), axis=0)


def owner_kernel(marks_ref, got_ref, measured_ref, out_ref, *, last):
    at = pl.ds(pl.multiple_of(marks_ref[1] * 8, 8), 8)
    row = measured_ref[at, :] - sum(slabs(got_ref[...]))
    if last:
        high = row.astype(BF16).astype(F32)
        row = jnp.concatenate([high, row - high], axis=0)
    out_ref[...] = jnp.concatenate([row] * (out_ref.shape[0] // row.shape[0]), axis=0).astype(BF16)


def residual_kernel(own_ref, out_ref):
    pieces = slabs(own_ref[...].astype(F32))
    rows = jnp.concatenate([high + low for high, low in zip(pieces[::2], pieces[1::2])], axis=0)
    for t in range(out_ref.shape[0] // LANES):
        lanes = slice(t * LANES, (t + 1) * LANES)
        out_ref[lanes, :] = rows[:, lanes].T


def estimate_kernel(marks_ref, state_ref, *rest, tau, middle):
    if middle:
        power_ref, pair_ref, out_hbm, scaled_ref, sem = rest
        scales = [None, group_scale(power_ref[1:2, 0:1] + pair_ref[1:2, 0:1], tau), None]
    else:
        *powers, _, out_hbm, scaled_ref, sem = rest
        scales = [scale[:, 0:1] for scale in scales_of(powers, tau)]
    blocks, _, block = scaled_ref.shape
    start = marks_ref[0]
    bounds = (start, start + GROUP)
    wanted, stores = [], []
    for j in range(blocks):
        cols = slice(j * block, (j + 1) * block)
        half = j * block // GROUP
        inside = bounds[0] <= j * block if half == 0 else (j + 1) * block <= bounds[1]
        wanted.append(inside if middle else jnp.logical_not(inside))
        stores.append(pltpu.make_async_copy(scaled_ref.at[j], out_hbm.at[:, cols], sem.at[j]))

        @pl.when(wanted[j])
        def _():
            if middle:
                scale = scales[1]
            else:
                before = j * block + lax.broadcasted_iota(jnp.int32, (1, block), 1) < bounds[half]
                scale = jnp.where(before, scales[half], scales[half + 1])
            scaled_ref[j] = state_ref[:, cols] * scale
            stores[j].start()

    for j in range(blocks):
        pl.when(wanted[j])(stores[j].wait)


SMEM = pl.BlockSpec(memory_space=pltpu.SMEM)
VMEM = pl.BlockSpec(memory_space=pltpu.VMEM)
HBM = pl.BlockSpec(memory_space=pltpu.HBM)


def struct(dtype, *shape):
    return jax.ShapeDtypeStruct(shape, dtype)


def call(kernel, name, args, outs, *, ins=None, out_specs=None, scratch=(), cost=None, alias=None):
    return pl.pallas_call(
        kernel, in_specs=ins or [VMEM] * len(args), out_specs=out_specs or [VMEM] * len(outs), out_shape=outs,
        scratch_shapes=list(scratch), compiler_params=PARAMS, name=name, cost_estimate=cost,
        input_output_aliases=alias or {},
    )(*args)


def stay(x):
    return pltpu.with_memory_space_constraint(x, pltpu.HBM)


def first_call(where, offsets, groups, depth, measured, state, lead):
    coefs, sources = state.shape
    sensors, own = measured.shape
    total = 2 * own
    dma = pltpu.SemaphoreType.DMA((sources // BLOCK,))
    inputs = (offsets, jnp.asarray(windowed_cosines()), groups, depth, measured, state, lead)
    return call(
        first_kernel,
        "first_forward",
        [where] + [stay(x) for x in inputs],
        [
            struct(BF16, 2, coefs, total),
            struct(BF16, 2, total, coefs),
            struct(BF16, total, sensors),
            struct(jnp.int32, 3),
            struct(F32, own, sensors),
            struct(F32, 1, sources),
            struct(F32, coefs, sources),
            struct(BF16, sensors, sources),
        ],
        ins=[SMEM] + [HBM] * len(inputs),
        out_specs=[VMEM, VMEM, VMEM, SMEM, VMEM, VMEM, VMEM, VMEM],
        scratch=[
            pltpu.SMEM(offsets.shape, jnp.int32),
            pltpu.VMEM((4, K, K), BF16),
            pltpu.VMEM((1, sources), jnp.int32),
            pltpu.VMEM((sensors, own), F32),
            pltpu.VMEM((coefs, sensors), F32),
            dma,
            dma,
            pltpu.SemaphoreType.DMA((5,)),
        ],
    )


def step_call(marks, got, others, table, scale, depth, state, lead):
    coefs, sources = state.shape
    sensors = lead.shape[0]
    first, last = scale is None, others is not None
    args = [marks, got] + ([others] if last else []) + [table, depth, state, lead] + ([] if first else [scale])
    return call(
        lambda *refs: step_kernel(*refs, first=first, last=last, block=BLOCK),
        "step",
        args,
        [struct(F32, coefs, sources), struct(F32, 8, LANES)],
        ins=[SMEM] + [VMEM] * (len(args) - 1),
        scratch=[pltpu.VMEM((coefs, sensors), BF16)] + ([pltpu.VMEM((table.shape[2], sensors), BF16)] if last else []),
    )


def forward_call(marks, state, depth, lead, table_t, power, pair, tau):
    coefs, sources = state.shape
    sensors = lead.shape[0]
    return call(
        lambda *refs: forward_kernel(*refs, block=BLOCK, tau=tau),
        "forward",
        [marks, state, depth, lead, table_t, power, pair],
        [struct(F32, 3 * table_t.shape[1], sensors)],
        ins=[SMEM] + [VMEM] * 6,
        scratch=[pltpu.VMEM((2, 2 * coefs, GROUP), BF16)],
        cost=pl.CostEstimate(flops=4 * coefs * sources * sensors, bytes_accessed=8 << 20, transcendentals=0),
    )[0]


def estimate_call(marks, state, powers, tau, so_far=None):
    coefs, sources = state.shape
    blocks = sources // BLOCK
    middle = so_far is None
    args = [marks, state, *powers] + ([] if middle else [so_far])
    return call(
        lambda *refs: estimate_kernel(*refs, tau=tau, middle=middle),
        "estimate",
        args,
        [struct(F32, coefs, sources)],
        ins=[SMEM] + [VMEM] * (1 + len(powers)) + ([] if middle else [HBM]),
        out_specs=[HBM],
        scratch=[pltpu.VMEM((blocks, coefs, BLOCK), F32), pltpu.SemaphoreType.DMA((blocks,))],
        alias={} if middle else {len(args) - 1: 0},
        cost=pl.CostEstimate(flops=coefs * sources, bytes_accessed=4 << 20, transcendentals=0),
    )[0]


def shards(measured, lead_field, depth, coefficients, offsets, group_ids):
    sensors, own = measured.shape
    sources = lead_field.shape[1]
    frames = coefficients.shape[1]
    frm_count = lax.axis_size("frm")
    src_count = math.prod(AXES.values())
    total = own * frm_count
    coefs = frames * K
    tau = group_weight * math.sqrt(GROUP * frames * frm_count * K)
    where = jnp.stack([lax.axis_index("frm"), lax.axis_index(PLANE)])

    def exchange(rows, axes):
        return lax.all_to_all(rows, axes, 0, 0, tiled=True)

    def move(x, chips, cores):
        route = []
        for chip in range(src_count):
            for core in range(frm_count):
                to = (chip + chips) % src_count * frm_count + (core + cores) % frm_count
                route.append((chip * frm_count + core, to))
        return lax.ppermute(x, (*SRC, "frm"), route)

    state = coefficients.transpose(1, 2, 0).reshape(coefs, sources)
    table, table_t, folded, marks, rows, depth_row, state, lead = first_call(
        where, offsets, group_ids.reshape(1, sources), depth.reshape(1, sources), measured, state, lead_field
    )
    scale = None
    for iteration in range(ITERS):
        last = iteration == ITERS - 1
        plane = call(
            plane_kernel, "plane_sum", [exchange(folded, PLANES)], [struct(F32, 8 * AXES["z"], sensors)]
        )[0]
        slab = call(
            lambda *refs, last=last: owner_kernel(*refs, last=last),
            "owner",
            [marks, exchange(plane, "z"), rows],
            [struct(BF16, total, sensors)],
            ins=[SMEM, VMEM, VMEM],
        )[0]
        got = exchange(slab, PLANE if last else PLANES)
        others = move(got, 0, 1) if last else None
        state, power = step_call(marks, got, others, table, scale, depth_row, state, lead)
        pair = move(power, 0, 1)
        powers = [power, pair, move(power, 1, 0), move(power, 1, 1), move(power, -1, 0), move(power, -1, 1)]
        if not last:
            parts = forward_call(marks, state, depth_row, lead, table_t, power, pair, tau)
            folded, scale = call(
                lambda *refs: fold_kernel(*refs, tau=tau),
                "fold",
                [parts, *powers],
                [struct(BF16, total, sensors), struct(F32, 8, LANES)],
            )

    residual = call(residual_kernel, "residual", [got], [struct(F32, sensors, own)])[0]
    estimate = estimate_call(marks, state, powers[:2], tau)
    estimate = estimate_call(marks, state, powers, tau, estimate)
    return (estimate.reshape(frames, K, sources).transpose(2, 0, 1), residual)


def solution(mesh):
    fine = Mesh(mesh.devices.reshape(*AXES.values(), mesh.shape["frm"]), (*AXES, "frm"))
    return jax.shard_map(
        shards,
        mesh=fine,
        in_specs=(
            P(None, "frm"),
            P(None, SRC),
            P(SRC),
            P(SRC, "frm", None),
            P("frm"),
            P(SRC),
        ),
        out_specs=(P(SRC, "frm", None), P(None, "frm")),
        check_vma=False,
    )
```

time: 173 us -> 174 us (level)
  blocking collectives: 97.7 us -> 118 us
  waiting for transfers between devices: 22.8 us -> 11.4 us
  starting transfers between devices: 24.3 us -> 15.3 us
    all_to_all x9, blocking collectives: 97.7 us -> 118 us  [exchange(): return lax.all_to_all(rows, axes, 0, 0, tiled=True)]
    ppermute x15 -> x16, waiting for transfers between devices: 22.8 us -> 11.4 us  [move(): return lax.ppermute(x, (*SRC, 'frm'), route)]
    ppermute x15 -> x16, starting transfers between devices: 24.3 us -> 15.3 us  [move(): return lax.ppermute(x, (*SRC, 'frm'), route)]
    pallas_call x20 -> x17, Pallas kernels: 27.2 us -> 28.3 us  [call(): pl.pallas_call(kernel, in_specs=ins or [VMEM] * len(args), out_specs=out_...]
  transfers between devices with their start and end apart: 15 -> 16, of which waited for: 13 -> 7; matrix products, arithmetic and copies ran while one was open for 0% -> 0% of each run, Pallas kernels for 5% -> 6%
where the time goes in v5:
time: 174 us
  blocking collectives  118 us (68%)
  Pallas kernels  28.3 us (16%)
  starting transfers between devices  15.3 us (9%)
  waiting for transfers between devices  11.4 us (7%)
    all_to_all x9, blocking collectives, exchange(): return lax.all_to_all(rows, axes, 0, 0, tiled=True)  118 us
    pallas_call x17, Pallas kernels, call(): pl.pallas_call(kernel, in_specs=ins or [VMEM] * len(args), out_specs=out_...  28.3 us
    ppermute x16, starting transfers between devices, move(): return lax.ppermute(x, (*SRC, 'frm'), route)  15.3 us
    ppermute x16, waiting for transfers between devices, move(): return lax.ppermute(x, (*SRC, 'frm'), route)  11.4 us
  transfers between devices with their start and end apart: 16, of which 7 were waited for; matrix products, arithmetic and copies ran while one was open for 0% of the time, Pallas kernels for 6%

profile of v5, /device:TPU:1, one launch (start us, length us, event | category | flops | bytes accessed | tf_op | source)
XLA Modules:
  0.0 173.9 jit_solution(8434308521288201708)
XLA Ops:
  0.6 0.1 pad_add_fusion.where_ref
  0.7 6.6 %first_forward.1 = (bf16[2,256,256]{2,1,0:T(8,128)(2,1)S(1)}, bf16[2,256,256]{2,1,0:T(8,128)(2,1)S(1)}, bf16[256,512]{1,0:T(8,128)(2,1)S(1)}, s32[3]{0:T(128)S(1...) custom-call(s32[2]{0:T(128)S(1)} %pad_add_fusion.where_ref, ...), custom_call_target="tpu_custom_call" | custom-call | tf_op jit(solution)/shard_map/first_forward/pallas_call | solution.py:285
  7.3 17.2 %all_to_all.99 = bf16[32,8,512]{2,1,0:T(8,128)(2,1)S(1)} all-to-all(bf16[32,8,512]{2,1,0:T(8,128)(2,1)S(1)} %bitcast.45), channel_id=1, replica_groups=mesh['x'=4,'z'=8,'y'=4,'frm'=2] {'frm','x','y'}, dimensions={0} | all-to-all | bytes 524288 | tf_op jit(solution)/shard_map/all_to_all | solution.py:390
  24.5 0.1 plane_sum.3
  24.6 15.8 %all_to_all.100 = f32[8,8,512]{2,1,0:T(8,128)S(1)} all-to-all(f32[8,8,512]{2,1,0:T(8,128)S(1)} %bitcast.39), channel_id=1, replica_groups=mesh['x'=4,'z'=8,'y'=4,'frm'=2] {'z'}, dimensions={0} | all-to-all | bytes 262144 | tf_op jit(solution)/shard_map/all_to_all | solution.py:390
  40.3 0.6 owner.3
  40.9 14.3 %all_to_all.101 = bf16[32,8,512]{2,1,0:T(8,128)(2,1)S(1)} all-to-all(bf16[32,8,512]{2,1,0:T(8,128)(2,1)S(1)} %bitcast.35), channel_id=1, replica_groups=mesh['x'=4,'z'=8,'y'=4,'frm'=2] {'frm','x','y'}, dimensions={0} | all-to-all | bytes 524288 | tf_op jit(solution)/shard_map/all_to_all | solution.py:390
  55.2 2.4 %step.3 = (f32[256,4096]{1,0:T(8,128)S(1)}, f32[8,128]{1,0:T(8,128)S(1)}) custom-call(s32[3]{0:T(128)S(1)} %get-tuple-element.20.refs_0_, bf16[256,512]{1,0:T(8,128)(2,1)S(1)} %bitcast.32, bf16[2,256,256]{2,1,0:T(8,128)(2,1)S(1)} %get-tuple-element.23.refs_2_.refs_3_, f32[1,4096]{1,0:T(1,128)S(1)} %get-tuple-element.24.refs_3_.refs_2_.refs_4_, ...), custom_call_target="tpu_custom_call" | custom-call | tf_op jit(solution)/shard_map/step/pallas_call | solution.py:285
  57.7 0.7 collective-permute-start
  58.3 0.5 collective-permute-start.4
  58.9 0.1 collective-permute-start.3
  58.9 2.0 %collective-permute-start.2 = (f32[8,128]{1,0:T(8,128)S(1)}, f32[8,128]{1,0:T(8,128)S(1)}, u32[]{:S(2)}, u32[]{:S(2)}) collective-permute-start(f32[8,128]{1,0:T(8,128)S(1)} %get-tuple-element.29.refs_5_.refs_1_), channel_id=1, source_target_pairs={{0,3},{1,2},{2,5},{3,4},{4,7},{5,6},{6,9},{7,8},{8,11},{9,10},{10,... | collective-permute-start | bytes 12296 | tf_op jit(solution)/shard_map/ppermute | solution.py:398
  60.9 0.9 collective-permute-start.1
  61.9 3.5 %forward.2.refs_0_ = f32[768,512]{1,0:T(8,128)S(1)} custom-call(s32[3]{0:T(128)S(1)} %get-tuple-element.20.refs_0_, f32[256,4096]{1,0:T(8,128)S(1)} %get-tuple-element.27.refs_1_.refs_4_, f32[1,4096]{1,0:T(1,128)S(1)} %get-tuple-element.24.refs_3_.refs_2_.refs_4_, bf16[512,4096]{1,0:T(8,128)(2,1)S(1)} %get-tuple-element.26.refs_5_.refs_3_.refs_6_, ...), custom_call_target="tpu_custom_call" | custom-call | flops 2147483648 | bytes 8388608 | tf_op jit(solution)/shard_map/forward/pallas_call | solution.py:285
  65.4 2.3 %collective-permute-done.2.refs_4_ = f32[8,128]{1,0:T(8,128)S(1)} collective-permute-done((f32[8,128]{1,0:T(8,128)S(1)}, f32[8,128]{1,0:T(8,128)S(1)}, u32[]{:S(2)}, u32[]{:S(2)}) %collective-permute-start.2) | collective-permute-done | bytes 4128 | tf_op jit(solution)/shard_map/ppermute | solution.py:398
  67.7 1.1 collective-permute-done.1.refs_3_
  68.8 0.2 fold.2
  69.0 12.5 %all_to_all.102 = bf16[32,8,512]{2,1,0:T(8,128)(2,1)S(1)} all-to-all(bf16[32,8,512]{2,1,0:T(8,128)(2,1)S(1)} %bitcast.46), channel_id=1, replica_groups=mesh['x'=4,'z'=8,'y'=4,'frm'=2] {'frm','x','y'}, dimensions={0} | all-to-all | bytes 524288 | tf_op jit(solution)/shard_map/all_to_all | solution.py:390
  81.6 0.1 plane_sum.4
  81.6 10.2 %all_to_all.103 = f32[8,8,512]{2,1,0:T(8,128)S(1)} all-to-all(f32[8,8,512]{2,1,0:T(8,128)S(1)} %bitcast.40), channel_id=1, replica_groups=mesh['x'=4,'z'=8,'y'=4,'frm'=2] {'z'}, dimensions={0} | all-to-all | bytes 262144 | tf_op jit(solution)/shard_map/all_to_all | solution.py:390
  91.9 0.6 owner.4
  92.4 14.2 %all_to_all.104 = bf16[32,8,512]{2,1,0:T(8,128)(2,1)S(1)} all-to-all(bf16[32,8,512]{2,1,0:T(8,128)(2,1)S(1)} %bitcast.37), channel_id=1, replica_groups=mesh['x'=4,'z'=8,'y'=4,'frm'=2] {'frm','x','y'}, dimensions={0} | all-to-all | bytes 524288 | tf_op jit(solution)/shard_map/all_to_all | solution.py:390
  106.7 2.5 %step.4 = (f32[256,4096]{1,0:T(8,128)S(1)}, f32[8,128]{1,0:T(8,128)S(1)}) custom-call(s32[3]{0:T(128)S(1)} %get-tuple-element.20.refs_0_, bf16[256,512]{1,0:T(8,128)(2,1)S(1)} %bitcast.31, bf16[2,256,256]{2,1,0:T(8,128)(2,1)S(1)} %get-tuple-element.23.refs_2_.refs_3_, f32[1,4096]{1,0:T(1,128)S(1)} %get-tuple-element.24.refs_3_.refs_2_.refs_4_, ...), custom_call_target="tpu_custom_call" | custom-call | tf_op jit(solution)/shard_map/step/pallas_call | solution.py:285
  109.2 0.7 collective-permute-start.5
  109.9 0.3 collective-permute-start.9
  110.2 2.0 %collective-permute-start.7 = (f32[8,128]{1,0:T(8,128)S(1)}, f32[8,128]{1,0:T(8,128)S(1)}, u32[]{:S(2)}, u32[]{:S(2)}) collective-permute-start(f32[8,128]{1,0:T(8,128)S(1)} %get-tuple-element.33.refs_5_.refs_1_), channel_id=1, source_target_pairs={{0,3},{1,2},{2,5},{3,4},{4,7},{5,6},{6,9},{7,8},{8,11},{9,10},{10,... | collective-permute-start | bytes 12296 | tf_op jit(solution)/shard_map/ppermute | solution.py:398
  112.1 1.2 collective-permute-start.6
  113.4 3.5 %forward.3.refs_0_ = f32[768,512]{1,0:T(8,128)S(1)} custom-call(s32[3]{0:T(128)S(1)} %get-tuple-element.20.refs_0_, f32[256,4096]{1,0:T(8,128)S(1)} %get-tuple-element.32.refs_1_.refs_5_, f32[1,4096]{1,0:T(1,128)S(1)} %get-tuple-element.24.refs_3_.refs_2_.refs_4_, bf16[512,4096]{1,0:T(8,128)(2,1)S(1)} %get-tuple-element.26.refs_5_.refs_3_.refs_6_, ...), custom_call_target="tpu_custom_call" | custom-call | flops 2147483648 | bytes 8388608 | tf_op jit(solution)/shard_map/forward/pallas_call | solution.py:285
  116.9 2.0 %collective-permute-done.7.refs_4_ = f32[8,128]{1,0:T(8,128)S(1)} collective-permute-done((f32[8,128]{1,0:T(8,128)S(1)}, f32[8,128]{1,0:T(8,128)S(1)}, u32[]{:S(2)}, u32[]{:S(2)}) %collective-permute-start.7) | collective-permute-done | bytes 4128 | tf_op jit(solution)/shard_map/ppermute | solution.py:398
  118.9 1.1 collective-permute-done.6.refs_3_
  120.0 0.2 fold.3
  120.3 12.6 %all_to_all.105 = bf16[32,8,512]{2,1,0:T(8,128)(2,1)S(1)} all-to-all(bf16[32,8,512]{2,1,0:T(8,128)(2,1)S(1)} %bitcast.47), channel_id=1, replica_groups=mesh['x'=4,'z'=8,'y'=4,'frm'=2] {'frm','x','y'}, dimensions={0} | all-to-all | bytes 524288 | tf_op jit(solution)/shard_map/all_to_all | solution.py:390
  132.8 0.1 plane_sum.5
  132.9 10.2 %all_to_all.106 = f32[8,8,512]{2,1,0:T(8,128)S(1)} all-to-all(f32[8,8,512]{2,1,0:T(8,128)S(1)} %bitcast.41), channel_id=1, replica_groups=mesh['x'=4,'z'=8,'y'=4,'frm'=2] {'z'}, dimensions={0} | all-to-all | bytes 262144 | tf_op jit(solution)/shard_map/all_to_all | solution.py:390
  143.1 0.6 owner.5
  143.7 10.8 %all_to_all.107 = bf16[16,16,512]{2,1,0:T(8,128)(2,1)S(1)} all-to-all(bf16[16,16,512]{2,1,0:T(8,128)(2,1)S(1)} %bitcast.33), channel_id=1, replica_groups=mesh['x'=4,'z'=8,'y'=4,'frm'=2] {'x','y'}, dimensions={0} | all-to-all | bytes 524288 | tf_op jit(solution)/shard_map/all_to_all | solution.py:390
  154.5 3.1 %collective-permute-start.10 = (bf16[256,512]{1,0:T(8,128)(2,1)S(1)}, bf16[256,512]{1,0:T(8,128)(2,1)S(1)}, u32[]{:S(2)}, u32[]{:S(2)}) collective-permute-start(bf16[256,512]{1,0:T(8,128)(2,1)S(1)} %bitcast.28), channel_id=1, source_target_pairs={{0,1},{1,0},{2,3},{3,2},{4,5},{5,4},{6,7},{7,6},{8,9},{9,8},{10,11... | collective-permute-start | bytes 786440 | tf_op jit(solution)/shard_map/ppermute | solution.py:398
  157.6 1.2 collective-permute-done.10.refs_2_
  158.7 2.5 %step.5 = (f32[256,4096]{1,0:T(8,128)S(1)}, f32[8,128]{1,0:T(8,128)S(1)}) custom-call(s32[3]{0:T(128)S(1)} %get-tuple-element.20.refs_0_, bf16[256,512]{1,0:T(8,128)(2,1)S(1)} %bitcast.29, bf16[256,512]{1,0:T(8,128)(2,1)S(1)} %collective-permute-done.10.refs_2_, bf16[2,256,256]{2,1,0:T(8,128)(2,1)S(1)} %get-tuple-element.23.refs_2_.refs_3_, ...), custom_call_target="tpu_custom_call" | custom-call | tf_op jit(solution)/shard_map/step/pallas_call | solution.py:285
  161.2 0.4 collective-permute-start.11
  161.6 0.9 collective-permute-start.14
  162.5 1.1 collective-permute-start.13
  163.7 1.5 collective-permute-start.12
  165.1 0.8 residual.1
  166.0 1.8 %estimate.2.refs_8_ = f32[256,4096]{1,0:T(8,128)} custom-call(s32[3]{0:T(128)S(1)} %get-tuple-element.20.refs_0_, f32[256,4096]{1,0:T(8,128)S(1)} %get-tuple-element.36.refs_1_, f32[8,128]{1,0:T(8,128)S(1)} %get-tuple-element.37.refs_2_, f32[8,128]{1,0:T(8,128)S(1)} %collective-permute-done.11.refs_3_), custom_call_target="tpu_custom_call" | custom-call | flops 1048576 | bytes 4194304 | tf_op jit(solution)/shard_map/estimate/pallas_call | solution.py:285
  167.8 3.2 %collective-permute-done.13.refs_5_ = f32[8,128]{1,0:T(8,128)S(1)} collective-permute-done((f32[8,128]{1,0:T(8,128)S(1)}, f32[8,128]{1,0:T(8,128)S(1)}, u32[]{:S(2)}, u32[]{:S(2)}) %collective-permute-start.13) | collective-permute-done | bytes 4128 | tf_op jit(solution)/shard_map/ppermute | solution.py:398
  171.1 0.5 collective-permute-done.12.refs_4_
  171.5 2.2 %estimate.3 = f32[256,4096]{1,0:T(8,128)} custom-call(s32[3]{0:T(128)S(1)} %get-tuple-element.20.refs_0_, f32[256,4096]{1,0:T(8,128)S(1)} %get-tuple-element.36.refs_1_, f32[8,128]{1,0:T(8,128)S(1)} %get-tuple-element.37.refs_2_, f32[8,128]{1,0:T(8,128)S(1)} %collective-permute-done.11.refs_3_, ...), custom_call_target="tpu_custom_call", output_to_operand_aliasing={{}: (8, {})} | custom-call | flops 1048576 | bytes 4194304 | tf_op jit(solution)/shard_map/estimate/pallas_call | solution.py:285
  (11 shorter events, 0.0 us)
Async XLA Ops:
  57.7 4.2 %collective-permute-start = (f32[8,128]{1,0:T(8,128)S(1)}, f32[8,128]{1,0:T(8,128)S(1)}, u32[]{:S(2)}, u32[]{:S(2)}) collective-permute-start(f32[8,128]{1,0:T(8,128)S(1)} %get-tuple-element.29.refs_5_.refs_1_), channel_id=1, source_target_pairs={{0,1},{1,0},{2,3},{3,2},{4,5},{5,4},{6,7},{7,6},{8,9},{9,8},{10,11... | collective-permute-start | bytes 12296 | tf_op jit(solution)/shard_map/ppermute | solution.py:398
  58.3 7.1 %collective-permute-start.4 = (f32[8,128]{1,0:T(8,128)S(1)}, f32[8,128]{1,0:T(8,128)S(1)}, u32[]{:S(2)}, u32[]{:S(2)}) collective-permute-start(f32[8,128]{1,0:T(8,128)S(1)} %get-tuple-element.29.refs_5_.refs_1_), channel_id=1, source_target_pairs={{0,255},{1,254},{2,1},{3,0},{4,3},{5,2},{6,5},{7,4},{8,7},{9,6},{1... | collective-permute-start | bytes 12296 | tf_op jit(solution)/shard_map/ppermute | solution.py:398
  58.9 6.5 %collective-permute-start.3 = (f32[8,128]{1,0:T(8,128)S(1)}, f32[8,128]{1,0:T(8,128)S(1)}, u32[]{:S(2)}, u32[]{:S(2)}) collective-permute-start(f32[8,128]{1,0:T(8,128)S(1)} %get-tuple-element.29.refs_5_.refs_1_), channel_id=1, source_target_pairs={{0,254},{1,255},{2,0},{3,1},{4,2},{5,3},{6,4},{7,5},{8,6},{9,7},{1... | collective-permute-start | bytes 12296 | tf_op jit(solution)/shard_map/ppermute | solution.py:398
  58.9 8.8 %collective-permute-start.2 = (f32[8,128]{1,0:T(8,128)S(1)}, f32[8,128]{1,0:T(8,128)S(1)}, u32[]{:S(2)}, u32[]{:S(2)}) collective-permute-start(f32[8,128]{1,0:T(8,128)S(1)} %get-tuple-element.29.refs_5_.refs_1_), channel_id=1, source_target_pairs={{0,3},{1,2},{2,5},{3,4},{4,7},{5,6},{6,9},{7,8},{8,11},{9,10},{10,... | collective-permute-start | bytes 12296 | tf_op jit(solution)/shard_map/ppermute | solution.py:398
  60.9 7.9 %collective-permute-start.1 = (f32[8,128]{1,0:T(8,128)S(1)}, f32[8,128]{1,0:T(8,128)S(1)}, u32[]{:S(2)}, u32[]{:S(2)}) collective-permute-start(f32[8,128]{1,0:T(8,128)S(1)} %get-tuple-element.29.refs_5_.refs_1_), channel_id=1, source_target_pairs={{0,2},{1,3},{2,4},{3,5},{4,6},{5,7},{6,8},{7,9},{8,10},{9,11},{10,... | collective-permute-start | bytes 12296 | tf_op jit(solution)/shard_map/ppermute | solution.py:398
  109.2 4.2 %collective-permute-start.5 = (f32[8,128]{1,0:T(8,128)S(1)}, f32[8,128]{1,0:T(8,128)S(1)}, u32[]{:S(2)}, u32[]{:S(2)}) collective-permute-start(f32[8,128]{1,0:T(8,128)S(1)} %get-tuple-element.33.refs_5_.refs_1_), channel_id=1, source_target_pairs={{0,1},{1,0},{2,3},{3,2},{4,5},{5,4},{6,7},{7,6},{8,9},{9,8},{10,11... | collective-permute-start | bytes 12296 | tf_op jit(solution)/shard_map/ppermute | solution.py:398
  109.9 7.1 %collective-permute-start.9 = (f32[8,128]{1,0:T(8,128)S(1)}, f32[8,128]{1,0:T(8,128)S(1)}, u32[]{:S(2)}, u32[]{:S(2)}) collective-permute-start(f32[8,128]{1,0:T(8,128)S(1)} %get-tuple-element.33.refs_5_.refs_1_), channel_id=1, source_target_pairs={{0,255},{1,254},{2,1},{3,0},{4,3},{5,2},{6,5},{7,4},{8,7},{9,6},{1... | collective-permute-start | bytes 12296 | tf_op jit(solution)/shard_map/ppermute | solution.py:398
  110.1 6.8 %collective-permute-start.8 = (f32[8,128]{1,0:T(8,128)S(1)}, f32[8,128]{1,0:T(8,128)S(1)}, u32[]{:S(2)}, u32[]{:S(2)}) collective-permute-start(f32[8,128]{1,0:T(8,128)S(1)} %get-tuple-element.33.refs_5_.refs_1_), channel_id=1, source_target_pairs={{0,254},{1,255},{2,0},{3,1},{4,2},{5,3},{6,4},{7,5},{8,6},{9,7},{1... | collective-permute-start | bytes 12296 | tf_op jit(solution)/shard_map/ppermute | solution.py:398
  110.2 8.8 %collective-permute-start.7 = (f32[8,128]{1,0:T(8,128)S(1)}, f32[8,128]{1,0:T(8,128)S(1)}, u32[]{:S(2)}, u32[]{:S(2)}) collective-permute-start(f32[8,128]{1,0:T(8,128)S(1)} %get-tuple-element.33.refs_5_.refs_1_), channel_id=1, source_target_pairs={{0,3},{1,2},{2,5},{3,4},{4,7},{5,6},{6,9},{7,8},{8,11},{9,10},{10,... | collective-permute-start | bytes 12296 | tf_op jit(solution)/shard_map/ppermute | solution.py:398
  112.1 7.9 %collective-permute-start.6 = (f32[8,128]{1,0:T(8,128)S(1)}, f32[8,128]{1,0:T(8,128)S(1)}, u32[]{:S(2)}, u32[]{:S(2)}) collective-permute-start(f32[8,128]{1,0:T(8,128)S(1)} %get-tuple-element.33.refs_5_.refs_1_), channel_id=1, source_target_pairs={{0,2},{1,3},{2,4},{3,5},{4,6},{5,7},{6,8},{7,9},{8,10},{9,11},{10,... | collective-permute-start | bytes 12296 | tf_op jit(solution)/shard_map/ppermute | solution.py:398
  154.5 4.2 %collective-permute-start.10 = (bf16[256,512]{1,0:T(8,128)(2,1)S(1)}, bf16[256,512]{1,0:T(8,128)(2,1)S(1)}, u32[]{:S(2)}, u32[]{:S(2)}) collective-permute-start(bf16[256,512]{1,0:T(8,128)(2,1)S(1)} %bitcast.28), channel_id=1, source_target_pairs={{0,1},{1,0},{2,3},{3,2},{4,5},{5,4},{6,7},{7,6},{8,9},{9,8},{10,11... | collective-permute-start | bytes 786440 | tf_op jit(solution)/shard_map/ppermute | solution.py:398
  161.2 4.7 %collective-permute-start.11 = (f32[8,128]{1,0:T(8,128)S(1)}, f32[8,128]{1,0:T(8,128)S(1)}, u32[]{:S(2)}, u32[]{:S(2)}) collective-permute-start(f32[8,128]{1,0:T(8,128)S(1)} %get-tuple-element.37.refs_2_), channel_id=1, source_target_pairs={{0,1},{1,0},{2,3},{3,2},{4,5},{5,4},{6,7},{7,6},{8,9},{9,8},{10,11... | collective-permute-start | bytes 12296 | tf_op jit(solution)/shard_map/ppermute | solution.py:398
  161.6 6.2 %collective-permute-start.15 = (f32[8,128]{1,0:T(8,128)S(1)}, f32[8,128]{1,0:T(8,128)S(1)}, u32[]{:S(2)}, u32[]{:S(2)}) collective-permute-start(f32[8,128]{1,0:T(8,128)S(1)} %get-tuple-element.37.refs_2_), channel_id=1, source_target_pairs={{0,255},{1,254},{2,1},{3,0},{4,3},{5,2},{6,5},{7,4},{8,7},{9,6},{1... | collective-permute-start | bytes 12296 | tf_op jit(solution)/shard_map/ppermute | solution.py:398
  161.6 6.2 %collective-permute-start.14 = (f32[8,128]{1,0:T(8,128)S(1)}, f32[8,128]{1,0:T(8,128)S(1)}, u32[]{:S(2)}, u32[]{:S(2)}) collective-permute-start(f32[8,128]{1,0:T(8,128)S(1)} %get-tuple-element.37.refs_2_), channel_id=1, source_target_pairs={{0,254},{1,255},{2,0},{3,1},{4,2},{5,3},{6,4},{7,5},{8,6},{9,7},{1... | collective-permute-start | bytes 12296 | tf_op jit(solution)/shard_map/ppermute | solution.py:398
  162.5 8.5 %collective-permute-start.13 = (f32[8,128]{1,0:T(8,128)S(1)}, f32[8,128]{1,0:T(8,128)S(1)}, u32[]{:S(2)}, u32[]{:S(2)}) collective-permute-start(f32[8,128]{1,0:T(8,128)S(1)} %get-tuple-element.37.refs_2_), channel_id=1, source_target_pairs={{0,3},{1,2},{2,5},{3,4},{4,7},{5,6},{6,9},{7,8},{8,11},{9,10},{10,... | collective-permute-start | bytes 12296 | tf_op jit(solution)/shard_map/ppermute | solution.py:398
  163.7 7.9 %collective-permute-start.12 = (f32[8,128]{1,0:T(8,128)S(1)}, f32[8,128]{1,0:T(8,128)S(1)}, u32[]{:S(2)}, u32[]{:S(2)}) collective-permute-start(f32[8,128]{1,0:T(8,128)S(1)} %get-tuple-element.37.refs_2_), channel_id=1, source_target_pairs={{0,2},{1,3},{2,4},{3,5},{4,6},{5,7},{6,8},{7,9},{8,10},{9,11},{10,... | collective-permute-start | bytes 12296 | tf_op jit(solution)/shard_map/ppermute | solution.py:398

commit v6 on v5

--- a/solution.py
+++ b/solution.py
@@ -62,7 +62,7 @@
 
 
 def scales_of(powers, tau):
-    mine, pair, before, before_pair, after, after_pair = (ref[...] for ref in powers)
+    mine, pair, after, after_pair, before, before_pair = (ref[...] for ref in powers)
     chip = mine + pair
     return (
         group_scale(chip[0:1] + (before + before_pair)[2:3], tau),
@@ -74,7 +74,7 @@
 def first_kernel(
     where_ref, offsets_hbm, wave_hbm, group_hbm, depth_hbm, measured_hbm, coef_hbm, lead_hbm,
     table_ref, table_t_ref, out_ref, marks_ref, rows_ref, depth_ref, coef_ref, lead_ref,
-    offsets_ref, wave_ref, group_ref, measured_ref, acc_ref, coef_sem, lead_sem, small_sem,
+    offsets_ref, wave_ref, group_ref, measured_ref, turned_ref, acc_ref, coef_sem, lead_sem, small_sem,
 ):
     total = table_ref.shape[2]
     sources = lead_ref.shape[1]
@@ -102,12 +102,14 @@
         load.wait()
 
     groups = group_ref[...]
-    marks_ref[0] = jnp.sum((groups == groups[0:1, 0:1]).astype(jnp.int32))
-    marks_ref[1] = where_ref[1]
-    marks_ref[2] = where_ref[0]
+    edge = jnp.sum((groups == groups[0:1, 0:1]).astype(jnp.int32), axis=1, keepdims=True)
+    marks_ref[0:1, :] = jnp.broadcast_to(edge, (1, LANES))
+    marks_ref[1:2, :] = jnp.full((1, LANES), where_ref[0], jnp.int32)
+    marks_ref[2:8, :] = jnp.zeros((6, LANES), jnp.int32)
     for t in range(measured_ref.shape[0] // LANES):
         lanes = slice(t * LANES, (t + 1) * LANES)
-        rows_ref[:, lanes] = measured_ref[lanes, :].T
+        turned_ref[:, lanes] = measured_ref[lanes, :].T
+    rows_ref[...] = turned_ref[pl.ds(pl.multiple_of(where_ref[1] * 8, 8), 8), :]
     for f in range(offsets_ref.shape[0]):
         rows = slice(f * K, (f + 1) * K)
         for axis in range(2):
@@ -151,15 +153,16 @@
     if last:
         (samples_ref,) = rest
         own = samples_ref.shape[0] // 2
-        for ref, core in ((got_ref, marks_ref[2]), (other_ref, 1 - marks_ref[2])):
-            at = pl.ds(pl.multiple_of(core * own, own), own)
-            samples_ref[at, :] = jnp.concatenate(slabs(ref[...].astype(F32))[::2], axis=0).astype(BF16)
+        highs = [jnp.concatenate(slabs(ref[...].astype(F32))[::2], axis=0) for ref in (got_ref, other_ref)]
+        first_core = marks_ref[1:2, 0:1] == 0
+        samples_ref[:own] = jnp.where(first_core, *highs).astype(BF16)
+        samples_ref[own:] = jnp.where(first_core, *highs[::-1]).astype(BF16)
     else:
         samples_ref = got_ref
     turned = dot(table_ref[0], samples_ref[...]) + dot(table_ref[1], samples_ref[...])
     turned_ref[...] = turned.astype(BF16)
 
-    start = marks_ref[0]
+    start = marks_ref[0:1, 0:1]
     bounds = (start, start + GROUP)
     scales = None if first else [scale_ref[g : g + 1, 0:1] for g in range(3)]
     sums = [jnp.zeros((1, block), F32) for _ in range(4)]
@@ -189,7 +192,7 @@
 ):
     coefs, sources = state_ref.shape
     total = out_ref.shape[0] // 3
-    start = marks_ref[0]
+    start = marks_ref[0:1, 0:1]
     bounds = (start, start + GROUP)
     none = jnp.zeros((), BF16)
     for j in range(sources // block):
@@ -220,12 +223,11 @@
 
 def plane_kernel(got_ref, out_ref):
     total = sum(slabs(got_ref[...].astype(F32)))
-    out_ref[...] = jnp.concatenate([total] * (out_ref.shape[0] // 8), axis=0)
-
-
-def owner_kernel(marks_ref, got_ref, measured_ref, out_ref, *, last):
-    at = pl.ds(pl.multiple_of(marks_ref[1] * 8, 8), 8)
-    row = measured_ref[at, :] - sum(slabs(got_ref[...]))
+    out_ref[...] = jnp.concatenate([total] * (out_ref.shape[0] // 8), axis=0).astype(BF16)
+
+
+def owner_kernel(got_ref, measured_ref, out_ref, *, last):
+    row = measured_ref[...] - sum(slabs(got_ref[...].astype(F32)))
     if last:
         high = row.astype(BF16).astype(F32)
         row = jnp.concatenate([high, row - high], axis=0)
@@ -248,7 +250,7 @@
         *powers, _, out_hbm, scaled_ref, sem = rest
         scales = [scale[:, 0:1] for scale in scales_of(powers, tau)]
     blocks, _, block = scaled_ref.shape
-    start = marks_ref[0]
+    start = jnp.max(marks_ref[0:1, :])
     bounds = (start, start + GROUP)
     wanted, stores = [], []
     for j in range(blocks):
@@ -307,19 +309,19 @@
             struct(BF16, 2, coefs, total),
             struct(BF16, 2, total, coefs),
             struct(BF16, total, sensors),
-            struct(jnp.int32, 3),
-            struct(F32, own, sensors),
+            struct(jnp.int32, 8, LANES),
+            struct(F32, 8, sensors),
             struct(F32, 1, sources),
             struct(F32, coefs, sources),
             struct(BF16, sensors, sources),
         ],
         ins=[SMEM] + [HBM] * len(inputs),
-        out_specs=[VMEM, VMEM, VMEM, SMEM, VMEM, VMEM, VMEM, VMEM],
-        scratch=[
+                scratch=[
             pltpu.SMEM(offsets.shape, jnp.int32),
             pltpu.VMEM((4, K, K), BF16),
             pltpu.VMEM((1, sources), jnp.int32),
             pltpu.VMEM((sensors, own), F32),
+            pltpu.VMEM((own, sensors), F32),
             pltpu.VMEM((coefs, sensors), F32),
             dma,
             dma,
@@ -338,7 +340,6 @@
         "step",
         args,
         [struct(F32, coefs, sources), struct(F32, 8, LANES)],
-        ins=[SMEM] + [VMEM] * (len(args) - 1),
         scratch=[pltpu.VMEM((coefs, sensors), BF16)] + ([pltpu.VMEM((table.shape[2], sensors), BF16)] if last else []),
     )
 
@@ -351,7 +352,6 @@
         "forward",
         [marks, state, depth, lead, table_t, power, pair],
         [struct(F32, 3 * table_t.shape[1], sensors)],
-        ins=[SMEM] + [VMEM] * 6,
         scratch=[pltpu.VMEM((2, 2 * coefs, GROUP), BF16)],
         cost=pl.CostEstimate(flops=4 * coefs * sources * sensors, bytes_accessed=8 << 20, transcendentals=0),
     )[0]
@@ -367,7 +367,7 @@
         "estimate",
         args,
         [struct(F32, coefs, sources)],
-        ins=[SMEM] + [VMEM] * (1 + len(powers)) + ([] if middle else [HBM]),
+        ins=[VMEM] * (2 + len(powers)) + ([] if middle else [HBM]),
         out_specs=[HBM],
         scratch=[pltpu.VMEM((blocks, coefs, BLOCK), F32), pltpu.SemaphoreType.DMA((blocks,))],
         alias={} if middle else {len(args) - 1: 0},
@@ -405,22 +405,25 @@
     for iteration in range(ITERS):
         last = iteration == ITERS - 1
         plane = call(
-            plane_kernel, "plane_sum", [exchange(folded, PLANES)], [struct(F32, 8 * AXES["z"], sensors)]
+            plane_kernel, "plane_sum", [exchange(folded, PLANES)], [struct(BF16, 8 * AXES["z"], sensors)]
         )[0]
         slab = call(
             lambda *refs, last=last: owner_kernel(*refs, last=last),
             "owner",
-            [marks, exchange(plane, "z"), rows],
+            [exchange(plane, "z"), rows],
             [struct(BF16, total, sensors)],
-            ins=[SMEM, VMEM, VMEM],
         )[0]
         got = exchange(slab, PLANE if last else PLANES)
         others = move(got, 0, 1) if last else None
         state, power = step_call(marks, got, others, table, scale, depth_row, state, lead)
         pair = move(power, 0, 1)
-        powers = [power, pair, move(power, 1, 0), move(power, 1, 1), move(power, -1, 0), move(power, -1, 1)]
+        powers = [power, pair, move(power, -1, 0), move(power, -1, 1), move(power, 1, 0), move(power, 1, 1)]
+        if last:
+            residual = call(residual_kernel, "residual", [got], [struct(F32, sensors, own)])[0]
+            estimate = estimate_call(marks, state, [power, pair], tau)
+        else:
+            parts = forward_call(marks, state, depth_row, lead, table_t, power, pair, tau)
         if not last:
-            parts = forward_call(marks, state, depth_row, lead, table_t, power, pair, tau)
             folded, scale = call(
                 lambda *refs: fold_kernel(*refs, tau=tau),
                 "fold",
@@ -428,8 +431,6 @@
                 [struct(BF16, total, sensors), struct(F32, 8, LANES)],
             )
 
-    residual = call(residual_kernel, "residual", [got], [struct(F32, sensors, own)])[0]
-    estimate = estimate_call(marks, state, powers[:2], tau)
     estimate = estimate_call(marks, state, powers, tau, estimate)
     return (estimate.reshape(frames, K, sources).transpose(2, 0, 1), residual)
 

time: 174 us -> 169 us (0.971)
  Pallas kernels: 28.3 us -> 23.3 us
  blocking collectives: 118 us -> 113 us
  waiting for transfers between devices: 11.4 us -> 16 us
    pallas_call x17, Pallas kernels: 28.3 us -> 23.3 us  [call(): pl.pallas_call(kernel, in_specs=ins or [VMEM] * len(args), out_specs=out_...]
    all_to_all x9, blocking collectives: 118 us -> 113 us  [exchange(): return lax.all_to_all(rows, axes, 0, 0, tiled=True)]
    ppermute x16, waiting for transfers between devices: 11.4 us -> 16 us  [move(): return lax.ppermute(x, (*SRC, 'frm'), route)]
  transfers between devices with their start and end apart: 16 -> 16, of which waited for: 7 -> 7; matrix products, arithmetic and copies ran while one was open for 0% -> 0% of each run, Pallas kernels for 6% -> 5%
where the time goes in v6:
time: 169 us
  blocking collectives  113 us (67%)
  Pallas kernels  23.3 us (14%)
  waiting for transfers between devices  16 us (9%)
  starting transfers between devices  15.3 us (9%)
    all_to_all x9, blocking collectives, exchange(): return lax.all_to_all(rows, axes, 0, 0, tiled=True)  113 us
    pallas_call x17, Pallas kernels, call(): pl.pallas_call(kernel, in_specs=ins or [VMEM] * len(args), out_specs=out_...  23.3 us
    ppermute x16, waiting for transfers between devices, move(): return lax.ppermute(x, (*SRC, 'frm'), route)  16 us
    ppermute x16, starting transfers between devices, move(): return lax.ppermute(x, (*SRC, 'frm'), route)  15.3 us
  transfers between devices with their start and end apart: 16, of which 7 were waited for; matrix products, arithmetic and copies ran while one was open for 0% of the time, Pallas kernels for 5%

profile of v6, /device:TPU:1, one launch (start us, length us, event | category | flops | bytes accessed | tf_op | source)
XLA Modules:
  0.0 168.9 jit_solution(13075601706930411768)
XLA Ops:
  0.6 0.1 pad_add_fusion.where_ref
  0.7 6.6 %first_forward.1 = (bf16[2,256,256]{2,1,0:T(8,128)(2,1)S(1)}, bf16[2,256,256]{2,1,0:T(8,128)(2,1)S(1)}, bf16[256,512]{1,0:T(8,128)(2,1)S(1)}, s32[8,128]{1,0:T(8...) custom-call(s32[2]{0:T(128)S(1)} %pad_add_fusion.where_ref, ...), custom_call_target="tpu_custom_call" | custom-call | tf_op jit(solution)/shard_map/first_forward/pallas_call | solution.py:287
  7.3 17.2 %all_to_all.99 = bf16[32,8,512]{2,1,0:T(8,128)(2,1)S(1)} all-to-all(bf16[32,8,512]{2,1,0:T(8,128)(2,1)S(1)} %bitcast.42), channel_id=1, replica_groups=mesh['x'=4,'z'=8,'y'=4,'frm'=2] {'frm','x','y'}, dimensions={0} | all-to-all | bytes 524288 | tf_op jit(solution)/shard_map/all_to_all | solution.py:390
  24.5 15.3 %all_to_all.100 = bf16[8,8,512]{2,1,0:T(8,128)(2,1)S(1)} all-to-all(bf16[8,8,512]{2,1,0:T(8,128)(2,1)S(1)} %bitcast.39), channel_id=1, replica_groups=mesh['x'=4,'z'=8,'y'=4,'frm'=2] {'z'}, dimensions={0} | all-to-all | bytes 131072 | tf_op jit(solution)/shard_map/all_to_all | solution.py:390
  39.9 13.8 %all_to_all.101 = bf16[32,8,512]{2,1,0:T(8,128)(2,1)S(1)} all-to-all(bf16[32,8,512]{2,1,0:T(8,128)(2,1)S(1)} %bitcast.37), channel_id=1, replica_groups=mesh['x'=4,'z'=8,'y'=4,'frm'=2] {'frm','x','y'}, dimensions={0} | all-to-all | bytes 524288 | tf_op jit(solution)/shard_map/all_to_all | solution.py:390
  53.7 1.9 %step.3 = (f32[256,4096]{1,0:T(8,128)S(1)}, f32[8,128]{1,0:T(8,128)S(1)}) custom-call(s32[8,128]{1,0:T(8,128)S(1)} %get-tuple-element.20.refs_0_, bf16[256,512]{1,0:T(8,128)(2,1)S(1)} %bitcast.32, bf16[2,256,256]{2,1,0:T(8,128)(2,1)S(1)} %get-tuple-element.23.refs_2_.refs_3_, f32[1,4096]{1,0:T(1,128)S(1)} %get-tuple-element.24.refs_3_.refs_2_.refs_4_, ...), custom_call_target="tpu_custom_call" | custom-call | tf_op jit(solution)/shard_map/step/pallas_call | solution.py:287
  55.6 0.7 collective-permute-start
  56.3 1.2 collective-permute-start.1
  57.5 0.3 collective-permute-start.2
  57.7 1.4 collective-permute-start.3
  59.2 0.6 collective-permute-start.4
  59.8 3.0 %forward.2.refs_0_ = f32[768,512]{1,0:T(8,128)S(1)} custom-call(s32[8,128]{1,0:T(8,128)S(1)} %get-tuple-element.20.refs_0_, f32[256,4096]{1,0:T(8,128)S(1)} %get-tuple-element.27.refs_1_.refs_4_, f32[1,4096]{1,0:T(1,128)S(1)} %get-tuple-element.24.refs_3_.refs_2_.refs_4_, bf16[512,4096]{1,0:T(8,128)(2,1)S(1)} %get-tuple-element.26.refs_5_.refs_3_.refs_6_, ...), custom_call_target="tpu_custom_call" | custom-call | flops 2147483648 | bytes 8388608 | tf_op jit(solution)/shard_map/forward/pallas_call | solution.py:287
  62.8 0.0 collective-permute-done.2.refs_4_
  62.8 2.8 %collective-permute-done.3.refs_5_ = f32[8,128]{1,0:T(8,128)S(1)} collective-permute-done((f32[8,128]{1,0:T(8,128)S(1)}, f32[8,128]{1,0:T(8,128)S(1)}, u32[]{:S(2)}, u32[]{:S(2)}) %collective-permute-start.3) | collective-permute-done | bytes 4128 | tf_op jit(solution)/shard_map/ppermute | solution.py:398
  65.6 2.1 %collective-permute-done.4.refs_6_ = f32[8,128]{1,0:T(8,128)S(1)} collective-permute-done((f32[8,128]{1,0:T(8,128)S(1)}, f32[8,128]{1,0:T(8,128)S(1)}, u32[]{:S(2)}, u32[]{:S(2)}) %collective-permute-start.4) | collective-permute-done | bytes 4128 | tf_op jit(solution)/shard_map/ppermute | solution.py:398
  67.7 0.2 fold.2
  67.9 12.0 %all_to_all.102 = bf16[32,8,512]{2,1,0:T(8,128)(2,1)S(1)} all-to-all(bf16[32,8,512]{2,1,0:T(8,128)(2,1)S(1)} %bitcast.43), channel_id=1, replica_groups=mesh['x'=4,'z'=8,'y'=4,'frm'=2] {'frm','x','y'}, dimensions={0} | all-to-all | bytes 524288 | tf_op jit(solution)/shard_map/all_to_all | solution.py:390
  79.9 9.6 %all_to_all.103 = bf16[8,8,512]{2,1,0:T(8,128)(2,1)S(1)} all-to-all(bf16[8,8,512]{2,1,0:T(8,128)(2,1)S(1)} %bitcast.40), channel_id=1, replica_groups=mesh['x'=4,'z'=8,'y'=4,'frm'=2] {'z'}, dimensions={0} | all-to-all | bytes 131072 | tf_op jit(solution)/shard_map/all_to_all | solution.py:390
  89.6 13.6 %all_to_all.104 = bf16[32,8,512]{2,1,0:T(8,128)(2,1)S(1)} all-to-all(bf16[32,8,512]{2,1,0:T(8,128)(2,1)S(1)} %bitcast.38), channel_id=1, replica_groups=mesh['x'=4,'z'=8,'y'=4,'frm'=2] {'frm','x','y'}, dimensions={0} | all-to-all | bytes 524288 | tf_op jit(solution)/shard_map/all_to_all | solution.py:390
  103.2 2.0 %step.4 = (f32[256,4096]{1,0:T(8,128)S(1)}, f32[8,128]{1,0:T(8,128)S(1)}) custom-call(s32[8,128]{1,0:T(8,128)S(1)} %get-tuple-element.20.refs_0_, bf16[256,512]{1,0:T(8,128)(2,1)S(1)} %bitcast.31, bf16[2,256,256]{2,1,0:T(8,128)(2,1)S(1)} %get-tuple-element.23.refs_2_.refs_3_, f32[1,4096]{1,0:T(1,128)S(1)} %get-tuple-element.24.refs_3_.refs_2_.refs_4_, ...), custom_call_target="tpu_custom_call" | custom-call | tf_op jit(solution)/shard_map/step/pallas_call | solution.py:287
  105.1 0.7 collective-permute-start.5
  105.8 1.1 collective-permute-start.6
  107.0 0.3 collective-permute-start.7
  107.3 1.5 collective-permute-start.8
  108.8 0.6 collective-permute-start.9
  109.4 0.0 collective-permute-done.5.refs_6_.refs_2_
  109.4 3.0 %forward.3.refs_0_ = f32[768,512]{1,0:T(8,128)S(1)} custom-call(s32[8,128]{1,0:T(8,128)S(1)} %get-tuple-element.20.refs_0_, f32[256,4096]{1,0:T(8,128)S(1)} %get-tuple-element.32.refs_1_.refs_5_, f32[1,4096]{1,0:T(1,128)S(1)} %get-tuple-element.24.refs_3_.refs_2_.refs_4_, bf16[512,4096]{1,0:T(8,128)(2,1)S(1)} %get-tuple-element.26.refs_5_.refs_3_.refs_6_, ...), custom_call_target="tpu_custom_call" | custom-call | flops 2147483648 | bytes 8388608 | tf_op jit(solution)/shard_map/forward/pallas_call | solution.py:287
  112.4 0.0 collective-permute-done.6.refs_3_
  112.4 2.8 %collective-permute-done.8.refs_5_ = f32[8,128]{1,0:T(8,128)S(1)} collective-permute-done((f32[8,128]{1,0:T(8,128)S(1)}, f32[8,128]{1,0:T(8,128)S(1)}, u32[]{:S(2)}, u32[]{:S(2)}) %collective-permute-start.8) | collective-permute-done | bytes 4128 | tf_op jit(solution)/shard_map/ppermute | solution.py:398
  115.2 2.1 %collective-permute-done.9.refs_6_ = f32[8,128]{1,0:T(8,128)S(1)} collective-permute-done((f32[8,128]{1,0:T(8,128)S(1)}, f32[8,128]{1,0:T(8,128)S(1)}, u32[]{:S(2)}, u32[]{:S(2)}) %collective-permute-start.9) | collective-permute-done | bytes 4128 | tf_op jit(solution)/shard_map/ppermute | solution.py:398
  117.2 0.2 fold.3
  117.4 11.9 %all_to_all.105 = bf16[32,8,512]{2,1,0:T(8,128)(2,1)S(1)} all-to-all(bf16[32,8,512]{2,1,0:T(8,128)(2,1)S(1)} %bitcast.44), channel_id=1, replica_groups=mesh['x'=4,'z'=8,'y'=4,'frm'=2] {'frm','x','y'}, dimensions={0} | all-to-all | bytes 524288 | tf_op jit(solution)/shard_map/all_to_all | solution.py:390
  129.4 9.6 %all_to_all.106 = bf16[8,8,512]{2,1,0:T(8,128)(2,1)S(1)} all-to-all(bf16[8,8,512]{2,1,0:T(8,128)(2,1)S(1)} %bitcast.41), channel_id=1, replica_groups=mesh['x'=4,'z'=8,'y'=4,'frm'=2] {'z'}, dimensions={0} | all-to-all | bytes 131072 | tf_op jit(solution)/shard_map/all_to_all | solution.py:390
  139.1 10.1 %all_to_all.107 = bf16[16,16,512]{2,1,0:T(8,128)(2,1)S(1)} all-to-all(bf16[16,16,512]{2,1,0:T(8,128)(2,1)S(1)} %bitcast.36), channel_id=1, replica_groups=mesh['x'=4,'z'=8,'y'=4,'frm'=2] {'x','y'}, dimensions={0} | all-to-all | bytes 524288 | tf_op jit(solution)/shard_map/all_to_all | solution.py:390
  149.2 3.1 %collective-permute-start.10 = (bf16[256,512]{1,0:T(8,128)(2,1)S(1)}, bf16[256,512]{1,0:T(8,128)(2,1)S(1)}, u32[]{:S(2)}, u32[]{:S(2)}) collective-permute-start(bf16[256,512]{1,0:T(8,128)(2,1)S(1)} %bitcast.28), channel_id=1, source_target_pairs={{0,1},{1,0},{2,3},{3,2},{4,5},{5,4},{6,7},{7,6},{8,9},{9,8},{10,11... | collective-permute-start | bytes 786440 | tf_op jit(solution)/shard_map/ppermute | solution.py:398
  152.3 1.2 collective-permute-done.10.refs_2_
  153.4 2.0 %step.5 = (f32[256,4096]{1,0:T(8,128)S(1)}, f32[8,128]{1,0:T(8,128)S(1)}) custom-call(s32[8,128]{1,0:T(8,128)S(1)} %get-tuple-element.20.refs_0_, bf16[256,512]{1,0:T(8,128)(2,1)S(1)} %bitcast.29, bf16[256,512]{1,0:T(8,128)(2,1)S(1)} %collective-permute-done.10.refs_2_, bf16[2,256,256]{2,1,0:T(8,128)(2,1)S(1)} %get-tuple-element.23.refs_2_.refs_3_, ...), custom_call_target="tpu_custom_call" | custom-call | tf_op jit(solution)/shard_map/step/pallas_call | solution.py:287
  155.5 0.4 collective-permute-start.11
  155.9 0.7 collective-permute-start.12
  156.6 1.2 collective-permute-start.13
  157.8 0.6 collective-permute-start.14
  158.4 1.0 collective-permute-start.15
  159.4 0.8 residual.1
  160.2 1.5 estimate.2.refs_8_
  161.7 0.0 collective-permute-done.12.refs_4_
  161.7 4.0 %collective-permute-done.14.refs_6_ = f32[8,128]{1,0:T(8,128)S(1)} collective-permute-done((f32[8,128]{1,0:T(8,128)S(1)}, f32[8,128]{1,0:T(8,128)S(1)}, u32[]{:S(2)}, u32[]{:S(2)}) %collective-permute-start.14) | collective-permute-done | bytes 4128 | tf_op jit(solution)/shard_map/ppermute | solution.py:398
  165.7 1.1 collective-permute-done.15.refs_7_
  166.8 1.9 %estimate.3 = f32[256,4096]{1,0:T(8,128)} custom-call(s32[8,128]{1,0:T(8,128)S(1)} %get-tuple-element.20.refs_0_, f32[256,4096]{1,0:T(8,128)S(1)} %get-tuple-element.36.refs_1_, f32[8,128]{1,0:T(8,128)S(1)} %get-tuple-element.37.refs_2_, f32[8,128]{1,0:T(8,128)S(1)} %collective-permute-done.11.refs_3_, ...), custom_call_target="tpu_custom_call", output_to_operand_aliasing={{}: (8, {})} | custom-call | flops 1048576 | bytes 4194304 | tf_op jit(solution)/shard_map/estimate/pallas_call | solution.py:287
  (11 shorter events, 0.2 us)
Async XLA Ops:
  55.6 4.2 %collective-permute-start = (f32[8,128]{1,0:T(8,128)S(1)}, f32[8,128]{1,0:T(8,128)S(1)}, u32[]{:S(2)}, u32[]{:S(2)}) collective-permute-start(f32[8,128]{1,0:T(8,128)S(1)} %get-tuple-element.29.refs_5_.refs_1_), channel_id=1, source_target_pairs={{0,1},{1,0},{2,3},{3,2},{4,5},{5,4},{6,7},{7,6},{8,9},{9,8},{10,11... | collective-permute-start | bytes 12296 | tf_op jit(solution)/shard_map/ppermute | solution.py:398
  56.3 6.5 %collective-permute-start.1 = (f32[8,128]{1,0:T(8,128)S(1)}, f32[8,128]{1,0:T(8,128)S(1)}, u32[]{:S(2)}, u32[]{:S(2)}) collective-permute-start(f32[8,128]{1,0:T(8,128)S(1)} %get-tuple-element.29.refs_5_.refs_1_), channel_id=1, source_target_pairs={{0,254},{1,255},{2,0},{3,1},{4,2},{5,3},{6,4},{7,5},{8,6},{9,7},{1... | collective-permute-start | bytes 12296 | tf_op jit(solution)/shard_map/ppermute | solution.py:398
  57.5 5.4 %collective-permute-start.2 = (f32[8,128]{1,0:T(8,128)S(1)}, f32[8,128]{1,0:T(8,128)S(1)}, u32[]{:S(2)}, u32[]{:S(2)}) collective-permute-start(f32[8,128]{1,0:T(8,128)S(1)} %get-tuple-element.29.refs_5_.refs_1_), channel_id=1, source_target_pairs={{0,255},{1,254},{2,1},{3,0},{4,3},{5,2},{6,5},{7,4},{8,7},{9,6},{1... | collective-permute-start | bytes 12296 | tf_op jit(solution)/shard_map/ppermute | solution.py:398
  57.7 7.9 %collective-permute-start.3 = (f32[8,128]{1,0:T(8,128)S(1)}, f32[8,128]{1,0:T(8,128)S(1)}, u32[]{:S(2)}, u32[]{:S(2)}) collective-permute-start(f32[8,128]{1,0:T(8,128)S(1)} %get-tuple-element.29.refs_5_.refs_1_), channel_id=1, source_target_pairs={{0,2},{1,3},{2,4},{3,5},{4,6},{5,7},{6,8},{7,9},{8,10},{9,11},{10,... | collective-permute-start | bytes 12296 | tf_op jit(solution)/shard_map/ppermute | solution.py:398
  59.2 8.5 %collective-permute-start.4 = (f32[8,128]{1,0:T(8,128)S(1)}, f32[8,128]{1,0:T(8,128)S(1)}, u32[]{:S(2)}, u32[]{:S(2)}) collective-permute-start(f32[8,128]{1,0:T(8,128)S(1)} %get-tuple-element.29.refs_5_.refs_1_), channel_id=1, source_target_pairs={{0,3},{1,2},{2,5},{3,4},{4,7},{5,6},{6,9},{7,8},{8,11},{9,10},{10,... | collective-permute-start | bytes 12296 | tf_op jit(solution)/shard_map/ppermute | solution.py:398
  105.1 4.2 %collective-permute-start.5 = (f32[8,128]{1,0:T(8,128)S(1)}, f32[8,128]{1,0:T(8,128)S(1)}, u32[]{:S(2)}, u32[]{:S(2)}) collective-permute-start(f32[8,128]{1,0:T(8,128)S(1)} %get-tuple-element.33.refs_5_.refs_1_), channel_id=1, source_target_pairs={{0,1},{1,0},{2,3},{3,2},{4,5},{5,4},{6,7},{7,6},{8,9},{9,8},{10,11... | collective-permute-start | bytes 12296 | tf_op jit(solution)/shard_map/ppermute | solution.py:398
  105.8 6.5 %collective-permute-start.6 = (f32[8,128]{1,0:T(8,128)S(1)}, f32[8,128]{1,0:T(8,128)S(1)}, u32[]{:S(2)}, u32[]{:S(2)}) collective-permute-start(f32[8,128]{1,0:T(8,128)S(1)} %get-tuple-element.33.refs_5_.refs_1_), channel_id=1, source_target_pairs={{0,254},{1,255},{2,0},{3,1},{4,2},{5,3},{6,4},{7,5},{8,6},{9,7},{1... | collective-permute-start | bytes 12296 | tf_op jit(solution)/shard_map/ppermute | solution.py:398
  107.0 5.4 %collective-permute-start.7 = (f32[8,128]{1,0:T(8,128)S(1)}, f32[8,128]{1,0:T(8,128)S(1)}, u32[]{:S(2)}, u32[]{:S(2)}) collective-permute-start(f32[8,128]{1,0:T(8,128)S(1)} %get-tuple-element.33.refs_5_.refs_1_), channel_id=1, source_target_pairs={{0,255},{1,254},{2,1},{3,0},{4,3},{5,2},{6,5},{7,4},{8,7},{9,6},{1... | collective-permute-start | bytes 12296 | tf_op jit(solution)/shard_map/ppermute | solution.py:398
  107.3 7.9 %collective-permute-start.8 = (f32[8,128]{1,0:T(8,128)S(1)}, f32[8,128]{1,0:T(8,128)S(1)}, u32[]{:S(2)}, u32[]{:S(2)}) collective-permute-start(f32[8,128]{1,0:T(8,128)S(1)} %get-tuple-element.33.refs_5_.refs_1_), channel_id=1, source_target_pairs={{0,2},{1,3},{2,4},{3,5},{4,6},{5,7},{6,8},{7,9},{8,10},{9,11},{10,... | collective-permute-start | bytes 12296 | tf_op jit(solution)/shard_map/ppermute | solution.py:398
  108.8 8.5 %collective-permute-start.9 = (f32[8,128]{1,0:T(8,128)S(1)}, f32[8,128]{1,0:T(8,128)S(1)}, u32[]{:S(2)}, u32[]{:S(2)}) collective-permute-start(f32[8,128]{1,0:T(8,128)S(1)} %get-tuple-element.33.refs_5_.refs_1_), channel_id=1, source_target_pairs={{0,3},{1,2},{2,5},{3,4},{4,7},{5,6},{6,9},{7,8},{8,11},{9,10},{10,... | collective-permute-start | bytes 12296 | tf_op jit(solution)/shard_map/ppermute | solution.py:398
  149.2 4.2 %collective-permute-start.10 = (bf16[256,512]{1,0:T(8,128)(2,1)S(1)}, bf16[256,512]{1,0:T(8,128)(2,1)S(1)}, u32[]{:S(2)}, u32[]{:S(2)}) collective-permute-start(bf16[256,512]{1,0:T(8,128)(2,1)S(1)} %bitcast.28), channel_id=1, source_target_pairs={{0,1},{1,0},{2,3},{3,2},{4,5},{5,4},{6,7},{7,6},{8,9},{9,8},{10,11... | collective-permute-start | bytes 786440 | tf_op jit(solution)/shard_map/ppermute | solution.py:398
  155.5 4.7 %collective-permute-start.11 = (f32[8,128]{1,0:T(8,128)S(1)}, f32[8,128]{1,0:T(8,128)S(1)}, u32[]{:S(2)}, u32[]{:S(2)}) collective-permute-start(f32[8,128]{1,0:T(8,128)S(1)} %get-tuple-element.37.refs_2_), channel_id=1, source_target_pairs={{0,1},{1,0},{2,3},{3,2},{4,5},{5,4},{6,7},{7,6},{8,9},{9,8},{10,11... | collective-permute-start | bytes 12296 | tf_op jit(solution)/shard_map/ppermute | solution.py:398
  155.9 5.8 %collective-permute-start.12 = (f32[8,128]{1,0:T(8,128)S(1)}, f32[8,128]{1,0:T(8,128)S(1)}, u32[]{:S(2)}, u32[]{:S(2)}) collective-permute-start(f32[8,128]{1,0:T(8,128)S(1)} %get-tuple-element.37.refs_2_), channel_id=1, source_target_pairs={{0,254},{1,255},{2,0},{3,1},{4,2},{5,3},{6,4},{7,5},{8,6},{9,7},{1... | collective-permute-start | bytes 12296 | tf_op jit(solution)/shard_map/ppermute | solution.py:398
  156.6 5.2 %collective-permute-start.13 = (f32[8,128]{1,0:T(8,128)S(1)}, f32[8,128]{1,0:T(8,128)S(1)}, u32[]{:S(2)}, u32[]{:S(2)}) collective-permute-start(f32[8,128]{1,0:T(8,128)S(1)} %get-tuple-element.37.refs_2_), channel_id=1, source_target_pairs={{0,255},{1,254},{2,1},{3,0},{4,3},{5,2},{6,5},{7,4},{8,7},{9,6},{1... | collective-permute-start | bytes 12296 | tf_op jit(solution)/shard_map/ppermute | solution.py:398
  157.8 7.9 %collective-permute-start.14 = (f32[8,128]{1,0:T(8,128)S(1)}, f32[8,128]{1,0:T(8,128)S(1)}, u32[]{:S(2)}, u32[]{:S(2)}) collective-permute-start(f32[8,128]{1,0:T(8,128)S(1)} %get-tuple-element.37.refs_2_), channel_id=1, source_target_pairs={{0,2},{1,3},{2,4},{3,5},{4,6},{5,7},{6,8},{7,9},{8,10},{9,11},{10,... | collective-permute-start | bytes 12296 | tf_op jit(solution)/shard_map/ppermute | solution.py:398
  158.4 8.5 %collective-permute-start.15 = (f32[8,128]{1,0:T(8,128)S(1)}, f32[8,128]{1,0:T(8,128)S(1)}, u32[]{:S(2)}, u32[]{:S(2)}) collective-permute-start(f32[8,128]{1,0:T(8,128)S(1)} %get-tuple-element.37.refs_2_), channel_id=1, source_target_pairs={{0,3},{1,2},{2,5},{3,4},{4,7},{5,6},{6,9},{7,8},{8,11},{9,10},{10,... | collective-permute-start | bytes 12296 | tf_op jit(solution)/shard_map/ppermute | solution.py:398

commit v7 on v6

--- a/solution.py
+++ b/solution.py
@@ -15,6 +15,7 @@
 ITERS = 3
 LANES = 128
 BLOCK = 512
+FIRST_BLOCK = 2048
 step_size = 0.5
 shrink_one = 0.05
 group_weight = 0.03
@@ -62,12 +63,11 @@
 
 
 def scales_of(powers, tau):
-    mine, pair, after, after_pair, before, before_pair = (ref[...] for ref in powers)
-    chip = mine + pair
+    chip, after, before = (ref[...] for ref in powers)
     return (
-        group_scale(chip[0:1] + (before + before_pair)[2:3], tau),
+        group_scale(chip[0:1] + before[2:3], tau),
         group_scale(chip[1:2], tau),
-        group_scale(chip[2:3] + (after + after_pair)[0:1], tau),
+        group_scale(chip[2:3] + after[0:1], tau),
     )
 
 
@@ -187,7 +187,7 @@
 
 
 def forward_kernel(
-    marks_ref, state_ref, depth_ref, lead_ref, table_t_ref, power_ref, pair_ref, out_ref, weighted_ref, *,
+    marks_ref, state_ref, depth_ref, lead_ref, table_t_ref, chip_ref, out_ref, weighted_ref, *,
     block, tau,
 ):
     coefs, sources = state_ref.shape
@@ -204,7 +204,7 @@
         weighted_ref[half, :coefs, inner] = jnp.where(before, weighted, none)
         weighted_ref[half, coefs:, inner] = jnp.where(before, none, weighted)
     halves = [dot_t(weighted_ref[h], lead_ref[:, h * GROUP : (h + 1) * GROUP]) for h in range(2)]
-    middle = group_scale(power_ref[1:2, 0:1] + pair_ref[1:2, 0:1], tau) * (halves[0][coefs:] + halves[1][:coefs])
+    middle = group_scale(chip_ref[1:2, 0:1], tau) * (halves[0][coefs:] + halves[1][:coefs])
     parts = (halves[0][:coefs], middle, halves[1][coefs:])
     for g in range(3):
         out_ref[g * total : (g + 1) * total, :] = to_samples(table_t_ref, parts[g])
@@ -234,6 +234,10 @@
     out_ref[...] = jnp.concatenate([row] * (out_ref.shape[0] // row.shape[0]), axis=0).astype(BF16)
 
 
+def add_kernel(a_ref, b_ref, out_ref):
+    out_ref[...] = a_ref[...] + b_ref[...]
+
+
 def residual_kernel(own_ref, out_ref):
     pieces = slabs(own_ref[...].astype(F32))
     rows = jnp.concatenate([high + low for high, low in zip(pieces[::2], pieces[1::2])], axis=0)
@@ -244,8 +248,8 @@
 
 def estimate_kernel(marks_ref, state_ref, *rest, tau, middle):
     if middle:
-        power_ref, pair_ref, out_hbm, scaled_ref, sem = rest
-        scales = [None, group_scale(power_ref[1:2, 0:1] + pair_ref[1:2, 0:1], tau), None]
+        chip_ref, out_hbm, scaled_ref, sem = rest
+        scales = [None, group_scale(chip_ref[1:2, 0:1], tau), None]
     else:
         *powers, _, out_hbm, scaled_ref, sem = rest
         scales = [scale[:, 0:1] for scale in scales_of(powers, tau)]
@@ -299,7 +303,7 @@
     coefs, sources = state.shape
     sensors, own = measured.shape
     total = 2 * own
-    dma = pltpu.SemaphoreType.DMA((sources // BLOCK,))
+    dma = pltpu.SemaphoreType.DMA((sources // FIRST_BLOCK,))
     inputs = (offsets, jnp.asarray(windowed_cosines()), groups, depth, measured, state, lead)
     return call(
         first_kernel,
@@ -344,13 +348,13 @@
     )
 
 
-def forward_call(marks, state, depth, lead, table_t, power, pair, tau):
+def forward_call(marks, state, depth, lead, table_t, chip, tau):
     coefs, sources = state.shape
     sensors = lead.shape[0]
     return call(
         lambda *refs: forward_kernel(*refs, block=BLOCK, tau=tau),
         "forward",
-        [marks, state, depth, lead, table_t, power, pair],
+        [marks, state, depth, lead, table_t, chip],
         [struct(F32, 3 * table_t.shape[1], sensors)],
         scratch=[pltpu.VMEM((2, 2 * coefs, GROUP), BF16)],
         cost=pl.CostEstimate(flops=4 * coefs * sources * sensors, bytes_accessed=8 << 20, transcendentals=0),
@@ -417,12 +421,13 @@
         others = move(got, 0, 1) if last else None
         state, power = step_call(marks, got, others, table, scale, depth_row, state, lead)
         pair = move(power, 0, 1)
-        powers = [power, pair, move(power, -1, 0), move(power, -1, 1), move(power, 1, 0), move(power, 1, 1)]
+        chip = call(add_kernel, "chip_power", [power, pair], [struct(F32, 8, LANES)])[0]
+        powers = [chip, move(chip, -1, 0), move(chip, 1, 0)]
         if last:
             residual = call(residual_kernel, "residual", [got], [struct(F32, sensors, own)])[0]
-            estimate = estimate_call(marks, state, [power, pair], tau)
+            estimate = estimate_call(marks, state, [chip], tau)
         else:
-            parts = forward_call(marks, state, depth_row, lead, table_t, power, pair, tau)
+            parts = forward_call(marks, state, depth_row, lead, table_t, chip, tau)
         if not last:
             folded, scale = call(
                 lambda *refs: fold_kernel(*refs, tau=tau),

time: 169 us -> 166 us (0.982)
  starting transfers between devices: 15.3 us -> 9.38 us
  blocking collectives: 113 us -> 116 us
    ppermute x16 -> x10, starting transfers between devices: 15.3 us -> 9.38 us  [move(): return lax.ppermute(x, (*SRC, 'frm'), route)]
    all_to_all x9, blocking collectives: 113 us -> 116 us  [exchange(): return lax.all_to_all(rows, axes, 0, 0, tiled=True)]
    ppermute x16 -> x10, waiting for transfers between devices: 16 us -> 17.5 us  [move(): return lax.ppermute(x, (*SRC, 'frm'), route)]
    pallas_call x17 -> x20, Pallas kernels: 23.3 us -> 22.1 us  [call(): pl.pallas_call(kernel, in_specs=ins or [VMEM] * len(args), out_specs=out_...]
  transfers between devices with their start and end apart: 16 -> 10, of which waited for: 7 -> 7; matrix products, arithmetic and copies ran while one was open for 0% -> 0% of each run, Pallas kernels for 5% -> 5%
where the time goes in v7:
time: 166 us
  blocking collectives  116 us (70%)
  Pallas kernels  22.1 us (13%)
  waiting for transfers between devices  17.5 us (11%)
  starting transfers between devices  9.38 us (6%)
    all_to_all x9, blocking collectives, exchange(): return lax.all_to_all(rows, axes, 0, 0, tiled=True)  116 us
    pallas_call x20, Pallas kernels, call(): pl.pallas_call(kernel, in_specs=ins or [VMEM] * len(args), out_specs=out_...  22.1 us
    ppermute x10, waiting for transfers between devices, move(): return lax.ppermute(x, (*SRC, 'frm'), route)  17.5 us
    ppermute x10, starting transfers between devices, move(): return lax.ppermute(x, (*SRC, 'frm'), route)  9.38 us
  transfers between devices with their start and end apart: 10, of which 7 were waited for; matrix products, arithmetic and copies ran while one was open for 0% of the time, Pallas kernels for 5%

profile of v7, /device:TPU:1, one launch (start us, length us, event | category | flops | bytes accessed | tf_op | source)
XLA Modules:
  0.0 166.0 jit_solution(6318128849437117802)
XLA Ops:
  0.6 0.1 pad_add_fusion.where_ref
  0.7 5.3 %first_forward.1 = (bf16[2,256,256]{2,1,0:T(8,128)(2,1)S(1)}, bf16[2,256,256]{2,1,0:T(8,128)(2,1)S(1)}, bf16[256,512]{1,0:T(8,128)(2,1)S(1)}, s32[8,128]{1,0:T(8...) custom-call(s32[2]{0:T(128)S(1)} %pad_add_fusion.where_ref, ...), custom_call_target="tpu_custom_call" | custom-call | tf_op jit(solution)/shard_map/first_forward/pallas_call | solution.py:291
  6.0 17.2 %all_to_all.99 = bf16[32,8,512]{2,1,0:T(8,128)(2,1)S(1)} all-to-all(bf16[32,8,512]{2,1,0:T(8,128)(2,1)S(1)} %bitcast.42), channel_id=1, replica_groups=mesh['x'=4,'z'=8,'y'=4,'frm'=2] {'frm','x','y'}, dimensions={0} | all-to-all | bytes 524288 | tf_op jit(solution)/shard_map/all_to_all | solution.py:394
  23.3 15.3 %all_to_all.100 = bf16[8,8,512]{2,1,0:T(8,128)(2,1)S(1)} all-to-all(bf16[8,8,512]{2,1,0:T(8,128)(2,1)S(1)} %bitcast.39), channel_id=1, replica_groups=mesh['x'=4,'z'=8,'y'=4,'frm'=2] {'z'}, dimensions={0} | all-to-all | bytes 131072 | tf_op jit(solution)/shard_map/all_to_all | solution.py:394
  38.7 13.8 %all_to_all.101 = bf16[32,8,512]{2,1,0:T(8,128)(2,1)S(1)} all-to-all(bf16[32,8,512]{2,1,0:T(8,128)(2,1)S(1)} %bitcast.37), channel_id=1, replica_groups=mesh['x'=4,'z'=8,'y'=4,'frm'=2] {'frm','x','y'}, dimensions={0} | all-to-all | bytes 524288 | tf_op jit(solution)/shard_map/all_to_all | solution.py:394
  52.5 1.9 %step.3 = (f32[256,4096]{1,0:T(8,128)S(1)}, f32[8,128]{1,0:T(8,128)S(1)}) custom-call(s32[8,128]{1,0:T(8,128)S(1)} %get-tuple-element.20.refs_0_, bf16[256,512]{1,0:T(8,128)(2,1)S(1)} %bitcast.32, bf16[2,256,256]{2,1,0:T(8,128)(2,1)S(1)} %get-tuple-element.23.refs_2_.refs_3_, f32[1,4096]{1,0:T(1,128)S(1)} %get-tuple-element.24.refs_3_.refs_2_.refs_4_, ...), custom_call_target="tpu_custom_call" | custom-call | tf_op jit(solution)/shard_map/step/pallas_call | solution.py:291
  54.4 0.7 collective-permute-start
  55.0 0.8 collective-permute-done.b_ref
  55.9 1.1 collective-permute-start.1
  57.0 0.3 collective-permute-start.2
  57.3 3.0 %forward.2.refs_0_ = f32[768,512]{1,0:T(8,128)S(1)} custom-call(s32[8,128]{1,0:T(8,128)S(1)} %get-tuple-element.20.refs_0_, f32[256,4096]{1,0:T(8,128)S(1)} %get-tuple-element.27.refs_1_.refs_4_, f32[1,4096]{1,0:T(1,128)S(1)} %get-tuple-element.24.refs_3_.refs_2_.refs_4_, bf16[512,4096]{1,0:T(8,128)(2,1)S(1)} %get-tuple-element.26.refs_5_.refs_3_.refs_6_, ...), custom_call_target="tpu_custom_call" | custom-call | flops 2147483648 | bytes 8388608 | tf_op jit(solution)/shard_map/forward/pallas_call | solution.py:291
  60.4 0.0 collective-permute-done.1.refs_2_
  60.4 4.5 %collective-permute-done.2.refs_3_ = f32[8,128]{1,0:T(8,128)S(1)} collective-permute-done((f32[8,128]{1,0:T(8,128)S(1)}, f32[8,128]{1,0:T(8,128)S(1)}, u32[]{:S(2)}, u32[]{:S(2)}) %collective-permute-start.2) | collective-permute-done | bytes 4128 | tf_op jit(solution)/shard_map/ppermute | solution.py:402
  64.9 0.2 fold.2
  65.2 13.3 %all_to_all.102 = bf16[32,8,512]{2,1,0:T(8,128)(2,1)S(1)} all-to-all(bf16[32,8,512]{2,1,0:T(8,128)(2,1)S(1)} %bitcast.43), channel_id=1, replica_groups=mesh['x'=4,'z'=8,'y'=4,'frm'=2] {'frm','x','y'}, dimensions={0} | all-to-all | bytes 524288 | tf_op jit(solution)/shard_map/all_to_all | solution.py:394
  78.5 9.6 %all_to_all.103 = bf16[8,8,512]{2,1,0:T(8,128)(2,1)S(1)} all-to-all(bf16[8,8,512]{2,1,0:T(8,128)(2,1)S(1)} %bitcast.40), channel_id=1, replica_groups=mesh['x'=4,'z'=8,'y'=4,'frm'=2] {'z'}, dimensions={0} | all-to-all | bytes 131072 | tf_op jit(solution)/shard_map/all_to_all | solution.py:394
  88.2 13.6 %all_to_all.104 = bf16[32,8,512]{2,1,0:T(8,128)(2,1)S(1)} all-to-all(bf16[32,8,512]{2,1,0:T(8,128)(2,1)S(1)} %bitcast.38), channel_id=1, replica_groups=mesh['x'=4,'z'=8,'y'=4,'frm'=2] {'frm','x','y'}, dimensions={0} | all-to-all | bytes 524288 | tf_op jit(solution)/shard_map/all_to_all | solution.py:394
  101.8 2.0 %step.4 = (f32[256,4096]{1,0:T(8,128)S(1)}, f32[8,128]{1,0:T(8,128)S(1)}) custom-call(s32[8,128]{1,0:T(8,128)S(1)} %get-tuple-element.20.refs_0_, bf16[256,512]{1,0:T(8,128)(2,1)S(1)} %bitcast.31, bf16[2,256,256]{2,1,0:T(8,128)(2,1)S(1)} %get-tuple-element.23.refs_2_.refs_3_, f32[1,4096]{1,0:T(1,128)S(1)} %get-tuple-element.24.refs_3_.refs_2_.refs_4_, ...), custom_call_target="tpu_custom_call" | custom-call | tf_op jit(solution)/shard_map/step/pallas_call | solution.py:291
  103.8 0.9 collective-permute-start.3
  104.6 0.8 collective-permute-done.3.b_ref
  105.5 1.1 collective-permute-start.4
  106.6 0.3 collective-permute-start.5
  106.9 3.0 %forward.3.refs_0_ = f32[768,512]{1,0:T(8,128)S(1)} custom-call(s32[8,128]{1,0:T(8,128)S(1)} %get-tuple-element.20.refs_0_, f32[256,4096]{1,0:T(8,128)S(1)} %get-tuple-element.32.refs_1_.refs_5_, f32[1,4096]{1,0:T(1,128)S(1)} %get-tuple-element.24.refs_3_.refs_2_.refs_4_, bf16[512,4096]{1,0:T(8,128)(2,1)S(1)} %get-tuple-element.26.refs_5_.refs_3_.refs_6_, ...), custom_call_target="tpu_custom_call" | custom-call | flops 2147483648 | bytes 8388608 | tf_op jit(solution)/shard_map/forward/pallas_call | solution.py:291
  109.9 0.0 collective-permute-done.4.refs_2_
  109.9 4.5 %collective-permute-done.5.refs_3_ = f32[8,128]{1,0:T(8,128)S(1)} collective-permute-done((f32[8,128]{1,0:T(8,128)S(1)}, f32[8,128]{1,0:T(8,128)S(1)}, u32[]{:S(2)}, u32[]{:S(2)}) %collective-permute-start.5) | collective-permute-done | bytes 4128 | tf_op jit(solution)/shard_map/ppermute | solution.py:402
  114.5 0.2 fold.3
  114.7 13.3 %all_to_all.105 = bf16[32,8,512]{2,1,0:T(8,128)(2,1)S(1)} all-to-all(bf16[32,8,512]{2,1,0:T(8,128)(2,1)S(1)} %bitcast.44), channel_id=1, replica_groups=mesh['x'=4,'z'=8,'y'=4,'frm'=2] {'frm','x','y'}, dimensions={0} | all-to-all | bytes 524288 | tf_op jit(solution)/shard_map/all_to_all | solution.py:394
  128.1 9.6 %all_to_all.106 = bf16[8,8,512]{2,1,0:T(8,128)(2,1)S(1)} all-to-all(bf16[8,8,512]{2,1,0:T(8,128)(2,1)S(1)} %bitcast.41), channel_id=1, replica_groups=mesh['x'=4,'z'=8,'y'=4,'frm'=2] {'z'}, dimensions={0} | all-to-all | bytes 131072 | tf_op jit(solution)/shard_map/all_to_all | solution.py:394
  137.7 10.1 %all_to_all.107 = bf16[16,16,512]{2,1,0:T(8,128)(2,1)S(1)} all-to-all(bf16[16,16,512]{2,1,0:T(8,128)(2,1)S(1)} %bitcast.36), channel_id=1, replica_groups=mesh['x'=4,'z'=8,'y'=4,'frm'=2] {'x','y'}, dimensions={0} | all-to-all | bytes 524288 | tf_op jit(solution)/shard_map/all_to_all | solution.py:394
  147.9 3.1 %collective-permute-start.6 = (bf16[256,512]{1,0:T(8,128)(2,1)S(1)}, bf16[256,512]{1,0:T(8,128)(2,1)S(1)}, u32[]{:S(2)}, u32[]{:S(2)}) collective-permute-start(bf16[256,512]{1,0:T(8,128)(2,1)S(1)} %bitcast.28), channel_id=1, source_target_pairs={{0,1},{1,0},{2,3},{3,2},{4,5},{5,4},{6,7},{7,6},{8,9},{9,8},{10,11... | collective-permute-start | bytes 786440 | tf_op jit(solution)/shard_map/ppermute | solution.py:402
  150.9 1.2 collective-permute-done.6.refs_2_
  152.1 2.0 %step.5 = (f32[256,4096]{1,0:T(8,128)S(1)}, f32[8,128]{1,0:T(8,128)S(1)}) custom-call(s32[8,128]{1,0:T(8,128)S(1)} %get-tuple-element.20.refs_0_, bf16[256,512]{1,0:T(8,128)(2,1)S(1)} %bitcast.29, bf16[256,512]{1,0:T(8,128)(2,1)S(1)} %collective-permute-done.6.refs_2_, bf16[2,256,256]{2,1,0:T(8,128)(2,1)S(1)} %get-tuple-element.23.refs_2_.refs_3_, ...), custom_call_target="tpu_custom_call" | custom-call | tf_op jit(solution)/shard_map/step/pallas_call | solution.py:291
  154.2 0.4 collective-permute-start.7
  154.5 0.8 collective-permute-done.7.b_ref
  155.4 0.7 collective-permute-start.8
  156.1 0.8 collective-permute-start.9
  156.8 0.8 residual.1
  157.7 1.5 estimate.2.refs_5_
  159.2 0.0 collective-permute-done.8.refs_3_
  159.2 4.8 %collective-permute-done.9.refs_4_ = f32[8,128]{1,0:T(8,128)S(1)} collective-permute-done((f32[8,128]{1,0:T(8,128)S(1)}, f32[8,128]{1,0:T(8,128)S(1)}, u32[]{:S(2)}, u32[]{:S(2)}) %collective-permute-start.9) | collective-permute-done | bytes 4128 | tf_op jit(solution)/shard_map/ppermute | solution.py:402
  163.9 1.9 %estimate.3 = f32[256,4096]{1,0:T(8,128)} custom-call(s32[8,128]{1,0:T(8,128)S(1)} %get-tuple-element.20.refs_0_, f32[256,4096]{1,0:T(8,128)S(1)} %get-tuple-element.36.refs_1_, f32[8,128]{1,0:T(8,128)S(1)} %chip_power.5.refs_2_, f32[8,128]{1,0:T(8,128)S(1)} %collective-permute-done.8.refs_3_, ...), custom_call_target="tpu_custom_call", output_to_operand_aliasing={{}: (5, {})} | custom-call | flops 1048576 | bytes 4194304 | tf_op jit(solution)/shard_map/estimate/pallas_call | solution.py:291
  (9 shorter events, 0.2 us)
Async XLA Ops:
  54.4 1.5 collective-permute-start
  55.9 4.5 %collective-permute-start.1 = (f32[8,128]{1,0:T(8,128)S(1)}, f32[8,128]{1,0:T(8,128)S(1)}, u32[]{:S(2)}, u32[]{:S(2)}) collective-permute-start(f32[8,128]{1,0:T(8,128)S(1)} %chip_power.3.refs_5_.refs_1_), channel_id=1, source_target_pairs={{0,254},{1,255},{2,0},{3,1},{4,2},{5,3},{6,4},{7,5},{8,6},{9,7},{1... | collective-permute-start | bytes 12296 | tf_op jit(solution)/shard_map/ppermute | solution.py:402
  57.0 7.9 %collective-permute-start.2 = (f32[8,128]{1,0:T(8,128)S(1)}, f32[8,128]{1,0:T(8,128)S(1)}, u32[]{:S(2)}, u32[]{:S(2)}) collective-permute-start(f32[8,128]{1,0:T(8,128)S(1)} %chip_power.3.refs_5_.refs_1_), channel_id=1, source_target_pairs={{0,2},{1,3},{2,4},{3,5},{4,6},{5,7},{6,8},{7,9},{8,10},{9,11},{10,... | collective-permute-start | bytes 12296 | tf_op jit(solution)/shard_map/ppermute | solution.py:402
  103.8 1.7 %collective-permute-start.3 = (f32[8,128]{1,0:T(8,128)S(1)}, f32[8,128]{1,0:T(8,128)S(1)}, u32[]{:S(2)}, u32[]{:S(2)}) collective-permute-start(f32[8,128]{1,0:T(8,128)S(1)} %get-tuple-element.33.a_ref), channel_id=1, source_target_pairs={{0,1},{1,0},{2,3},{3,2},{4,5},{5,4},{6,7},{7,6},{8,9},{9,8},{10,11... | collective-permute-start | bytes 12296 | tf_op jit(solution)/shard_map/ppermute | solution.py:402
  105.5 4.5 %collective-permute-start.4 = (f32[8,128]{1,0:T(8,128)S(1)}, f32[8,128]{1,0:T(8,128)S(1)}, u32[]{:S(2)}, u32[]{:S(2)}) collective-permute-start(f32[8,128]{1,0:T(8,128)S(1)} %chip_power.4.refs_5_.refs_1_), channel_id=1, source_target_pairs={{0,254},{1,255},{2,0},{3,1},{4,2},{5,3},{6,4},{7,5},{8,6},{9,7},{1... | collective-permute-start | bytes 12296 | tf_op jit(solution)/shard_map/ppermute | solution.py:402
  106.6 7.9 %collective-permute-start.5 = (f32[8,128]{1,0:T(8,128)S(1)}, f32[8,128]{1,0:T(8,128)S(1)}, u32[]{:S(2)}, u32[]{:S(2)}) collective-permute-start(f32[8,128]{1,0:T(8,128)S(1)} %chip_power.4.refs_5_.refs_1_), channel_id=1, source_target_pairs={{0,2},{1,3},{2,4},{3,5},{4,6},{5,7},{6,8},{7,9},{8,10},{9,11},{10,... | collective-permute-start | bytes 12296 | tf_op jit(solution)/shard_map/ppermute | solution.py:402
  147.9 4.2 %collective-permute-start.6 = (bf16[256,512]{1,0:T(8,128)(2,1)S(1)}, bf16[256,512]{1,0:T(8,128)(2,1)S(1)}, u32[]{:S(2)}, u32[]{:S(2)}) collective-permute-start(bf16[256,512]{1,0:T(8,128)(2,1)S(1)} %bitcast.28), channel_id=1, source_target_pairs={{0,1},{1,0},{2,3},{3,2},{4,5},{5,4},{6,7},{7,6},{8,9},{9,8},{10,11... | collective-permute-start | bytes 786440 | tf_op jit(solution)/shard_map/ppermute | solution.py:402
  154.2 1.2 collective-permute-start.7
  155.4 3.8 %collective-permute-start.8 = (f32[8,128]{1,0:T(8,128)S(1)}, f32[8,128]{1,0:T(8,128)S(1)}, u32[]{:S(2)}, u32[]{:S(2)}) collective-permute-start(f32[8,128]{1,0:T(8,128)S(1)} %chip_power.5.refs_2_), channel_id=1, source_target_pairs={{0,254},{1,255},{2,0},{3,1},{4,2},{5,3},{6,4},{7,5},{8,6},{9,7},{1... | collective-permute-start | bytes 12296 | tf_op jit(solution)/shard_map/ppermute | solution.py:402
  156.1 7.9 %collective-permute-start.9 = (f32[8,128]{1,0:T(8,128)S(1)}, f32[8,128]{1,0:T(8,128)S(1)}, u32[]{:S(2)}, u32[]{:S(2)}) collective-permute-start(f32[8,128]{1,0:T(8,128)S(1)} %chip_power.5.refs_2_), channel_id=1, source_target_pairs={{0,2},{1,3},{2,4},{3,5},{4,6},{5,7},{6,8},{7,9},{8,10},{9,11},{10,... | collective-permute-start | bytes 12296 | tf_op jit(solution)/shard_map/ppermute | solution.py:402

commit v8 on v7

--- a/solution.py
+++ b/solution.py
@@ -16,6 +16,7 @@
 LANES = 128
 BLOCK = 512
 FIRST_BLOCK = 2048
+SPILL = 64
 step_size = 0.5
 shrink_one = 0.05
 group_weight = 0.03
@@ -63,7 +64,9 @@
 
 
 def scales_of(powers, tau):
-    chip, after, before = (ref[...] for ref in powers)
+    chip, one, two, core = (ref[...] for ref in powers)
+    core = core[1:2, :]
+    before, after = jnp.where(core == 0, one, two), jnp.where(core == 0, two, one)
     return (
         group_scale(chip[0:1] + before[2:3], tau),
         group_scale(chip[1:2], tau),
@@ -187,11 +190,12 @@
 
 
 def forward_kernel(
-    marks_ref, state_ref, depth_ref, lead_ref, table_t_ref, chip_ref, out_ref, weighted_ref, *,
+    marks_ref, state_ref, depth_ref, lead_ref, table_t_ref, chip_ref, mine_ref, theirs_ref, weighted_ref, *,
     block, tau,
 ):
     coefs, sources = state_ref.shape
-    total = out_ref.shape[0] // 3
+    own = mine_ref.shape[0] // 3
+    first_core = marks_ref[1:2, 0:1] == 0
     start = marks_ref[0:1, 0:1]
     bounds = (start, start + GROUP)
     none = jnp.zeros((), BF16)
@@ -207,18 +211,25 @@
     middle = group_scale(chip_ref[1:2, 0:1], tau) * (halves[0][coefs:] + halves[1][:coefs])
     parts = (halves[0][:coefs], middle, halves[1][coefs:])
     for g in range(3):
-        out_ref[g * total : (g + 1) * total, :] = to_samples(table_t_ref, parts[g])
-
-
-def fold_kernel(parts_ref, *rest, tau):
+        samples = to_samples(table_t_ref, parts[g])
+        front, back = samples[:own], samples[own:]
+        theirs = jnp.where(first_core, back[:SPILL], front[:SPILL])
+        mine_ref[g * own : (g + 1) * own, :] = jnp.where(first_core, front, back)
+        theirs_ref[g * SPILL : (g + 1) * SPILL, :] = theirs.astype(BF16)
+
+
+def fold_kernel(mine_ref, theirs_ref, *rest, tau):
     *powers, out_ref, scale_ref = rest
-    total = out_ref.shape[0]
+    own = out_ref.shape[0]
     scale_ref[...] = jnp.zeros_like(scale_ref)
-    scales = scales_of(powers, tau)
-    for g, scale in enumerate(scales):
+    mine, theirs = 0.0, 0.0
+    for g, scale in enumerate(scales_of(powers, tau)):
         scale_ref[g : g + 1, :] = scale
-    first, middle, last = (parts_ref[g * total : (g + 1) * total, :] for g in range(3))
-    out_ref[...] = (scales[0][:, 0:1] * first + middle + scales[2][:, 0:1] * last).astype(BF16)
+        by = 1.0 if g == 1 else scale[:, 0:1]
+        mine += by * mine_ref[g * own : (g + 1) * own, :]
+        theirs += by * theirs_ref[g * SPILL : (g + 1) * SPILL, :].astype(F32)
+    out_ref[:SPILL] = (mine[:SPILL] + theirs).astype(BF16)
+    out_ref[SPILL:] = mine[SPILL:].astype(BF16)
 
 
 def plane_kernel(got_ref, out_ref):
@@ -351,14 +362,15 @@
 def forward_call(marks, state, depth, lead, table_t, chip, tau):
     coefs, sources = state.shape
     sensors = lead.shape[0]
+    own = table_t.shape[1] // 2
     return call(
         lambda *refs: forward_kernel(*refs, block=BLOCK, tau=tau),
         "forward",
         [marks, state, depth, lead, table_t, chip],
-        [struct(F32, 3 * table_t.shape[1], sensors)],
+        [struct(F32, 3 * own, sensors), struct(BF16, 3 * SPILL, sensors)],
         scratch=[pltpu.VMEM((2, 2 * coefs, GROUP), BF16)],
         cost=pl.CostEstimate(flops=4 * coefs * sources * sensors, bytes_accessed=8 << 20, transcendentals=0),
-    )[0]
+    )
 
 
 def estimate_call(marks, state, powers, tau, so_far=None):
@@ -409,7 +421,7 @@
     for iteration in range(ITERS):
         last = iteration == ITERS - 1
         plane = call(
-            plane_kernel, "plane_sum", [exchange(folded, PLANES)], [struct(BF16, 8 * AXES["z"], sensors)]
+            plane_kernel, "plane_sum", [exchange(folded, PLANES if iteration == 0 else PLANE)], [struct(BF16, 8 * AXES["z"], sensors)]
         )[0]
         slab = call(
             lambda *refs, last=last: owner_kernel(*refs, last=last),
@@ -422,18 +434,26 @@
         state, power = step_call(marks, got, others, table, scale, depth_row, state, lead)
         pair = move(power, 0, 1)
         chip = call(add_kernel, "chip_power", [power, pair], [struct(F32, 8, LANES)])[0]
-        powers = [chip, move(chip, -1, 0), move(chip, 1, 0)]
+        route = []
+        for at in range(src_count):
+            route.append((at * frm_count, (at + 1) % src_count * frm_count))
+            route.append((at * frm_count + 1, (at - 1) % src_count * frm_count + 1))
+        side = lax.ppermute(chip, (*SRC, "frm"), route)
         if last:
             residual = call(residual_kernel, "residual", [got], [struct(F32, sensors, own)])[0]
             estimate = estimate_call(marks, state, [chip], tau)
+            side, residual, estimate = lax.optimization_barrier((side, residual, estimate))
+            powers = [chip, side, move(side, 0, 1), marks]
         else:
-            parts = forward_call(marks, state, depth_row, lead, table_t, chip, tau)
+            mine, theirs = forward_call(marks, state, depth_row, lead, table_t, chip, tau)
+            theirs, side = lax.optimization_barrier((theirs, side))
+            powers = [chip, side, move(side, 0, 1), marks]
         if not last:
             folded, scale = call(
                 lambda *refs: fold_kernel(*refs, tau=tau),
                 "fold",
-                [parts, *powers],
-                [struct(BF16, total, sensors), struct(F32, 8, LANES)],
+                [mine, move(theirs, 0, 1), *powers],
+                [struct(BF16, own, sensors), struct(F32, 8, LANES)],
             )
 
     estimate = estimate_call(marks, state, powers, tau, estimate)

time: 166 us -> 165 us (level)
  starting transfers between devices: 9.38 us -> 25.3 us
  waiting for transfers between devices: 17.5 us -> 6.79 us
  blocking collectives: 116 us -> 110 us
    ppermute x10 -> x9, starting transfers between devices: 9.38 us -> 22.2 us  [move(): return lax.ppermute(x, (*SRC, 'frm'), route)]
    ppermute x10 -> x9, waiting for transfers between devices: 17.5 us -> 6.79 us  [move(): return lax.ppermute(x, (*SRC, 'frm'), route)]
    all_to_all x9, blocking collectives: 116 us -> 110 us  [exchange(): return lax.all_to_all(rows, axes, 0, 0, tiled=True)]
    ppermute x0 -> x3, starting transfers between devices: none -> 3.01 us  [shards(): side = lax.ppermute(chip, (*SRC, 'frm'), route)]
  transfers between devices with their start and end apart: 10 -> 12, of which waited for: 7 -> 7; matrix products, arithmetic and copies ran while one was open for 0% -> 0% of each run, Pallas kernels for 5% -> 5%
where the time goes in v8:
time: 165 us
  blocking collectives  110 us (67%)
  starting transfers between devices  25.3 us (15%)
  Pallas kernels  22 us (13%)
  waiting for transfers between devices  6.79 us (4%)
    all_to_all x9, blocking collectives, exchange(): return lax.all_to_all(rows, axes, 0, 0, tiled=True)  110 us
    ppermute x9, starting transfers between devices, move(): return lax.ppermute(x, (*SRC, 'frm'), route)  22.2 us
    pallas_call x20, Pallas kernels, call(): pl.pallas_call(kernel, in_specs=ins or [VMEM] * len(args), out_specs=out_...  22 us
    ppermute x9, waiting for transfers between devices, move(): return lax.ppermute(x, (*SRC, 'frm'), route)  6.79 us
  transfers between devices with their start and end apart: 12, of which 7 were waited for; matrix products, arithmetic and copies ran while one was open for 0% of the time, Pallas kernels for 5%

profile of v8, /device:TPU:1, one launch (start us, length us, event | category | flops | bytes accessed | tf_op | source)
XLA Modules:
  0.0 164.8 jit_solution(966739257230680387)
XLA Ops:
  0.6 0.1 pad_add_fusion.where_ref
  0.7 5.3 %first_forward.1 = (bf16[2,256,256]{2,1,0:T(8,128)(2,1)S(1)}, bf16[2,256,256]{2,1,0:T(8,128)(2,1)S(1)}, bf16[256,512]{1,0:T(8,128)(2,1)S(1)}, s32[8,128]{1,0:T(8...) custom-call(s32[2]{0:T(128)S(1)} %pad_add_fusion.where_ref, ...), custom_call_target="tpu_custom_call" | custom-call | tf_op jit(solution)/shard_map/first_forward/pallas_call | solution.py:302
  6.0 17.2 %all_to_all.99 = bf16[32,8,512]{2,1,0:T(8,128)(2,1)S(1)} all-to-all(bf16[32,8,512]{2,1,0:T(8,128)(2,1)S(1)} %bitcast.42), channel_id=1, replica_groups=mesh['x'=4,'z'=8,'y'=4,'frm'=2] {'frm','x','y'}, dimensions={0} | all-to-all | bytes 524288 | tf_op jit(solution)/shard_map/all_to_all | solution.py:406
  23.3 15.3 %all_to_all.100 = bf16[8,8,512]{2,1,0:T(8,128)(2,1)S(1)} all-to-all(bf16[8,8,512]{2,1,0:T(8,128)(2,1)S(1)} %bitcast.39), channel_id=1, replica_groups=mesh['x'=4,'z'=8,'y'=4,'frm'=2] {'z'}, dimensions={0} | all-to-all | bytes 131072 | tf_op jit(solution)/shard_map/all_to_all | solution.py:406
  38.7 13.8 %all_to_all.101 = bf16[32,8,512]{2,1,0:T(8,128)(2,1)S(1)} all-to-all(bf16[32,8,512]{2,1,0:T(8,128)(2,1)S(1)} %bitcast.35), channel_id=1, replica_groups=mesh['x'=4,'z'=8,'y'=4,'frm'=2] {'frm','x','y'}, dimensions={0} | all-to-all | bytes 524288 | tf_op jit(solution)/shard_map/all_to_all | solution.py:406
  52.5 1.9 %step.3 = (f32[256,4096]{1,0:T(8,128)S(1)}, f32[8,128]{1,0:T(8,128)S(1)}) custom-call(s32[8,128]{1,0:T(8,128)S(1)} %get-tuple-element.31.refs_0_.refs_5_, bf16[256,512]{1,0:T(8,128)(2,1)S(1)} %bitcast.32, bf16[2,256,256]{2,1,0:T(8,128)(2,1)S(1)} %get-tuple-element.34.refs_2_.refs_3_, f32[1,4096]{1,0:T(1,128)S(1)} %get-tuple-element.35.refs_3_.refs_2_.refs_4_, ...), custom_call_target="tpu_custom_call" | custom-call | tf_op jit(solution)/shard_map/step/pallas_call | solution.py:302
  54.4 0.7 collective-permute-start
  55.0 0.8 collective-permute-done.b_ref
  55.9 1.2 collective-permute-start.1
  57.0 3.0 %forward.2 = (f32[384,512]{1,0:T(8,128)S(1)}, bf16[192,512]{1,0:T(8,128)(2,1)S(1)}) custom-call(s32[8,128]{1,0:T(8,128)S(1)} %get-tuple-element.31.refs_0_.refs_5_, f32[256,4096]{1,0:T(8,128)S(1)} %get-tuple-element.38.refs_1_.refs_4_, f32[1,4096]{1,0:T(1,128)S(1)} %get-tuple-element.35.refs_3_.refs_2_.refs_4_, ...), custom_call_target="tpu_custom_call" | custom-call | flops 2147483648 | bytes 8388608 | tf_op jit(solution)/shard_map/forward/pallas_call | solution.py:302
  60.1 0.0 collective-permute-done.1.refs_3_
  60.1 5.2 %collective-permute-start.2 = (bf16[192,512]{1,0:T(8,128)(2,1)S(1)}, bf16[192,512]{1,0:T(8,128)(2,1)S(1)}, u32[]{:S(2)}, u32[]{:S(2)}) collective-permute-start(bf16[192,512]{1,0:T(8,128)(2,1)S(1)} %get-tuple-element.43), channel_id=1, source_target_pairs={{0,1},{1,0},{2,3},{3,2},{4,5},{5,4},{6,7},{7,6},{8,9},{9,8},{10,11... | collective-permute-start | bytes 589832 | tf_op jit(solution)/shard_map/ppermute | solution.py:414
  65.3 0.0 collective-permute-start.3
  65.3 1.2 collective-permute-done.3.refs_4_
  66.4 0.0 collective-permute-done.2.refs_1_
  66.4 0.2 fold.2
  66.6 9.3 %all_to_all.102 = bf16[16,8,512]{2,1,0:T(8,128)(2,1)S(1)} all-to-all(bf16[16,8,512]{2,1,0:T(8,128)(2,1)S(1)} %bitcast.46), channel_id=1, replica_groups=mesh['x'=4,'z'=8,'y'=4,'frm'=2] {'x','y'}, dimensions={0} | all-to-all | bytes 262144 | tf_op jit(solution)/shard_map/all_to_all | solution.py:406
  75.9 9.6 %all_to_all.103 = bf16[8,8,512]{2,1,0:T(8,128)(2,1)S(1)} all-to-all(bf16[8,8,512]{2,1,0:T(8,128)(2,1)S(1)} %bitcast.40), channel_id=1, replica_groups=mesh['x'=4,'z'=8,'y'=4,'frm'=2] {'z'}, dimensions={0} | all-to-all | bytes 131072 | tf_op jit(solution)/shard_map/all_to_all | solution.py:406
  85.5 14.9 %all_to_all.104 = bf16[32,8,512]{2,1,0:T(8,128)(2,1)S(1)} all-to-all(bf16[32,8,512]{2,1,0:T(8,128)(2,1)S(1)} %bitcast.36), channel_id=1, replica_groups=mesh['x'=4,'z'=8,'y'=4,'frm'=2] {'frm','x','y'}, dimensions={0} | all-to-all | bytes 524288 | tf_op jit(solution)/shard_map/all_to_all | solution.py:406
  100.4 1.9 %step.4 = (f32[256,4096]{1,0:T(8,128)S(1)}, f32[8,128]{1,0:T(8,128)S(1)}) custom-call(s32[8,128]{1,0:T(8,128)S(1)} %get-tuple-element.31.refs_0_.refs_5_, bf16[256,512]{1,0:T(8,128)(2,1)S(1)} %bitcast.31, bf16[2,256,256]{2,1,0:T(8,128)(2,1)S(1)} %get-tuple-element.34.refs_2_.refs_3_, f32[1,4096]{1,0:T(1,128)S(1)} %get-tuple-element.35.refs_3_.refs_2_.refs_4_, ...), custom_call_target="tpu_custom_call" | custom-call | tf_op jit(solution)/shard_map/step/pallas_call | solution.py:302
  102.4 0.9 collective-permute-start.4
  103.2 0.8 collective-permute-done.4.b_ref
  104.0 1.2 collective-permute-start.5
  105.2 3.0 %forward.3 = (f32[384,512]{1,0:T(8,128)S(1)}, bf16[192,512]{1,0:T(8,128)(2,1)S(1)}) custom-call(s32[8,128]{1,0:T(8,128)S(1)} %get-tuple-element.31.refs_0_.refs_5_, f32[256,4096]{1,0:T(8,128)S(1)} %get-tuple-element.47.refs_1_.refs_5_, f32[1,4096]{1,0:T(1,128)S(1)} %get-tuple-element.35.refs_3_.refs_2_.refs_4_, ...), custom_call_target="tpu_custom_call" | custom-call | flops 2147483648 | bytes 8388608 | tf_op jit(solution)/shard_map/forward/pallas_call | solution.py:302
  108.2 0.0 collective-permute-done.5.refs_3_
  108.2 5.2 %collective-permute-start.6 = (bf16[192,512]{1,0:T(8,128)(2,1)S(1)}, bf16[192,512]{1,0:T(8,128)(2,1)S(1)}, u32[]{:S(2)}, u32[]{:S(2)}) collective-permute-start(bf16[192,512]{1,0:T(8,128)(2,1)S(1)} %get-tuple-element.51), channel_id=1, source_target_pairs={{0,1},{1,0},{2,3},{3,2},{4,5},{5,4},{6,7},{7,6},{8,9},{9,8},{10,11... | collective-permute-start | bytes 589832 | tf_op jit(solution)/shard_map/ppermute | solution.py:414
  113.4 0.0 collective-permute-start.7
  113.4 1.2 collective-permute-done.7.refs_4_
  114.6 0.0 collective-permute-done.6.refs_1_
  114.6 0.2 fold.3
  114.8 9.3 %all_to_all.105 = bf16[16,8,512]{2,1,0:T(8,128)(2,1)S(1)} all-to-all(bf16[16,8,512]{2,1,0:T(8,128)(2,1)S(1)} %bitcast.47), channel_id=1, replica_groups=mesh['x'=4,'z'=8,'y'=4,'frm'=2] {'x','y'}, dimensions={0} | all-to-all | bytes 262144 | tf_op jit(solution)/shard_map/all_to_all | solution.py:406
  124.1 9.6 %all_to_all.106 = bf16[8,8,512]{2,1,0:T(8,128)(2,1)S(1)} all-to-all(bf16[8,8,512]{2,1,0:T(8,128)(2,1)S(1)} %bitcast.41), channel_id=1, replica_groups=mesh['x'=4,'z'=8,'y'=4,'frm'=2] {'z'}, dimensions={0} | all-to-all | bytes 131072 | tf_op jit(solution)/shard_map/all_to_all | solution.py:406
  133.7 10.9 %all_to_all.107 = bf16[16,16,512]{2,1,0:T(8,128)(2,1)S(1)} all-to-all(bf16[16,16,512]{2,1,0:T(8,128)(2,1)S(1)} %bitcast.34), channel_id=1, replica_groups=mesh['x'=4,'z'=8,'y'=4,'frm'=2] {'x','y'}, dimensions={0} | all-to-all | bytes 524288 | tf_op jit(solution)/shard_map/all_to_all | solution.py:406
  144.6 3.6 %collective-permute-start.8 = (bf16[256,512]{1,0:T(8,128)(2,1)S(1)}, bf16[256,512]{1,0:T(8,128)(2,1)S(1)}, u32[]{:S(2)}, u32[]{:S(2)}) collective-permute-start(bf16[256,512]{1,0:T(8,128)(2,1)S(1)} %bitcast.28), channel_id=1, source_target_pairs={{0,1},{1,0},{2,3},{3,2},{4,5},{5,4},{6,7},{7,6},{8,9},{9,8},{10,11... | collective-permute-start | bytes 786440 | tf_op jit(solution)/shard_map/ppermute | solution.py:414
  148.2 1.2 collective-permute-done.8.refs_2_
  149.3 2.0 %step.5 = (f32[256,4096]{1,0:T(8,128)S(1)}, f32[8,128]{1,0:T(8,128)S(1)}) custom-call(s32[8,128]{1,0:T(8,128)S(1)} %get-tuple-element.31.refs_0_.refs_5_, bf16[256,512]{1,0:T(8,128)(2,1)S(1)} %bitcast.29, bf16[256,512]{1,0:T(8,128)(2,1)S(1)} %collective-permute-done.8.refs_2_, bf16[2,256,256]{2,1,0:T(8,128)(2,1)S(1)} %get-tuple-element.34.refs_2_.refs_3_, ...), custom_call_target="tpu_custom_call" | custom-call | tf_op jit(solution)/shard_map/step/pallas_call | solution.py:302
  151.4 0.4 collective-permute-start.9
  151.8 0.8 collective-permute-done.9.b_ref
  152.6 0.7 collective-permute-start.10
  153.3 0.8 residual.1
  154.1 1.5 estimate.2.refs_6_
  155.6 0.0 collective-permute-done.10.refs_3_
  155.6 6.3 %collective-permute-start.11 = (f32[8,128]{1,0:T(8,128)S(1)}, f32[8,128]{1,0:T(8,128)S(1)}, u32[]{:S(2)}, u32[]{:S(2)}) collective-permute-start(f32[8,128]{1,0:T(8,128)S(1)} %collective-permute-done.10.refs_3_), channel_id=1, source_target_pairs={{0,1},{1,0},{2,3},{3,2},{4,5},{5,4},{6,7},{7,6},{8,9},{9,8},{10,11... | collective-permute-start | bytes 12296 | tf_op jit(solution)/shard_map/ppermute | solution.py:414
  162.0 0.8 collective-permute-done.11.refs_4_
  162.8 1.9 %estimate.3 = f32[256,4096]{1,0:T(8,128)} custom-call(s32[8,128]{1,0:T(8,128)S(1)} %get-tuple-element.31.refs_0_.refs_5_, f32[256,4096]{1,0:T(8,128)S(1)} %get-tuple-element.55.refs_1_, f32[8,128]{1,0:T(8,128)S(1)} %chip_power.5.refs_2_, f32[8,128]{1,0:T(8,128)S(1)} %collective-permute-done.10.refs_3_, ...), custom_call_target="tpu_custom_call", output_to_operand_aliasing={{}: (6, {})} | custom-call | flops 1048576 | bytes 4194304 | tf_op jit(solution)/shard_map/estimate/pallas_call | solution.py:302
  (9 shorter events, 0.2 us)
Async XLA Ops:
  54.4 1.5 collective-permute-start
  55.9 4.2 %collective-permute-start.1 = (f32[8,128]{1,0:T(8,128)S(1)}, f32[8,128]{1,0:T(8,128)S(1)}, u32[]{:S(2)}, u32[]{:S(2)}) collective-permute-start(f32[8,128]{1,0:T(8,128)S(1)} %chip_power.3.refs_5_.refs_2_), channel_id=1, source_target_pairs={{0,2},{1,255},{2,4},{3,1},{4,6},{5,3},{6,8},{7,5},{8,10},{9,7},{10... | collective-permute-start | bytes 12296 | tf_op jit(solution)/shard_map/ppermute | solution.py:441
  60.1 6.4 %collective-permute-start.2 = (bf16[192,512]{1,0:T(8,128)(2,1)S(1)}, bf16[192,512]{1,0:T(8,128)(2,1)S(1)}, u32[]{:S(2)}, u32[]{:S(2)}) collective-permute-start(bf16[192,512]{1,0:T(8,128)(2,1)S(1)} %get-tuple-element.43), channel_id=1, source_target_pairs={{0,1},{1,0},{2,3},{3,2},{4,5},{5,4},{6,7},{7,6},{8,9},{9,8},{10,11... | collective-permute-start | bytes 589832 | tf_op jit(solution)/shard_map/ppermute | solution.py:414
  65.3 1.2 collective-permute-start.3
  102.4 1.7 %collective-permute-start.4 = (f32[8,128]{1,0:T(8,128)S(1)}, f32[8,128]{1,0:T(8,128)S(1)}, u32[]{:S(2)}, u32[]{:S(2)}) collective-permute-start(f32[8,128]{1,0:T(8,128)S(1)} %get-tuple-element.48.a_ref), channel_id=1, source_target_pairs={{0,1},{1,0},{2,3},{3,2},{4,5},{5,4},{6,7},{7,6},{8,9},{9,8},{10,11... | collective-permute-start | bytes 12296 | tf_op jit(solution)/shard_map/ppermute | solution.py:414
  104.0 4.2 %collective-permute-start.5 = (f32[8,128]{1,0:T(8,128)S(1)}, f32[8,128]{1,0:T(8,128)S(1)}, u32[]{:S(2)}, u32[]{:S(2)}) collective-permute-start(f32[8,128]{1,0:T(8,128)S(1)} %chip_power.4.refs_5_.refs_2_), channel_id=1, source_target_pairs={{0,2},{1,255},{2,4},{3,1},{4,6},{5,3},{6,8},{7,5},{8,10},{9,7},{10... | collective-permute-start | bytes 12296 | tf_op jit(solution)/shard_map/ppermute | solution.py:441
  108.2 6.4 %collective-permute-start.6 = (bf16[192,512]{1,0:T(8,128)(2,1)S(1)}, bf16[192,512]{1,0:T(8,128)(2,1)S(1)}, u32[]{:S(2)}, u32[]{:S(2)}) collective-permute-start(bf16[192,512]{1,0:T(8,128)(2,1)S(1)} %get-tuple-element.51), channel_id=1, source_target_pairs={{0,1},{1,0},{2,3},{3,2},{4,5},{5,4},{6,7},{7,6},{8,9},{9,8},{10,11... | collective-permute-start | bytes 589832 | tf_op jit(solution)/shard_map/ppermute | solution.py:414
  113.4 1.2 collective-permute-start.7
  144.6 4.8 %collective-permute-start.8 = (bf16[256,512]{1,0:T(8,128)(2,1)S(1)}, bf16[256,512]{1,0:T(8,128)(2,1)S(1)}, u32[]{:S(2)}, u32[]{:S(2)}) collective-permute-start(bf16[256,512]{1,0:T(8,128)(2,1)S(1)} %bitcast.28), channel_id=1, source_target_pairs={{0,1},{1,0},{2,3},{3,2},{4,5},{5,4},{6,7},{7,6},{8,9},{9,8},{10,11... | collective-permute-start | bytes 786440 | tf_op jit(solution)/shard_map/ppermute | solution.py:414
  151.4 1.2 collective-permute-start.9
  152.6 3.0 %collective-permute-start.10 = (f32[8,128]{1,0:T(8,128)S(1)}, f32[8,128]{1,0:T(8,128)S(1)}, u32[]{:S(2)}, u32[]{:S(2)}) collective-permute-start(f32[8,128]{1,0:T(8,128)S(1)} %chip_power.5.refs_2_), channel_id=1, source_target_pairs={{0,2},{1,255},{2,4},{3,1},{4,6},{5,3},{6,8},{7,5},{8,10},{9,7},{10... | collective-permute-start | bytes 12296 | tf_op jit(solution)/shard_map/ppermute | solution.py:441
  155.6 7.2 %collective-permute-start.11 = (f32[8,128]{1,0:T(8,128)S(1)}, f32[8,128]{1,0:T(8,128)S(1)}, u32[]{:S(2)}, u32[]{:S(2)}) collective-permute-start(f32[8,128]{1,0:T(8,128)S(1)} %collective-permute-done.10.refs_3_), channel_id=1, source_target_pairs={{0,1},{1,0},{2,3},{3,2},{4,5},{5,4},{6,7},{7,6},{8,9},{9,8},{10,11... | collective-permute-start | bytes 12296 | tf_op jit(solution)/shard_map/ppermute | solution.py:414

commit v9 on v8

--- a/solution.py
+++ b/solution.py
@@ -64,9 +64,13 @@
 
 
 def scales_of(powers, tau):
-    chip, one, two, core = (ref[...] for ref in powers)
-    core = core[1:2, :]
-    before, after = jnp.where(core == 0, one, two), jnp.where(core == 0, two, one)
+    chip, *others = (ref[...] for ref in powers)
+    if len(others) == 2:
+        after, before = others
+    else:
+        one, two, marks = others
+        first_core = marks[1:2, :] == 0
+        before, after = jnp.where(first_core, one, two), jnp.where(first_core, two, one)
     return (
         group_scale(chip[0:1] + before[2:3], tau),
         group_scale(chip[1:2], tau),
@@ -146,22 +150,20 @@
 def step_kernel(
     marks_ref, got_ref, *rest, first, last, block
 ):
-    if last:
-        other_ref, *rest = rest
+    other_ref, *rest = rest
     table_ref, depth_ref, state_ref, lead_ref, *rest = rest
     if not first:
         scale_ref, *rest = rest
     new_ref, power_ref, turned_ref, *rest = rest
     sources = state_ref.shape[1]
+    (samples_ref,) = rest
+    own = samples_ref.shape[0] // 2
+    halves = [ref[...].astype(F32) for ref in (got_ref, other_ref)]
     if last:
-        (samples_ref,) = rest
-        own = samples_ref.shape[0] // 2
-        highs = [jnp.concatenate(slabs(ref[...].astype(F32))[::2], axis=0) for ref in (got_ref, other_ref)]
-        first_core = marks_ref[1:2, 0:1] == 0
-        samples_ref[:own] = jnp.where(first_core, *highs).astype(BF16)
-        samples_ref[own:] = jnp.where(first_core, *highs[::-1]).astype(BF16)
-    else:
-        samples_ref = got_ref
+        halves = [jnp.concatenate(slabs(half)[::2], axis=0) for half in halves]
+    first_core = marks_ref[1:2, 0:1] == 0
+    samples_ref[:own] = jnp.where(first_core, *halves).astype(BF16)
+    samples_ref[own:] = jnp.where(first_core, *halves[::-1]).astype(BF16)
     turned = dot(table_ref[0], samples_ref[...]) + dot(table_ref[1], samples_ref[...])
     turned_ref[...] = turned.astype(BF16)
 
@@ -345,17 +347,17 @@
     )
 
 
-def step_call(marks, got, others, table, scale, depth, state, lead):
+def step_call(marks, got, others, table, scale, depth, state, lead, last):
     coefs, sources = state.shape
     sensors = lead.shape[0]
-    first, last = scale is None, others is not None
-    args = [marks, got] + ([others] if last else []) + [table, depth, state, lead] + ([] if first else [scale])
+    first = scale is None
+    args = [marks, got, others, table, depth, state, lead] + ([] if first else [scale])
     return call(
         lambda *refs: step_kernel(*refs, first=first, last=last, block=BLOCK),
         "step",
         args,
         [struct(F32, coefs, sources), struct(F32, 8, LANES)],
-        scratch=[pltpu.VMEM((coefs, sensors), BF16)] + ([pltpu.VMEM((table.shape[2], sensors), BF16)] if last else []),
+        scratch=[pltpu.VMEM((coefs, sensors), BF16), pltpu.VMEM((table.shape[2], sensors), BF16)],
     )
 
 
@@ -413,6 +415,11 @@
                 route.append((chip * frm_count + core, to))
         return lax.ppermute(x, (*SRC, "frm"), route)
 
+    opposite = []
+    for chip in range(src_count):
+        opposite.append((chip * frm_count, (chip + 1) % src_count * frm_count))
+        opposite.append((chip * frm_count + 1, (chip - 1) % src_count * frm_count + 1))
+
     state = coefficients.transpose(1, 2, 0).reshape(coefs, sources)
     table, table_t, folded, marks, rows, depth_row, state, lead = first_call(
         where, offsets, group_ids.reshape(1, sources), depth.reshape(1, sources), measured, state, lead_field
@@ -427,25 +434,21 @@
             lambda *refs, last=last: owner_kernel(*refs, last=last),
             "owner",
             [exchange(plane, "z"), rows],
-            [struct(BF16, total, sensors)],
+            [struct(BF16, total if last else own, sensors)],
         )[0]
-        got = exchange(slab, PLANE if last else PLANES)
-        others = move(got, 0, 1) if last else None
-        state, power = step_call(marks, got, others, table, scale, depth_row, state, lead)
+        got = exchange(slab, PLANE)
+        state, power = step_call(
+            marks, got, move(got, 0, 1), table, scale, depth_row, state, lead, last
+        )
         pair = move(power, 0, 1)
         chip = call(add_kernel, "chip_power", [power, pair], [struct(F32, 8, LANES)])[0]
-        route = []
-        for at in range(src_count):
-            route.append((at * frm_count, (at + 1) % src_count * frm_count))
-            route.append((at * frm_count + 1, (at - 1) % src_count * frm_count + 1))
-        side = lax.ppermute(chip, (*SRC, "frm"), route)
         if last:
             residual = call(residual_kernel, "residual", [got], [struct(F32, sensors, own)])[0]
             estimate = estimate_call(marks, state, [chip], tau)
-            side, residual, estimate = lax.optimization_barrier((side, residual, estimate))
-            powers = [chip, side, move(side, 0, 1), marks]
+            powers = [chip, move(chip, -1, 0), move(chip, 1, 0)]
         else:
             mine, theirs = forward_call(marks, state, depth_row, lead, table_t, chip, tau)
+            side = lax.ppermute(chip, (*SRC, "frm"), opposite)
             theirs, side = lax.optimization_barrier((theirs, side))
             powers = [chip, side, move(side, 0, 1), marks]
         if not last:

time: 165 us -> 163 us (0.988)
  blocking collectives: 110 us -> 101 us
  waiting for transfers between devices: 6.79 us -> 12.7 us
    all_to_all x9, blocking collectives: 110 us -> 101 us  [exchange(): return lax.all_to_all(rows, axes, 0, 0, tiled=True)]
    ppermute x9 -> x12, waiting for transfers between devices: 6.79 us -> 12.7 us  [move(): return lax.ppermute(x, (*SRC, 'frm'), route)]
    ppermute x9 -> x12, starting transfers between devices: 22.2 us -> 23.8 us  [move(): return lax.ppermute(x, (*SRC, 'frm'), route)]
  transfers between devices with their start and end apart: 12 -> 14, of which waited for: 7 -> 9; matrix products, arithmetic and copies ran while one was open for 0% -> 0% of each run, Pallas kernels for 5% -> 5%
where the time goes in v9:
time: 163 us; the launch traced here: 162 us
  blocking collectives  101 us (62%)
  starting transfers between devices  25.9 us (16%)
  Pallas kernels  22.1 us (14%)
  waiting for transfers between devices  12.7 us (8%)
    all_to_all x9, blocking collectives, exchange(): return lax.all_to_all(rows, axes, 0, 0, tiled=True)  101 us
    ppermute x12, starting transfers between devices, move(): return lax.ppermute(x, (*SRC, 'frm'), route)  23.8 us
    pallas_call x20, Pallas kernels, call(): pl.pallas_call(kernel, in_specs=ins or [VMEM] * len(args), out_specs=out_...  22.1 us
    ppermute x12, waiting for transfers between devices, move(): return lax.ppermute(x, (*SRC, 'frm'), route)  12.7 us
  transfers between devices with their start and end apart: 14, of which 9 were waited for; matrix products, arithmetic and copies ran while one was open for 0% of the time, Pallas kernels for 5%

profile of v9, /device:TPU:1, one launch (start us, length us, event | category | flops | bytes accessed | tf_op | source)
XLA Modules:
  0.0 162.5 jit_solution(14915274188548681179)
XLA Ops:
  0.6 0.1 pad_add_fusion.where_ref
  0.7 5.3 %first_forward.1 = (bf16[2,256,256]{2,1,0:T(8,128)(2,1)S(1)}, bf16[2,256,256]{2,1,0:T(8,128)(2,1)S(1)}, bf16[256,512]{1,0:T(8,128)(2,1)S(1)}, s32[8,128]{1,0:T(8...) custom-call(s32[2]{0:T(128)S(1)} %pad_add_fusion.where_ref, ...), custom_call_target="tpu_custom_call" | custom-call | tf_op jit(solution)/shard_map/first_forward/pallas_call | solution.py:304
  6.0 17.2 %all_to_all.99 = bf16[32,8,512]{2,1,0:T(8,128)(2,1)S(1)} all-to-all(bf16[32,8,512]{2,1,0:T(8,128)(2,1)S(1)} %bitcast.44), channel_id=1, replica_groups=mesh['x'=4,'z'=8,'y'=4,'frm'=2] {'frm','x','y'}, dimensions={0} | all-to-all | bytes 524288 | tf_op jit(solution)/shard_map/all_to_all | solution.py:408
  23.3 15.3 %all_to_all.100 = bf16[8,8,512]{2,1,0:T(8,128)(2,1)S(1)} all-to-all(bf16[8,8,512]{2,1,0:T(8,128)(2,1)S(1)} %bitcast.41), channel_id=1, replica_groups=mesh['x'=4,'z'=8,'y'=4,'frm'=2] {'z'}, dimensions={0} | all-to-all | bytes 131072 | tf_op jit(solution)/shard_map/all_to_all | solution.py:408
  38.6 9.6 %all_to_all.101 = bf16[16,8,512]{2,1,0:T(8,128)(2,1)S(1)} all-to-all(bf16[16,8,512]{2,1,0:T(8,128)(2,1)S(1)} %bitcast.37), channel_id=1, replica_groups=mesh['x'=4,'z'=8,'y'=4,'frm'=2] {'x','y'}, dimensions={0} | all-to-all | bytes 262144 | tf_op jit(solution)/shard_map/all_to_all | solution.py:408
  48.3 3.2 %collective-permute-start = (bf16[128,512]{1,0:T(8,128)(2,1)S(1)}, bf16[128,512]{1,0:T(8,128)(2,1)S(1)}, u32[]{:S(2)}, u32[]{:S(2)}) collective-permute-start(bf16[128,512]{1,0:T(8,128)(2,1)S(1)} %bitcast.35), channel_id=1, source_target_pairs={{0,1},{1,0},{2,3},{3,2},{4,5},{5,4},{6,7},{7,6},{8,9},{9,8},{10,11... | collective-permute-start | bytes 393224 | tf_op jit(solution)/shard_map/ppermute | solution.py:416
  51.4 1.0 collective-permute-done.refs_2_
  52.4 1.9 %step.3 = (f32[256,4096]{1,0:T(8,128)S(1)}, f32[8,128]{1,0:T(8,128)S(1)}) custom-call(s32[8,128]{1,0:T(8,128)S(1)} %get-tuple-element.28.refs_0_.refs_5_, bf16[128,512]{1,0:T(8,128)(2,1)S(1)} %bitcast.36, bf16[128,512]{1,0:T(8,128)(2,1)S(1)} %collective-permute-done.refs_2_, bf16[2,256,256]{2,1,0:T(8,128)(2,1)S(1)} %get-tuple-element.31.refs_3_, ...), custom_call_target="tpu_custom_call" | custom-call | tf_op jit(solution)/shard_map/step/pallas_call | solution.py:304
  54.4 0.4 collective-permute-start.1
  54.8 0.8 collective-permute-done.1.b_ref
  55.6 1.1 collective-permute-start.2
  56.6 3.0 %forward.2 = (f32[384,512]{1,0:T(8,128)S(1)}, bf16[192,512]{1,0:T(8,128)(2,1)S(1)}) custom-call(s32[8,128]{1,0:T(8,128)S(1)} %get-tuple-element.28.refs_0_.refs_5_, f32[256,4096]{1,0:T(8,128)S(1)} %get-tuple-element.35.refs_1_.refs_5_, f32[1,4096]{1,0:T(1,128)S(1)} %get-tuple-element.32.refs_4_.refs_2_, ...), custom_call_target="tpu_custom_call" | custom-call | flops 2147483648 | bytes 8388608 | tf_op jit(solution)/shard_map/forward/pallas_call | solution.py:304
  59.7 0.0 collective-permute-done.2.refs_3_
  59.7 5.3 %collective-permute-start.3 = (bf16[192,512]{1,0:T(8,128)(2,1)S(1)}, bf16[192,512]{1,0:T(8,128)(2,1)S(1)}, u32[]{:S(2)}, u32[]{:S(2)}) collective-permute-start(bf16[192,512]{1,0:T(8,128)(2,1)S(1)} %get-tuple-element.40), channel_id=1, source_target_pairs={{0,1},{1,0},{2,3},{3,2},{4,5},{5,4},{6,7},{7,6},{8,9},{9,8},{10,11... | collective-permute-start | bytes 589832 | tf_op jit(solution)/shard_map/ppermute | solution.py:416
  65.0 0.0 collective-permute-start.4
  65.0 1.2 collective-permute-done.4.refs_4_
  66.1 0.0 collective-permute-done.3.refs_1_
  66.1 0.2 fold.2
  66.3 9.3 %all_to_all.102 = bf16[16,8,512]{2,1,0:T(8,128)(2,1)S(1)} all-to-all(bf16[16,8,512]{2,1,0:T(8,128)(2,1)S(1)} %bitcast.48), channel_id=1, replica_groups=mesh['x'=4,'z'=8,'y'=4,'frm'=2] {'x','y'}, dimensions={0} | all-to-all | bytes 262144 | tf_op jit(solution)/shard_map/all_to_all | solution.py:408
  75.6 9.6 %all_to_all.103 = bf16[8,8,512]{2,1,0:T(8,128)(2,1)S(1)} all-to-all(bf16[8,8,512]{2,1,0:T(8,128)(2,1)S(1)} %bitcast.42), channel_id=1, replica_groups=mesh['x'=4,'z'=8,'y'=4,'frm'=2] {'z'}, dimensions={0} | all-to-all | bytes 131072 | tf_op jit(solution)/shard_map/all_to_all | solution.py:408
  85.2 10.1 %all_to_all.104 = bf16[16,8,512]{2,1,0:T(8,128)(2,1)S(1)} all-to-all(bf16[16,8,512]{2,1,0:T(8,128)(2,1)S(1)} %bitcast.39), channel_id=1, replica_groups=mesh['x'=4,'z'=8,'y'=4,'frm'=2] {'x','y'}, dimensions={0} | all-to-all | bytes 262144 | tf_op jit(solution)/shard_map/all_to_all | solution.py:408
  95.4 3.7 %collective-permute-start.5 = (bf16[128,512]{1,0:T(8,128)(2,1)S(1)}, bf16[128,512]{1,0:T(8,128)(2,1)S(1)}, u32[]{:S(2)}, u32[]{:S(2)}) collective-permute-start(bf16[128,512]{1,0:T(8,128)(2,1)S(1)} %bitcast.33), channel_id=1, source_target_pairs={{0,1},{1,0},{2,3},{3,2},{4,5},{5,4},{6,7},{7,6},{8,9},{9,8},{10,11... | collective-permute-start | bytes 393224 | tf_op jit(solution)/shard_map/ppermute | solution.py:416
  99.1 1.0 collective-permute-done.5.refs_2_
  100.1 2.0 %step.4 = (f32[256,4096]{1,0:T(8,128)S(1)}, f32[8,128]{1,0:T(8,128)S(1)}) custom-call(s32[8,128]{1,0:T(8,128)S(1)} %get-tuple-element.28.refs_0_.refs_5_, bf16[128,512]{1,0:T(8,128)(2,1)S(1)} %bitcast.34, bf16[128,512]{1,0:T(8,128)(2,1)S(1)} %collective-permute-done.5.refs_2_, bf16[2,256,256]{2,1,0:T(8,128)(2,1)S(1)} %get-tuple-element.31.refs_3_, ...), custom_call_target="tpu_custom_call" | custom-call | tf_op jit(solution)/shard_map/step/pallas_call | solution.py:304
  102.1 0.4 collective-permute-start.6
  102.5 0.8 collective-permute-done.6.b_ref
  103.3 1.1 collective-permute-start.7
  104.4 3.0 %forward.3 = (f32[384,512]{1,0:T(8,128)S(1)}, bf16[192,512]{1,0:T(8,128)(2,1)S(1)}) custom-call(s32[8,128]{1,0:T(8,128)S(1)} %get-tuple-element.28.refs_0_.refs_5_, f32[256,4096]{1,0:T(8,128)S(1)} %get-tuple-element.44.refs_1_.refs_5_, f32[1,4096]{1,0:T(1,128)S(1)} %get-tuple-element.32.refs_4_.refs_2_, ...), custom_call_target="tpu_custom_call" | custom-call | flops 2147483648 | bytes 8388608 | tf_op jit(solution)/shard_map/forward/pallas_call | solution.py:304
  107.4 0.0 collective-permute-done.7.refs_3_
  107.4 5.3 %collective-permute-start.8 = (bf16[192,512]{1,0:T(8,128)(2,1)S(1)}, bf16[192,512]{1,0:T(8,128)(2,1)S(1)}, u32[]{:S(2)}, u32[]{:S(2)}) collective-permute-start(bf16[192,512]{1,0:T(8,128)(2,1)S(1)} %get-tuple-element.48), channel_id=1, source_target_pairs={{0,1},{1,0},{2,3},{3,2},{4,5},{5,4},{6,7},{7,6},{8,9},{9,8},{10,11... | collective-permute-start | bytes 589832 | tf_op jit(solution)/shard_map/ppermute | solution.py:416
  112.7 0.0 collective-permute-start.9
  112.7 1.2 collective-permute-done.9.refs_4_
  113.9 0.0 collective-permute-done.8.refs_1_
  113.9 0.2 fold.3
  114.0 9.3 %all_to_all.105 = bf16[16,8,512]{2,1,0:T(8,128)(2,1)S(1)} all-to-all(bf16[16,8,512]{2,1,0:T(8,128)(2,1)S(1)} %bitcast.49), channel_id=1, replica_groups=mesh['x'=4,'z'=8,'y'=4,'frm'=2] {'x','y'}, dimensions={0} | all-to-all | bytes 262144 | tf_op jit(solution)/shard_map/all_to_all | solution.py:408
  123.3 9.6 %all_to_all.106 = bf16[8,8,512]{2,1,0:T(8,128)(2,1)S(1)} all-to-all(bf16[8,8,512]{2,1,0:T(8,128)(2,1)S(1)} %bitcast.43), channel_id=1, replica_groups=mesh['x'=4,'z'=8,'y'=4,'frm'=2] {'z'}, dimensions={0} | all-to-all | bytes 131072 | tf_op jit(solution)/shard_map/all_to_all | solution.py:408
  133.0 10.9 %all_to_all.107 = bf16[16,16,512]{2,1,0:T(8,128)(2,1)S(1)} all-to-all(bf16[16,16,512]{2,1,0:T(8,128)(2,1)S(1)} %bitcast.32), channel_id=1, replica_groups=mesh['x'=4,'z'=8,'y'=4,'frm'=2] {'x','y'}, dimensions={0} | all-to-all | bytes 524288 | tf_op jit(solution)/shard_map/all_to_all | solution.py:408
  143.8 3.6 %collective-permute-start.10 = (bf16[256,512]{1,0:T(8,128)(2,1)S(1)}, bf16[256,512]{1,0:T(8,128)(2,1)S(1)}, u32[]{:S(2)}, u32[]{:S(2)}) collective-permute-start(bf16[256,512]{1,0:T(8,128)(2,1)S(1)} %bitcast.28), channel_id=1, source_target_pairs={{0,1},{1,0},{2,3},{3,2},{4,5},{5,4},{6,7},{7,6},{8,9},{9,8},{10,11... | collective-permute-start | bytes 786440 | tf_op jit(solution)/shard_map/ppermute | solution.py:416
  147.4 1.2 collective-permute-done.10.refs_2_
  148.6 2.0 %step.5 = (f32[256,4096]{1,0:T(8,128)S(1)}, f32[8,128]{1,0:T(8,128)S(1)}) custom-call(s32[8,128]{1,0:T(8,128)S(1)} %get-tuple-element.28.refs_0_.refs_5_, bf16[256,512]{1,0:T(8,128)(2,1)S(1)} %bitcast.29, bf16[256,512]{1,0:T(8,128)(2,1)S(1)} %collective-permute-done.10.refs_2_, bf16[2,256,256]{2,1,0:T(8,128)(2,1)S(1)} %get-tuple-element.31.refs_3_, ...), custom_call_target="tpu_custom_call" | custom-call | tf_op jit(solution)/shard_map/step/pallas_call | solution.py:304
  150.6 0.4 collective-permute-start.11
  151.1 0.8 collective-permute-done.11.b_ref
  151.9 0.7 collective-permute-start.12
  152.6 0.8 collective-permute-start.13
  153.3 0.8 residual.1
  154.2 1.5 estimate.2.refs_5_
  155.7 4.8 %collective-permute-done.13.refs_4_ = f32[8,128]{1,0:T(8,128)S(1)} collective-permute-done((f32[8,128]{1,0:T(8,128)S(1)}, f32[8,128]{1,0:T(8,128)S(1)}, u32[]{:S(2)}, u32[]{:S(2)}) %collective-permute-start.13) | collective-permute-done | bytes 4128 | tf_op jit(solution)/shard_map/ppermute | solution.py:416
  160.4 1.9 %estimate.3 = f32[256,4096]{1,0:T(8,128)} custom-call(s32[8,128]{1,0:T(8,128)S(1)} %get-tuple-element.28.refs_0_.refs_5_, f32[256,4096]{1,0:T(8,128)S(1)} %get-tuple-element.52.refs_1_, f32[8,128]{1,0:T(8,128)S(1)} %chip_power.5.refs_2_, f32[8,128]{1,0:T(8,128)S(1)} %collective-permute-done.12.refs_3_, ...), custom_call_target="tpu_custom_call", output_to_operand_aliasing={{}: (5, {})} | custom-call | flops 1048576 | bytes 4194304 | tf_op jit(solution)/shard_map/estimate/pallas_call | solution.py:304
  (10 shorter events, 0.2 us)
Async XLA Ops:
  48.3 4.2 %collective-permute-start = (bf16[128,512]{1,0:T(8,128)(2,1)S(1)}, bf16[128,512]{1,0:T(8,128)(2,1)S(1)}, u32[]{:S(2)}, u32[]{:S(2)}) collective-permute-start(bf16[128,512]{1,0:T(8,128)(2,1)S(1)} %bitcast.35), channel_id=1, source_target_pairs={{0,1},{1,0},{2,3},{3,2},{4,5},{5,4},{6,7},{7,6},{8,9},{9,8},{10,11... | collective-permute-start | bytes 393224 | tf_op jit(solution)/shard_map/ppermute | solution.py:416
  54.4 1.2 collective-permute-start.1
  55.6 4.1 %collective-permute-start.2 = (f32[8,128]{1,0:T(8,128)S(1)}, f32[8,128]{1,0:T(8,128)S(1)}, u32[]{:S(2)}, u32[]{:S(2)}) collective-permute-start(f32[8,128]{1,0:T(8,128)S(1)} %chip_power.3.refs_5_.refs_2_), channel_id=1, source_target_pairs={{0,2},{1,255},{2,4},{3,1},{4,6},{5,3},{6,8},{7,5},{8,10},{9,7},{10... | collective-permute-start | bytes 12296 | tf_op jit(solution)/shard_map/ppermute | solution.py:451
  59.7 6.5 %collective-permute-start.3 = (bf16[192,512]{1,0:T(8,128)(2,1)S(1)}, bf16[192,512]{1,0:T(8,128)(2,1)S(1)}, u32[]{:S(2)}, u32[]{:S(2)}) collective-permute-start(bf16[192,512]{1,0:T(8,128)(2,1)S(1)} %get-tuple-element.40), channel_id=1, source_target_pairs={{0,1},{1,0},{2,3},{3,2},{4,5},{5,4},{6,7},{7,6},{8,9},{9,8},{10,11... | collective-permute-start | bytes 589832 | tf_op jit(solution)/shard_map/ppermute | solution.py:416
  65.0 1.2 collective-permute-start.4
  95.4 4.7 %collective-permute-start.5 = (bf16[128,512]{1,0:T(8,128)(2,1)S(1)}, bf16[128,512]{1,0:T(8,128)(2,1)S(1)}, u32[]{:S(2)}, u32[]{:S(2)}) collective-permute-start(bf16[128,512]{1,0:T(8,128)(2,1)S(1)} %bitcast.33), channel_id=1, source_target_pairs={{0,1},{1,0},{2,3},{3,2},{4,5},{5,4},{6,7},{7,6},{8,9},{9,8},{10,11... | collective-permute-start | bytes 393224 | tf_op jit(solution)/shard_map/ppermute | solution.py:416
  102.1 1.2 collective-permute-start.6
  103.3 4.1 %collective-permute-start.7 = (f32[8,128]{1,0:T(8,128)S(1)}, f32[8,128]{1,0:T(8,128)S(1)}, u32[]{:S(2)}, u32[]{:S(2)}) collective-permute-start(f32[8,128]{1,0:T(8,128)S(1)} %chip_power.4.refs_5_.refs_2_), channel_id=1, source_target_pairs={{0,2},{1,255},{2,4},{3,1},{4,6},{5,3},{6,8},{7,5},{8,10},{9,7},{10... | collective-permute-start | bytes 12296 | tf_op jit(solution)/shard_map/ppermute | solution.py:451
  107.4 6.5 %collective-permute-start.8 = (bf16[192,512]{1,0:T(8,128)(2,1)S(1)}, bf16[192,512]{1,0:T(8,128)(2,1)S(1)}, u32[]{:S(2)}, u32[]{:S(2)}) collective-permute-start(bf16[192,512]{1,0:T(8,128)(2,1)S(1)} %get-tuple-element.48), channel_id=1, source_target_pairs={{0,1},{1,0},{2,3},{3,2},{4,5},{5,4},{6,7},{7,6},{8,9},{9,8},{10,11... | collective-permute-start | bytes 589832 | tf_op jit(solution)/shard_map/ppermute | solution.py:416
  112.7 1.2 collective-permute-start.9
  143.8 4.8 %collective-permute-start.10 = (bf16[256,512]{1,0:T(8,128)(2,1)S(1)}, bf16[256,512]{1,0:T(8,128)(2,1)S(1)}, u32[]{:S(2)}, u32[]{:S(2)}) collective-permute-start(bf16[256,512]{1,0:T(8,128)(2,1)S(1)} %bitcast.28), channel_id=1, source_target_pairs={{0,1},{1,0},{2,3},{3,2},{4,5},{5,4},{6,7},{7,6},{8,9},{9,8},{10,11... | collective-permute-start | bytes 786440 | tf_op jit(solution)/shard_map/ppermute | solution.py:416
  150.6 1.2 collective-permute-start.11
  151.9 3.8 %collective-permute-start.12 = (f32[8,128]{1,0:T(8,128)S(1)}, f32[8,128]{1,0:T(8,128)S(1)}, u32[]{:S(2)}, u32[]{:S(2)}) collective-permute-start(f32[8,128]{1,0:T(8,128)S(1)} %chip_power.5.refs_2_), channel_id=1, source_target_pairs={{0,254},{1,255},{2,0},{3,1},{4,2},{5,3},{6,4},{7,5},{8,6},{9,7},{1... | collective-permute-start | bytes 12296 | tf_op jit(solution)/shard_map/ppermute | solution.py:416
  152.6 7.9 %collective-permute-start.13 = (f32[8,128]{1,0:T(8,128)S(1)}, f32[8,128]{1,0:T(8,128)S(1)}, u32[]{:S(2)}, u32[]{:S(2)}) collective-permute-start(f32[8,128]{1,0:T(8,128)S(1)} %chip_power.5.refs_2_), channel_id=1, source_target_pairs={{0,2},{1,3},{2,4},{3,5},{4,6},{5,7},{6,8},{7,9},{8,10},{9,11},{10,... | collective-permute-start | bytes 12296 | tf_op jit(solution)/shard_map/ppermute | solution.py:416

commit v10 on v9

--- a/solution.py
+++ b/solution.py
@@ -15,7 +15,7 @@
 ITERS = 3
 LANES = 128
 BLOCK = 512
-FIRST_BLOCK = 2048
+FIRST_BLOCK = 4096
 SPILL = 64
 step_size = 0.5
 shrink_one = 0.05

time: 163 us -> 163 us (level)
  no operation moved by 1% of the time
where the time goes in v10:
time: 163 us
  blocking collectives  101 us (62%)
  starting transfers between devices  25.9 us (16%)
  Pallas kernels  22.6 us (14%)
  waiting for transfers between devices  12.7 us (8%)
    all_to_all x9, blocking collectives, exchange(): return lax.all_to_all(rows, axes, 0, 0, tiled=True)  101 us
    ppermute x12, starting transfers between devices, move(): return lax.ppermute(x, (*SRC, 'frm'), route)  23.8 us
    pallas_call x20, Pallas kernels, call(): pl.pallas_call(kernel, in_specs=ins or [VMEM] * len(args), out_specs=out_...  22.6 us
    ppermute x12, waiting for transfers between devices, move(): return lax.ppermute(x, (*SRC, 'frm'), route)  12.7 us
  transfers between devices with their start and end apart: 14, of which 9 were waited for; matrix products, arithmetic and copies ran while one was open for 0% of the time, Pallas kernels for 5%

profile of v10, /device:TPU:1, one launch (start us, length us, event | category | flops | bytes accessed | tf_op | source)
XLA Modules:
  0.0 163.0 jit_solution(12208488082570577057)
XLA Ops:
  0.6 0.1 pad_add_fusion.where_ref
  0.7 5.9 %first_forward.1 = (bf16[2,256,256]{2,1,0:T(8,128)(2,1)S(1)}, bf16[2,256,256]{2,1,0:T(8,128)(2,1)S(1)}, bf16[256,512]{1,0:T(8,128)(2,1)S(1)}, s32[8,128]{1,0:T(8...) custom-call(s32[2]{0:T(128)S(1)} %pad_add_fusion.where_ref, ...), custom_call_target="tpu_custom_call" | custom-call | tf_op jit(solution)/shard_map/first_forward/pallas_call | solution.py:304
  6.6 17.2 %all_to_all.99 = bf16[32,8,512]{2,1,0:T(8,128)(2,1)S(1)} all-to-all(bf16[32,8,512]{2,1,0:T(8,128)(2,1)S(1)} %bitcast.44), channel_id=1, replica_groups=mesh['x'=4,'z'=8,'y'=4,'frm'=2] {'frm','x','y'}, dimensions={0} | all-to-all | bytes 524288 | tf_op jit(solution)/shard_map/all_to_all | solution.py:408
  23.9 15.3 %all_to_all.100 = bf16[8,8,512]{2,1,0:T(8,128)(2,1)S(1)} all-to-all(bf16[8,8,512]{2,1,0:T(8,128)(2,1)S(1)} %bitcast.41), channel_id=1, replica_groups=mesh['x'=4,'z'=8,'y'=4,'frm'=2] {'z'}, dimensions={0} | all-to-all | bytes 131072 | tf_op jit(solution)/shard_map/all_to_all | solution.py:408
  39.2 9.6 %all_to_all.101 = bf16[16,8,512]{2,1,0:T(8,128)(2,1)S(1)} all-to-all(bf16[16,8,512]{2,1,0:T(8,128)(2,1)S(1)} %bitcast.37), channel_id=1, replica_groups=mesh['x'=4,'z'=8,'y'=4,'frm'=2] {'x','y'}, dimensions={0} | all-to-all | bytes 262144 | tf_op jit(solution)/shard_map/all_to_all | solution.py:408
  48.8 3.2 %collective-permute-start = (bf16[128,512]{1,0:T(8,128)(2,1)S(1)}, bf16[128,512]{1,0:T(8,128)(2,1)S(1)}, u32[]{:S(2)}, u32[]{:S(2)}) collective-permute-start(bf16[128,512]{1,0:T(8,128)(2,1)S(1)} %bitcast.35), channel_id=1, source_target_pairs={{0,1},{1,0},{2,3},{3,2},{4,5},{5,4},{6,7},{7,6},{8,9},{9,8},{10,11... | collective-permute-start | bytes 393224 | tf_op jit(solution)/shard_map/ppermute | solution.py:416
  52.0 1.0 collective-permute-done.refs_2_
  53.0 1.9 %step.3 = (f32[256,4096]{1,0:T(8,128)S(1)}, f32[8,128]{1,0:T(8,128)S(1)}) custom-call(s32[8,128]{1,0:T(8,128)S(1)} %get-tuple-element.28.refs_0_.refs_5_, bf16[128,512]{1,0:T(8,128)(2,1)S(1)} %bitcast.36, bf16[128,512]{1,0:T(8,128)(2,1)S(1)} %collective-permute-done.refs_2_, bf16[2,256,256]{2,1,0:T(8,128)(2,1)S(1)} %get-tuple-element.31.refs_3_, ...), custom_call_target="tpu_custom_call" | custom-call | tf_op jit(solution)/shard_map/step/pallas_call | solution.py:304
  54.9 0.4 collective-permute-start.1
  55.3 0.8 collective-permute-done.1.b_ref
  56.1 1.1 collective-permute-start.2
  57.2 3.0 %forward.2 = (f32[384,512]{1,0:T(8,128)S(1)}, bf16[192,512]{1,0:T(8,128)(2,1)S(1)}) custom-call(s32[8,128]{1,0:T(8,128)S(1)} %get-tuple-element.28.refs_0_.refs_5_, f32[256,4096]{1,0:T(8,128)S(1)} %get-tuple-element.35.refs_1_.refs_5_, f32[1,4096]{1,0:T(1,128)S(1)} %get-tuple-element.32.refs_4_.refs_2_, ...), custom_call_target="tpu_custom_call" | custom-call | flops 2147483648 | bytes 8388608 | tf_op jit(solution)/shard_map/forward/pallas_call | solution.py:304
  60.2 0.0 collective-permute-done.2.refs_3_
  60.2 5.3 %collective-permute-start.3 = (bf16[192,512]{1,0:T(8,128)(2,1)S(1)}, bf16[192,512]{1,0:T(8,128)(2,1)S(1)}, u32[]{:S(2)}, u32[]{:S(2)}) collective-permute-start(bf16[192,512]{1,0:T(8,128)(2,1)S(1)} %get-tuple-element.40), channel_id=1, source_target_pairs={{0,1},{1,0},{2,3},{3,2},{4,5},{5,4},{6,7},{7,6},{8,9},{9,8},{10,11... | collective-permute-start | bytes 589832 | tf_op jit(solution)/shard_map/ppermute | solution.py:416
  65.5 0.0 collective-permute-start.4
  65.5 1.2 collective-permute-done.4.refs_4_
  66.7 0.2 fold.2
  66.9 9.3 %all_to_all.102 = bf16[16,8,512]{2,1,0:T(8,128)(2,1)S(1)} all-to-all(bf16[16,8,512]{2,1,0:T(8,128)(2,1)S(1)} %bitcast.48), channel_id=1, replica_groups=mesh['x'=4,'z'=8,'y'=4,'frm'=2] {'x','y'}, dimensions={0} | all-to-all | bytes 262144 | tf_op jit(solution)/shard_map/all_to_all | solution.py:408
  76.1 9.6 %all_to_all.103 = bf16[8,8,512]{2,1,0:T(8,128)(2,1)S(1)} all-to-all(bf16[8,8,512]{2,1,0:T(8,128)(2,1)S(1)} %bitcast.42), channel_id=1, replica_groups=mesh['x'=4,'z'=8,'y'=4,'frm'=2] {'z'}, dimensions={0} | all-to-all | bytes 131072 | tf_op jit(solution)/shard_map/all_to_all | solution.py:408
  85.8 10.1 %all_to_all.104 = bf16[16,8,512]{2,1,0:T(8,128)(2,1)S(1)} all-to-all(bf16[16,8,512]{2,1,0:T(8,128)(2,1)S(1)} %bitcast.39), channel_id=1, replica_groups=mesh['x'=4,'z'=8,'y'=4,'frm'=2] {'x','y'}, dimensions={0} | all-to-all | bytes 262144 | tf_op jit(solution)/shard_map/all_to_all | solution.py:408
  95.9 3.7 %collective-permute-start.5 = (bf16[128,512]{1,0:T(8,128)(2,1)S(1)}, bf16[128,512]{1,0:T(8,128)(2,1)S(1)}, u32[]{:S(2)}, u32[]{:S(2)}) collective-permute-start(bf16[128,512]{1,0:T(8,128)(2,1)S(1)} %bitcast.33), channel_id=1, source_target_pairs={{0,1},{1,0},{2,3},{3,2},{4,5},{5,4},{6,7},{7,6},{8,9},{9,8},{10,11... | collective-permute-start | bytes 393224 | tf_op jit(solution)/shard_map/ppermute | solution.py:416
  99.6 1.0 collective-permute-done.5.refs_2_
  100.6 2.0 %step.4 = (f32[256,4096]{1,0:T(8,128)S(1)}, f32[8,128]{1,0:T(8,128)S(1)}) custom-call(s32[8,128]{1,0:T(8,128)S(1)} %get-tuple-element.28.refs_0_.refs_5_, bf16[128,512]{1,0:T(8,128)(2,1)S(1)} %bitcast.34, bf16[128,512]{1,0:T(8,128)(2,1)S(1)} %collective-permute-done.5.refs_2_, bf16[2,256,256]{2,1,0:T(8,128)(2,1)S(1)} %get-tuple-element.31.refs_3_, ...), custom_call_target="tpu_custom_call" | custom-call | tf_op jit(solution)/shard_map/step/pallas_call | solution.py:304
  102.6 0.4 collective-permute-start.6
  103.0 0.8 collective-permute-done.6.b_ref
  103.8 1.1 collective-permute-start.7
  104.9 3.0 %forward.3 = (f32[384,512]{1,0:T(8,128)S(1)}, bf16[192,512]{1,0:T(8,128)(2,1)S(1)}) custom-call(s32[8,128]{1,0:T(8,128)S(1)} %get-tuple-element.28.refs_0_.refs_5_, f32[256,4096]{1,0:T(8,128)S(1)} %get-tuple-element.44.refs_1_.refs_5_, f32[1,4096]{1,0:T(1,128)S(1)} %get-tuple-element.32.refs_4_.refs_2_, ...), custom_call_target="tpu_custom_call" | custom-call | flops 2147483648 | bytes 8388608 | tf_op jit(solution)/shard_map/forward/pallas_call | solution.py:304
  107.9 0.0 collective-permute-done.7.refs_3_
  107.9 5.3 %collective-permute-start.8 = (bf16[192,512]{1,0:T(8,128)(2,1)S(1)}, bf16[192,512]{1,0:T(8,128)(2,1)S(1)}, u32[]{:S(2)}, u32[]{:S(2)}) collective-permute-start(bf16[192,512]{1,0:T(8,128)(2,1)S(1)} %get-tuple-element.48), channel_id=1, source_target_pairs={{0,1},{1,0},{2,3},{3,2},{4,5},{5,4},{6,7},{7,6},{8,9},{9,8},{10,11... | collective-permute-start | bytes 589832 | tf_op jit(solution)/shard_map/ppermute | solution.py:416
  113.2 0.0 collective-permute-start.9
  113.2 1.2 collective-permute-done.9.refs_4_
  114.4 0.0 collective-permute-done.8.refs_1_
  114.4 0.2 fold.3
  114.6 9.3 %all_to_all.105 = bf16[16,8,512]{2,1,0:T(8,128)(2,1)S(1)} all-to-all(bf16[16,8,512]{2,1,0:T(8,128)(2,1)S(1)} %bitcast.49), channel_id=1, replica_groups=mesh['x'=4,'z'=8,'y'=4,'frm'=2] {'x','y'}, dimensions={0} | all-to-all | bytes 262144 | tf_op jit(solution)/shard_map/all_to_all | solution.py:408
  123.9 9.6 %all_to_all.106 = bf16[8,8,512]{2,1,0:T(8,128)(2,1)S(1)} all-to-all(bf16[8,8,512]{2,1,0:T(8,128)(2,1)S(1)} %bitcast.43), channel_id=1, replica_groups=mesh['x'=4,'z'=8,'y'=4,'frm'=2] {'z'}, dimensions={0} | all-to-all | bytes 131072 | tf_op jit(solution)/shard_map/all_to_all | solution.py:408
  133.5 10.9 %all_to_all.107 = bf16[16,16,512]{2,1,0:T(8,128)(2,1)S(1)} all-to-all(bf16[16,16,512]{2,1,0:T(8,128)(2,1)S(1)} %bitcast.32), channel_id=1, replica_groups=mesh['x'=4,'z'=8,'y'=4,'frm'=2] {'x','y'}, dimensions={0} | all-to-all | bytes 524288 | tf_op jit(solution)/shard_map/all_to_all | solution.py:408
  144.4 3.6 %collective-permute-start.10 = (bf16[256,512]{1,0:T(8,128)(2,1)S(1)}, bf16[256,512]{1,0:T(8,128)(2,1)S(1)}, u32[]{:S(2)}, u32[]{:S(2)}) collective-permute-start(bf16[256,512]{1,0:T(8,128)(2,1)S(1)} %bitcast.28), channel_id=1, source_target_pairs={{0,1},{1,0},{2,3},{3,2},{4,5},{5,4},{6,7},{7,6},{8,9},{9,8},{10,11... | collective-permute-start | bytes 786440 | tf_op jit(solution)/shard_map/ppermute | solution.py:416
  148.0 1.2 collective-permute-done.10.refs_2_
  149.1 2.0 %step.5 = (f32[256,4096]{1,0:T(8,128)S(1)}, f32[8,128]{1,0:T(8,128)S(1)}) custom-call(s32[8,128]{1,0:T(8,128)S(1)} %get-tuple-element.28.refs_0_.refs_5_, bf16[256,512]{1,0:T(8,128)(2,1)S(1)} %bitcast.29, bf16[256,512]{1,0:T(8,128)(2,1)S(1)} %collective-permute-done.10.refs_2_, bf16[2,256,256]{2,1,0:T(8,128)(2,1)S(1)} %get-tuple-element.31.refs_3_, ...), custom_call_target="tpu_custom_call" | custom-call | tf_op jit(solution)/shard_map/step/pallas_call | solution.py:304
  151.2 0.4 collective-permute-start.11
  151.6 0.8 collective-permute-done.11.b_ref
  152.4 0.7 collective-permute-start.12
  153.1 0.8 collective-permute-start.13
  153.9 0.8 residual.1
  154.7 1.5 estimate.2.refs_5_
  156.2 0.0 collective-permute-done.12.refs_3_
  156.2 4.8 %collective-permute-done.13.refs_4_ = f32[8,128]{1,0:T(8,128)S(1)} collective-permute-done((f32[8,128]{1,0:T(8,128)S(1)}, f32[8,128]{1,0:T(8,128)S(1)}, u32[]{:S(2)}, u32[]{:S(2)}) %collective-permute-start.13) | collective-permute-done | bytes 4128 | tf_op jit(solution)/shard_map/ppermute | solution.py:416
  161.0 1.9 %estimate.3 = f32[256,4096]{1,0:T(8,128)} custom-call(s32[8,128]{1,0:T(8,128)S(1)} %get-tuple-element.28.refs_0_.refs_5_, f32[256,4096]{1,0:T(8,128)S(1)} %get-tuple-element.52.refs_1_, f32[8,128]{1,0:T(8,128)S(1)} %chip_power.5.refs_2_, f32[8,128]{1,0:T(8,128)S(1)} %collective-permute-done.12.refs_3_, ...), custom_call_target="tpu_custom_call", output_to_operand_aliasing={{}: (5, {})} | custom-call | flops 1048576 | bytes 4194304 | tf_op jit(solution)/shard_map/estimate/pallas_call | solution.py:304
  (10 shorter events, 0.2 us)
Async XLA Ops:
  48.8 4.2 %collective-permute-start = (bf16[128,512]{1,0:T(8,128)(2,1)S(1)}, bf16[128,512]{1,0:T(8,128)(2,1)S(1)}, u32[]{:S(2)}, u32[]{:S(2)}) collective-permute-start(bf16[128,512]{1,0:T(8,128)(2,1)S(1)} %bitcast.35), channel_id=1, source_target_pairs={{0,1},{1,0},{2,3},{3,2},{4,5},{5,4},{6,7},{7,6},{8,9},{9,8},{10,11... | collective-permute-start | bytes 393224 | tf_op jit(solution)/shard_map/ppermute | solution.py:416
  54.9 1.2 collective-permute-start.1
  56.1 4.1 %collective-permute-start.2 = (f32[8,128]{1,0:T(8,128)S(1)}, f32[8,128]{1,0:T(8,128)S(1)}, u32[]{:S(2)}, u32[]{:S(2)}) collective-permute-start(f32[8,128]{1,0:T(8,128)S(1)} %chip_power.3.refs_5_.refs_2_), channel_id=1, source_target_pairs={{0,2},{1,255},{2,4},{3,1},{4,6},{5,3},{6,8},{7,5},{8,10},{9,7},{10... | collective-permute-start | bytes 12296 | tf_op jit(solution)/shard_map/ppermute | solution.py:451
  60.2 6.5 %collective-permute-start.3 = (bf16[192,512]{1,0:T(8,128)(2,1)S(1)}, bf16[192,512]{1,0:T(8,128)(2,1)S(1)}, u32[]{:S(2)}, u32[]{:S(2)}) collective-permute-start(bf16[192,512]{1,0:T(8,128)(2,1)S(1)} %get-tuple-element.40), channel_id=1, source_target_pairs={{0,1},{1,0},{2,3},{3,2},{4,5},{5,4},{6,7},{7,6},{8,9},{9,8},{10,11... | collective-permute-start | bytes 589832 | tf_op jit(solution)/shard_map/ppermute | solution.py:416
  65.5 1.2 collective-permute-start.4
  95.9 4.7 %collective-permute-start.5 = (bf16[128,512]{1,0:T(8,128)(2,1)S(1)}, bf16[128,512]{1,0:T(8,128)(2,1)S(1)}, u32[]{:S(2)}, u32[]{:S(2)}) collective-permute-start(bf16[128,512]{1,0:T(8,128)(2,1)S(1)} %bitcast.33), channel_id=1, source_target_pairs={{0,1},{1,0},{2,3},{3,2},{4,5},{5,4},{6,7},{7,6},{8,9},{9,8},{10,11... | collective-permute-start | bytes 393224 | tf_op jit(solution)/shard_map/ppermute | solution.py:416
  102.6 1.2 collective-permute-start.6
  103.8 4.1 %collective-permute-start.7 = (f32[8,128]{1,0:T(8,128)S(1)}, f32[8,128]{1,0:T(8,128)S(1)}, u32[]{:S(2)}, u32[]{:S(2)}) collective-permute-start(f32[8,128]{1,0:T(8,128)S(1)} %chip_power.4.refs_5_.refs_2_), channel_id=1, source_target_pairs={{0,2},{1,255},{2,4},{3,1},{4,6},{5,3},{6,8},{7,5},{8,10},{9,7},{10... | collective-permute-start | bytes 12296 | tf_op jit(solution)/shard_map/ppermute | solution.py:451
  107.9 6.5 %collective-permute-start.8 = (bf16[192,512]{1,0:T(8,128)(2,1)S(1)}, bf16[192,512]{1,0:T(8,128)(2,1)S(1)}, u32[]{:S(2)}, u32[]{:S(2)}) collective-permute-start(bf16[192,512]{1,0:T(8,128)(2,1)S(1)} %get-tuple-element.48), channel_id=1, source_target_pairs={{0,1},{1,0},{2,3},{3,2},{4,5},{5,4},{6,7},{7,6},{8,9},{9,8},{10,11... | collective-permute-start | bytes 589832 | tf_op jit(solution)/shard_map/ppermute | solution.py:416
  113.2 1.2 collective-permute-start.9
  144.4 4.8 %collective-permute-start.10 = (bf16[256,512]{1,0:T(8,128)(2,1)S(1)}, bf16[256,512]{1,0:T(8,128)(2,1)S(1)}, u32[]{:S(2)}, u32[]{:S(2)}) collective-permute-start(bf16[256,512]{1,0:T(8,128)(2,1)S(1)} %bitcast.28), channel_id=1, source_target_pairs={{0,1},{1,0},{2,3},{3,2},{4,5},{5,4},{6,7},{7,6},{8,9},{9,8},{10,11... | collective-permute-start | bytes 786440 | tf_op jit(solution)/shard_map/ppermute | solution.py:416
  151.2 1.2 collective-permute-start.11
  152.4 3.8 %collective-permute-start.12 = (f32[8,128]{1,0:T(8,128)S(1)}, f32[8,128]{1,0:T(8,128)S(1)}, u32[]{:S(2)}, u32[]{:S(2)}) collective-permute-start(f32[8,128]{1,0:T(8,128)S(1)} %chip_power.5.refs_2_), channel_id=1, source_target_pairs={{0,254},{1,255},{2,0},{3,1},{4,2},{5,3},{6,4},{7,5},{8,6},{9,7},{1... | collective-permute-start | bytes 12296 | tf_op jit(solution)/shard_map/ppermute | solution.py:416
  153.1 7.9 %collective-permute-start.13 = (f32[8,128]{1,0:T(8,128)S(1)}, f32[8,128]{1,0:T(8,128)S(1)}, u32[]{:S(2)}, u32[]{:S(2)}) collective-permute-start(f32[8,128]{1,0:T(8,128)S(1)} %chip_power.5.refs_2_), channel_id=1, source_target_pairs={{0,2},{1,3},{2,4},{3,5},{4,6},{5,7},{6,8},{7,9},{8,10},{9,11},{10,... | collective-permute-start | bytes 12296 | tf_op jit(solution)/shard_map/ppermute | solution.py:416
